TPU v7x, 512 devices: a whole 4x4x16 slice. The times are simulated.
512 devices in a mesh: gx: 32 (over y, z_hi, x), gy: 16 (over z_lo, core).
Axes of the slice: x: 4, y: 4, z: 16 (z_hi: 2, z_lo: 8; z = z_hi * 8 + z_lo), core: 2. Of those that a mesh axis runs over, the one named last changes fastest.
Arguments:
- e_field: float32 [3, 256, 256, 128], P(None, 'gx', 'gy'), may hold values from -30 to 30
- h_field: float32 [3, 256, 256, 128], P(None, 'gx', 'gy'), may hold values from -30 to 30
- material: int32 [256, 256, 64], P('gx', 'gy'), may hold values from 0 to 3
- permittivity: float32 [4], replicated, may hold values from 1 to 12
- frequencies: float32 [4], replicated, may hold values from 0.6 to 2.4
Outputs:
- e_out: float32 [3, 256, 256, 128], P(None, 'gx', 'gy')
- h_out: float32 [3, 256, 256, 128], P(None, 'gx', 'gy')
- gram: float32 [8, 8], replicated
All inputs are finite; a program needn't handle non-finite values.
Results may differ from a plain program's by a relative error of at most 0.000096.
Values sent between devices are 32-bit elements; how exact they have to be, the bound alone decides.
No kernel may reach another device: no remote copies, remote signals or barrier semaphores. Data moves between devices by JAX's collectives and lax.ppermute only.
A program may use at most 64 MiB of HBM per device.

v0:
```python
import jax
import jax.numpy as jnp
from jax import lax
from jax.sharding import PartitionSpec as P

NZ = 64
SOURCES = 2
FILTERS = 4
MATERIALS = 4
ITERS = 4


TIME_STEP = 0.5


def from_behind(value, axis, steps):
    count = lax.axis_size(axis)
    pairs = [(source, (source + steps) % count) for source in range(count)]
    return lax.ppermute(value, axis, pairs)


def forward_z(field):
    pad = jnp.zeros(field.shape[:-1] + (SOURCES,), field.dtype)
    return jnp.concatenate([field[..., SOURCES:], pad], axis=-1) - field


def backward_z(field):
    pad = jnp.zeros(field.shape[:-1] + (SOURCES,), field.dtype)
    return field - jnp.concatenate([pad, field[..., :-SOURCES]], axis=-1)


def next_values(e_field):
    plane_x = from_behind(e_field[1:3, :1], "gx", -1)
    plane_y = from_behind(jnp.stack([e_field[0][:, :1], e_field[2][:, :1]]), "gy", -1)
    ey_next_x = jnp.concatenate([e_field[1, 1:], plane_x[0]], axis=0)
    ez_next_x = jnp.concatenate([e_field[2, 1:], plane_x[1]], axis=0)
    ex_next_y = jnp.concatenate([e_field[0][:, 1:], plane_y[0]], axis=1)
    ez_next_y = jnp.concatenate([e_field[2][:, 1:], plane_y[1]], axis=1)
    return (ey_next_x, ez_next_x, ex_next_y, ez_next_y)


def prev_values(h_field):
    plane_x = from_behind(h_field[1:3, -1:], "gx", 1)
    plane_y = from_behind(jnp.stack([h_field[0][:, -1:], h_field[2][:, -1:]]), "gy", 1)
    hy_prev_x = jnp.concatenate([plane_x[0], h_field[1, :-1]], axis=0)
    hz_prev_x = jnp.concatenate([plane_x[1], h_field[2, :-1]], axis=0)
    hx_prev_y = jnp.concatenate([plane_y[0], h_field[0][:, :-1]], axis=1)
    hz_prev_y = jnp.concatenate([plane_y[1], h_field[2][:, :-1]], axis=1)
    return (hy_prev_x, hz_prev_x, hx_prev_y, hz_prev_y)


def advance(e_field, h_field, scaled, next_fn, prev_fn):
    e_x, e_y, e_z = (e_field[0], e_field[1], e_field[2])
    ey_next_x, ez_next_x, ex_next_y, ez_next_y = next_fn(e_field)
    curl_x = ez_next_y - e_z - forward_z(e_y)
    curl_y = forward_z(e_x) - (ez_next_x - e_z)
    curl_z = ey_next_x - e_y - (ex_next_y - e_x)
    h_field = h_field - TIME_STEP * jnp.stack([curl_x, curl_y, curl_z])
    h_x, h_y, h_z = (h_field[0], h_field[1], h_field[2])
    hy_prev_x, hz_prev_x, hx_prev_y, hz_prev_y = prev_fn(h_field)
    curl_x = h_z - hz_prev_y - backward_z(h_y)
    curl_y = backward_z(h_x) - (h_z - hz_prev_x)
    curl_z = h_y - hy_prev_x - (h_x - hx_prev_y)
    e_field = jnp.stack([e_x + scaled * curl_x, e_y + scaled * curl_y, e_z + scaled * curl_z])
    return (e_field, h_field)


def body(e_field, h_field, material, permittivity, frequencies):
    onehot = (material[..., None] == jnp.arange(MATERIALS, dtype=jnp.int32)).astype(jnp.float32)
    permit_cell = jnp.sum(onehot * permittivity, axis=-1)
    permit = jnp.repeat(permit_cell, SOURCES, axis=-1)
    scaled = TIME_STEP / permit
    filtered = jnp.zeros((FILTERS,) + e_field.shape, jnp.float32)
    for step in range(ITERS):
        e_field, h_field = advance(e_field, h_field, scaled, next_values, prev_values)
        weights = jnp.cos(frequencies * ((step + 1) * TIME_STEP))
        filtered = filtered + weights[:, None, None, None, None] * e_field[None]
    count = filtered[0].size // SOURCES
    weighted = (filtered * permit[None, None]).reshape(FILTERS, count, SOURCES)
    plain = filtered.reshape(FILTERS, count, SOURCES)
    local = jnp.einsum("kms,lmt->kslt", weighted, plain, precision=lax.Precision.HIGHEST)
    local = local.reshape(FILTERS * SOURCES, FILTERS * SOURCES)
    summed = lax.psum(local, ("gx", "gy"))
    cells = e_field.shape[1] * lax.axis_size("gx") * e_field.shape[2] * lax.axis_size("gy") * NZ
    return (e_field, h_field, summed / cells)


def solution(mesh):
    in_specs = (P(None, "gx", "gy", None), P(None, "gx", "gy", None), P("gx", "gy", None), P(), P())
    out_specs = (P(None, "gx", "gy", None), P(None, "gx", "gy", None), P())
    return jax.shard_map(body, mesh=mesh, in_specs=in_specs, out_specs=out_specs, check_vma=False)
```

profile of v0, /device:TPU:1, one launch (start us, length us, event | category | flops | bytes accessed | tf_op | source)
XLA Modules:
  0.0 369.0 jit_solution(447718432147306307)
XLA Ops:
  1.4 20.9 %collective-permute-start.1 = (f32[2,1,16,128]{3,2,1,0:T(8,128)S(1)}, f32[2,1,16,128]{3,2,1,0:T(8,128)S(1)}, u32[]{:S(2)}, u32[]{:S(2)}) collective-permute-start(f32[2,1,16,128]{3,2,1,0:T(8,128)S(1)} %slice.390), channel_id=1, source_target_pairs={{0,496},{16,0},{32,16},{48,32},{64,48},{80,64},{96,80},{112,96},{1... | collective-permute-start | bytes 49160 | tf_op jit(solution)/shard_map/ppermute | solution.py:19
  23.2 2.9 collective-permute-start
  29.6 14.0 %mul.282 = f32[24576,2]{1,0:T(8,128)} reshape(f32[3,8,16,128]{3,2,1,0:T(8,128)S(1)} %mul.281) | data formatting | bytes 393216 | tf_op jit(solution)/shard_map/mul | solution.py:79
  43.6 7.5 %copy.782 = f32[2,24576]{1,0:T(2,128)S(1)} copy(f32[2,24576]{0,1:T(8,128)} %bitcast.290) | data formatting | bytes 393216 | tf_op jit(solution)/shard_map/mul | solution.py:79
  51.5 2.7 collective-permute-start.2
  57.0 14.7 %collective-permute-done.3 = f32[2,1,16,128]{3,2,1,0:T(8,128)S(1)} collective-permute-done((f32[2,1,16,128]{3,2,1,0:T(8,128)S(1)}, f32[2,1,16,128]{3,2,1,0:T(8,128)S(1)}, u32[]{:S(2)}, u32[]{:S(2)}) %collective-permute-start.3) | collective-permute-done | bytes 16416 | tf_op jit(solution)/shard_map/ppermute | solution.py:19
  76.4 6.3 %collective-permute-start.4 = (f32[2,8,1,128]{3,1,2,0:T(8,128)S(1)}, f32[2,8,1,128]{3,1,2,0:T(8,128)S(1)}, u32[]{:S(2)}, u32[]{:S(2)}) collective-permute-start(f32[2,8,1,128]{3,1,2,0:T(8,128)S(1)} %pad_maximum_fusion.9), channel_id=1, source_target_pairs={{0,15},{1,0},{2,1},{3,2},{4,3},{5,4},{6,5},{7,6},{8,7},{9,8},{10,9... | collective-permute-start | bytes 24584 | tf_op jit(solution)/shard_map/ppermute | solution.py:19
  82.9 14.0 %mul.260 = f32[24576,2]{1,0:T(8,128)} reshape(f32[3,8,16,128]{3,2,1,0:T(8,128)S(1)} %pad_maximum_fusion.1) | data formatting | bytes 393216 | tf_op jit(solution)/shard_map/mul | solution.py:77
  96.9 7.5 %copy.777 = f32[2,24576]{1,0:T(2,128)S(1)} copy(f32[2,24576]{0,1:T(8,128)} %bitcast.291) | data formatting | bytes 393216 | tf_op jit(solution)/shard_map/mul | solution.py:77
  108.5 4.7 %collective-permute-done.6 = f32[2,8,1,128]{3,1,2,0:T(8,128)S(1)} collective-permute-done((f32[2,8,1,128]{3,1,2,0:T(8,128)S(1)}, f32[2,8,1,128]{3,1,2,0:T(8,128)S(1)}, u32[]{:S(2)}, u32[]{:S(2)}) %collective-permute-start.6) | collective-permute-done | bytes 8224 | tf_op jit(solution)/shard_map/ppermute | solution.py:19
  113.2 10.8 %collective-permute-done.7 = f32[2,1,16,128]{3,2,1,0:T(8,128)S(1)} collective-permute-done((f32[2,1,16,128]{3,2,1,0:T(8,128)S(1)}, f32[2,1,16,128]{3,2,1,0:T(8,128)S(1)}, u32[]{:S(2)}, u32[]{:S(2)}) %collective-permute-start.7) | collective-permute-done | bytes 16416 | tf_op jit(solution)/shard_map/ppermute | solution.py:19
  124.2 4.1 %collective-permute-start.9 = (f32[2,1,16,128]{3,2,1,0:T(8,128)S(1)}, f32[2,1,16,128]{3,2,1,0:T(8,128)S(1)}, u32[]{:S(2)}, u32[]{:S(2)}) collective-permute-start(f32[2,1,16,128]{3,2,1,0:T(8,128)S(1)} %pad_maximum_fusion.5), channel_id=1, source_target_pairs={{0,496},{16,0},{32,16},{48,32},{64,48},{80,64},{96,80},{112,96},{1... | collective-permute-start | bytes 49160 | tf_op jit(solution)/shard_map/ppermute | solution.py:19
  129.2 11.8 %collective-permute-start.8 = (f32[2,8,1,128]{3,1,2,0:T(8,128)S(1)}, f32[2,8,1,128]{3,1,2,0:T(8,128)S(1)}, u32[]{:S(2)}, u32[]{:S(2)}) collective-permute-start(f32[2,8,1,128]{3,1,2,0:T(8,128)S(1)} %pad_maximum_fusion.11), channel_id=1, source_target_pairs={{0,15},{1,0},{2,1},{3,2},{4,3},{5,4},{6,5},{7,6},{8,7},{9,8},{10,9... | collective-permute-start | bytes 24584 | tf_op jit(solution)/shard_map/ppermute | solution.py:19
  141.1 14.0 %mul.265 = f32[24576,2]{1,0:T(8,128)} reshape(f32[3,8,16,128]{3,2,1,0:T(8,128)S(1)} %pad_maximum_fusion.2) | data formatting | bytes 393216 | tf_op jit(solution)/shard_map/mul | solution.py:77
  155.1 7.5 %copy.778 = f32[2,24576]{1,0:T(2,128)S(1)} copy(f32[2,24576]{0,1:T(8,128)} %bitcast.292) | data formatting | bytes 393216 | tf_op jit(solution)/shard_map/mul | solution.py:77
  169.5 13.3 %collective-permute-done.11 = f32[2,1,16,128]{3,2,1,0:T(8,128)S(1)} collective-permute-done((f32[2,1,16,128]{3,2,1,0:T(8,128)S(1)}, f32[2,1,16,128]{3,2,1,0:T(8,128)S(1)}, u32[]{:S(2)}, u32[]{:S(2)}) %collective-permute-start.11) | collective-permute-done | bytes 16416 | tf_op jit(solution)/shard_map/ppermute | solution.py:19
  183.0 3.4 collective-permute-start.13
  187.6 9.7 %collective-permute-start.12 = (f32[2,8,1,128]{3,1,2,0:T(8,128)S(1)}, f32[2,8,1,128]{3,1,2,0:T(8,128)S(1)}, u32[]{:S(2)}, u32[]{:S(2)}) collective-permute-start(f32[2,8,1,128]{3,1,2,0:T(8,128)S(1)} %pad_maximum_fusion.13), channel_id=1, source_target_pairs={{0,15},{1,0},{2,1},{3,2},{4,3},{5,4},{6,5},{7,6},{8,7},{9,8},{10,9... | collective-permute-start | bytes 24584 | tf_op jit(solution)/shard_map/ppermute | solution.py:19
  197.4 14.0 %mul.271 = f32[24576,2]{1,0:T(8,128)} reshape(f32[3,8,16,128]{3,2,1,0:T(8,128)S(1)} %pad_maximum_fusion.3) | data formatting | bytes 393216 | tf_op jit(solution)/shard_map/mul | solution.py:77
  211.4 7.5 %copy.779 = f32[2,24576]{1,0:T(2,128)S(1)} copy(f32[2,24576]{0,1:T(8,128)} %bitcast.293) | data formatting | bytes 393216 | tf_op jit(solution)/shard_map/mul | solution.py:77
  225.8 13.4 %collective-permute-done.15 = f32[2,1,16,128]{3,2,1,0:T(8,128)S(1)} collective-permute-done((f32[2,1,16,128]{3,2,1,0:T(8,128)S(1)}, f32[2,1,16,128]{3,2,1,0:T(8,128)S(1)}, u32[]{:S(2)}, u32[]{:S(2)}) %collective-permute-start.15) | collective-permute-done | bytes 16416 | tf_op jit(solution)/shard_map/ppermute | solution.py:19
  239.3 14.0 %mul.277 = f32[24576,2]{1,0:T(8,128)} reshape(f32[3,8,16,128]{3,2,1,0:T(8,128)S(1)} %pad_maximum_fusion) | data formatting | bytes 393216 | tf_op jit(solution)/shard_map/mul | solution.py:77
  253.3 7.5 %copy.780 = f32[2,24576]{1,0:T(2,128)S(1)} copy(f32[2,24576]{0,1:T(8,128)} %bitcast.294) | data formatting | bytes 393216 | tf_op jit(solution)/shard_map/mul | solution.py:77
  264.8 103.5 %psum.7 = f32[8,8]{1,0:T(8,128)S(1)} all-reduce(f32[8,8]{1,0:T(8,128)S(1)} %fusion.85), channel_id=1, replica_groups=mesh['gx'=32,'gy'=16] {'gx','gy'}, use_global_device_ids=true, to_apply=%region_1.0 | all-reduce | flops 64 | bytes 512 | tf_op jit(solution)/shard_map/psum | solution.py:83
  (153 shorter events, 37.5 us)
Async XLA Ops:
  1.4 49.8 %collective-permute-start.1 = (f32[2,1,16,128]{3,2,1,0:T(8,128)S(1)}, f32[2,1,16,128]{3,2,1,0:T(8,128)S(1)}, u32[]{:S(2)}, u32[]{:S(2)}) collective-permute-start(f32[2,1,16,128]{3,2,1,0:T(8,128)S(1)} %slice.390), channel_id=1, source_target_pairs={{0,496},{16,0},{32,16},{48,32},{64,48},{80,64},{96,80},{112,96},{1... | collective-permute-start | bytes 49160 | tf_op jit(solution)/shard_map/ppermute | solution.py:19
  23.2 28.0 %collective-permute-start = (f32[2,8,1,128]{3,1,2,0:T(8,128)S(1)}, f32[2,8,1,128]{3,1,2,0:T(8,128)S(1)}, u32[]{:S(2)}, u32[]{:S(2)}) collective-permute-start(f32[2,8,1,128]{3,1,2,0:T(8,128)S(1)} %pad_maximum_fusion.7), channel_id=1, source_target_pairs={{0,15},{1,0},{2,1},{3,2},{4,3},{5,4},{6,5},{7,6},{8,7},{9,8},{10,9... | collective-permute-start | bytes 24584 | tf_op jit(solution)/shard_map/ppermute | solution.py:19
  29.6 21.6 %copy-start = (f32[3,8,16,128]{3,2,1,0:T(8,128)S(1)}, f32[3,8,16,128]{3,2,1,0:T(8,128)}, u32[]{:S(2)}) copy-start(f32[3,8,16,128]{3,2,1,0:T(8,128)} %param.5) | copy-start | bytes 589828
  29.6 21.8 %copy-start.2 = (f32[3,8,16,128]{3,2,1,0:T(8,128)S(1)}, f32[3,8,16,128]{3,2,1,0:T(8,128)}, u32[]{:S(2)}) copy-start(f32[3,8,16,128]{3,2,1,0:T(8,128)} %param.6) | copy-start | bytes 589828
  51.5 5.5 %collective-permute-start.2 = (f32[2,8,1,128]{3,1,2,0:T(8,128)S(1)}, f32[2,8,1,128]{3,1,2,0:T(8,128)S(1)}, u32[]{:S(2)}, u32[]{:S(2)}) collective-permute-start(f32[2,8,1,128]{3,1,2,0:T(8,128)S(1)} %pad_maximum_fusion.8), channel_id=1, source_target_pairs={{0,1},{1,2},{2,3},{3,4},{4,5},{5,6},{6,7},{7,8},{8,9},{9,10},{10,1... | collective-permute-start | bytes 24584 | tf_op jit(solution)/shard_map/ppermute | solution.py:19
  54.2 17.4 %collective-permute-start.3 = (f32[2,1,16,128]{3,2,1,0:T(8,128)S(1)}, f32[2,1,16,128]{3,2,1,0:T(8,128)S(1)}, u32[]{:S(2)}, u32[]{:S(2)}) collective-permute-start(f32[2,1,16,128]{3,2,1,0:T(8,128)S(1)} %slice.517), channel_id=1, source_target_pairs={{0,16},{16,32},{32,48},{48,64},{64,80},{80,96},{96,112},{112,128},... | collective-permute-start | bytes 49160 | tf_op jit(solution)/shard_map/ppermute | solution.py:19
  71.8 4.5 %collective-permute-start.5 = (f32[2,1,16,128]{3,2,1,0:T(8,128)S(1)}, f32[2,1,16,128]{3,2,1,0:T(8,128)S(1)}, u32[]{:S(2)}, u32[]{:S(2)}) collective-permute-start(f32[2,1,16,128]{3,2,1,0:T(8,128)S(1)} %pad_maximum_fusion.6), channel_id=1, source_target_pairs={{0,496},{16,0},{32,16},{48,32},{64,48},{80,64},{96,80},{112,96},{1... | collective-permute-start | bytes 49160 | tf_op jit(solution)/shard_map/ppermute | solution.py:19
  76.4 28.0 %collective-permute-start.4 = (f32[2,8,1,128]{3,1,2,0:T(8,128)S(1)}, f32[2,8,1,128]{3,1,2,0:T(8,128)S(1)}, u32[]{:S(2)}, u32[]{:S(2)}) collective-permute-start(f32[2,8,1,128]{3,1,2,0:T(8,128)S(1)} %pad_maximum_fusion.9), channel_id=1, source_target_pairs={{0,15},{1,0},{2,1},{3,2},{4,3},{5,4},{6,5},{7,6},{8,7},{9,8},{10,9... | collective-permute-start | bytes 24584 | tf_op jit(solution)/shard_map/ppermute | solution.py:19
  104.6 8.6 %collective-permute-start.6 = (f32[2,8,1,128]{3,1,2,0:T(8,128)S(1)}, f32[2,8,1,128]{3,1,2,0:T(8,128)S(1)}, u32[]{:S(2)}, u32[]{:S(2)}) collective-permute-start(f32[2,8,1,128]{3,1,2,0:T(8,128)S(1)} %pad_maximum_fusion.10), channel_id=1, source_target_pairs={{0,1},{1,2},{2,3},{3,4},{4,5},{5,6},{6,7},{7,8},{8,9},{9,10},{10,1... | collective-permute-start | bytes 24584 | tf_op jit(solution)/shard_map/ppermute | solution.py:19
  106.6 17.4 %collective-permute-start.7 = (f32[2,1,16,128]{3,2,1,0:T(8,128)S(1)}, f32[2,1,16,128]{3,2,1,0:T(8,128)S(1)}, u32[]{:S(2)}, u32[]{:S(2)}) collective-permute-start(f32[2,1,16,128]{3,2,1,0:T(8,128)S(1)} %slice.545), channel_id=1, source_target_pairs={{0,16},{16,32},{32,48},{48,64},{64,80},{80,96},{96,112},{112,128},... | collective-permute-start | bytes 49160 | tf_op jit(solution)/shard_map/ppermute | solution.py:19
  124.2 5.0 %collective-permute-start.9 = (f32[2,1,16,128]{3,2,1,0:T(8,128)S(1)}, f32[2,1,16,128]{3,2,1,0:T(8,128)S(1)}, u32[]{:S(2)}, u32[]{:S(2)}) collective-permute-start(f32[2,1,16,128]{3,2,1,0:T(8,128)S(1)} %pad_maximum_fusion.5), channel_id=1, source_target_pairs={{0,496},{16,0},{32,16},{48,32},{64,48},{80,64},{96,80},{112,96},{1... | collective-permute-start | bytes 49160 | tf_op jit(solution)/shard_map/ppermute | solution.py:19
  129.2 33.5 %collective-permute-start.8 = (f32[2,8,1,128]{3,1,2,0:T(8,128)S(1)}, f32[2,8,1,128]{3,1,2,0:T(8,128)S(1)}, u32[]{:S(2)}, u32[]{:S(2)}) collective-permute-start(f32[2,8,1,128]{3,1,2,0:T(8,128)S(1)} %pad_maximum_fusion.11), channel_id=1, source_target_pairs={{0,15},{1,0},{2,1},{3,2},{4,3},{5,4},{6,5},{7,6},{8,7},{9,8},{10,9... | collective-permute-start | bytes 24584 | tf_op jit(solution)/shard_map/ppermute | solution.py:19
  162.9 6.6 %collective-permute-start.10 = (f32[2,8,1,128]{3,1,2,0:T(8,128)S(1)}, f32[2,8,1,128]{3,1,2,0:T(8,128)S(1)}, u32[]{:S(2)}, u32[]{:S(2)}) collective-permute-start(f32[2,8,1,128]{3,1,2,0:T(8,128)S(1)} %pad_maximum_fusion.12), channel_id=1, source_target_pairs={{0,1},{1,2},{2,3},{3,4},{4,5},{5,6},{6,7},{7,8},{8,9},{9,10},{10,1... | collective-permute-start | bytes 24584 | tf_op jit(solution)/shard_map/ppermute | solution.py:19
  164.9 18.0 %collective-permute-start.11 = (f32[2,1,16,128]{3,2,1,0:T(8,128)S(1)}, f32[2,1,16,128]{3,2,1,0:T(8,128)S(1)}, u32[]{:S(2)}, u32[]{:S(2)}) collective-permute-start(f32[2,1,16,128]{3,2,1,0:T(8,128)S(1)} %slice.573), channel_id=1, source_target_pairs={{0,16},{16,32},{32,48},{48,64},{64,80},{80,96},{96,112},{112,128},... | collective-permute-start | bytes 49160 | tf_op jit(solution)/shard_map/ppermute | solution.py:19
  183.0 4.5 %collective-permute-start.13 = (f32[2,1,16,128]{3,2,1,0:T(8,128)S(1)}, f32[2,1,16,128]{3,2,1,0:T(8,128)S(1)}, u32[]{:S(2)}, u32[]{:S(2)}) collective-permute-start(f32[2,1,16,128]{3,2,1,0:T(8,128)S(1)} %pad_maximum_fusion.4), channel_id=1, source_target_pairs={{0,496},{16,0},{32,16},{48,32},{64,48},{80,64},{96,80},{112,96},{1... | collective-permute-start | bytes 49160 | tf_op jit(solution)/shard_map/ppermute | solution.py:19
  187.6 31.4 %collective-permute-start.12 = (f32[2,8,1,128]{3,1,2,0:T(8,128)S(1)}, f32[2,8,1,128]{3,1,2,0:T(8,128)S(1)}, u32[]{:S(2)}, u32[]{:S(2)}) collective-permute-start(f32[2,8,1,128]{3,1,2,0:T(8,128)S(1)} %pad_maximum_fusion.13), channel_id=1, source_target_pairs={{0,15},{1,0},{2,1},{3,2},{4,3},{5,4},{6,5},{7,6},{8,7},{9,8},{10,9... | collective-permute-start | bytes 24584 | tf_op jit(solution)/shard_map/ppermute | solution.py:19
  219.1 41.8 %copy-start.1 = (f32[3,8,16,128]{3,2,1,0:T(8,128)}, f32[3,8,16,128]{3,2,1,0:T(8,128)S(1)}, u32[]{:S(2)}) copy-start(f32[3,8,16,128]{3,2,1,0:T(8,128)S(1)} %fusion.3) | copy-start | bytes 589828
  219.2 6.6 %collective-permute-start.14 = (f32[2,8,1,128]{3,1,2,0:T(8,128)S(1)}, f32[2,8,1,128]{3,1,2,0:T(8,128)S(1)}, u32[]{:S(2)}, u32[]{:S(2)}) collective-permute-start(f32[2,8,1,128]{3,1,2,0:T(8,128)S(1)} %pad_maximum_fusion.14), channel_id=1, source_target_pairs={{0,1},{1,2},{2,3},{3,4},{4,5},{5,6},{6,7},{7,8},{8,9},{9,10},{10,1... | collective-permute-start | bytes 24584 | tf_op jit(solution)/shard_map/ppermute | solution.py:19
  221.2 18.0 %collective-permute-start.15 = (f32[2,1,16,128]{3,2,1,0:T(8,128)S(1)}, f32[2,1,16,128]{3,2,1,0:T(8,128)S(1)}, u32[]{:S(2)}, u32[]{:S(2)}) collective-permute-start(f32[2,1,16,128]{3,2,1,0:T(8,128)S(1)} %slice.602), channel_id=1, source_target_pairs={{0,16},{16,32},{32,48},{48,64},{64,80},{80,96},{96,112},{112,128},... | collective-permute-start | bytes 49160 | tf_op jit(solution)/shard_map/ppermute | solution.py:19
  239.3 21.6 %copy-start.3 = (f32[3,8,16,128]{3,2,1,0:T(8,128)}, f32[3,8,16,128]{3,2,1,0:T(8,128)S(1)}, u32[]{:S(2)}) copy-start(f32[3,8,16,128]{3,2,1,0:T(8,128)S(1)} %pad_maximum_fusion) | copy-start | bytes 589828
where the time goes:
time: 370 us; the launch traced here: 369 us
  local copies, waits for them, and re-layouts  113 us (31%)
  blocking collectives  104 us (28%)
  starting transfers between devices  77.3 us (21%)
  waiting for transfers between devices  67.1 us (18%)
  other arithmetic  4.46 us (1%)
    psum x1, blocking collectives, body(): summed = lax.psum(local, ('gx', 'gy'))  104 us
    mul x8, local copies, waits for them, and re-layouts, body(): filtered = filtered + weights[:, None, None, None, None] * e_field[None]  86.2 us
    ppermute x16, starting transfers between devices, from_behind(): return lax.ppermute(value, axis, pairs)  77.3 us
    ppermute x16, waiting for transfers between devices, from_behind(): return lax.ppermute(value, axis, pairs)  67.1 us
    mul x4, local copies, waits for them, and re-layouts, body(): weighted = (filtered * permit[None, None]).reshape(FILTERS, count, SOURCES)  22.1 us
  transfers between devices with their start and end apart: 16, of which 11 were waited for; matrix products, arithmetic and copies ran while one was open for 25% of the time, Pallas kernels for 0%

commit v1 on v0

v1 whole, which is shorter than its diff:
```python
import jax
import jax.numpy as jnp
from jax import lax
from jax.experimental import pallas as pl
from jax.experimental.pallas import tpu as pltpu
from jax.sharding import PartitionSpec as P

NZ = 64
SOURCES = 2
FILTERS = 4
MATERIALS = 4
ITERS = 4
TIME_STEP = 0.5

BX, BY, LANES = 8, 16, NZ * SOURCES
HALO = ITERS
PX = BX + 2 * HALO
PY = BY + 2 * HALO
XTILES = 49
YTILES = 7 * PX // 2

VMEM = pl.BlockSpec(memory_space=pltpu.VMEM)
SMEM = pl.BlockSpec(memory_space=pltpu.SMEM)
PARAMS = pltpu.CompilerParams(vmem_limit_bytes=32 * 1024 * 1024)


def iota(shape, dim):
    return lax.broadcasted_iota(jnp.int32, shape, dim)


def call(kernel, outs, name, n_in, scratch=(), smem=(), flops=0, size=0):
    return pl.pallas_call(
        kernel,
        out_shape=outs,
        in_specs=[SMEM if i in smem else VMEM for i in range(n_in)],
        out_specs=jax.tree.map(lambda _: VMEM, outs),
        scratch_shapes=list(scratch),
        compiler_params=PARAMS,
        cost_estimate=pl.CostEstimate(flops=flops, bytes_accessed=size, transcendentals=0),
        name=name,
    )


def f32(*shape):
    return jax.ShapeDtypeStruct(shape, jnp.float32)


def pack_x(e_ref, h_ref, m_ref, a_ref, b_ref):
    even = lax.rem(lax.axis_index("gx"), 2) == 0
    row, col = iota((NZ, LANES), 0), iota((NZ, LANES), 1)
    low = (col == row).astype(jnp.bfloat16)
    high = (col == row + NZ).astype(jnp.bfloat16)
    for out, upper in ((a_ref, even), (b_ref, jnp.logical_not(even))):
        wide = jnp.where(upper, BX - HALO, 0)
        narrow = jnp.where(upper, BX - HALO + 1, 0)
        tile = 0
        for ref, c, n, start in (
            (e_ref, 0, 4, wide), (e_ref, 1, 4, wide), (e_ref, 2, 4, wide),
            (h_ref, 0, 3, narrow), (h_ref, 1, 4, wide), (h_ref, 2, 4, wide),
        ):
            out[pl.ds(tile, 2 * n)] = ref[c, pl.ds(start, n)].reshape(2 * n, 8, LANES)
            tile += 2 * n
        for i in range(3):
            cells = m_ref[narrow + i].astype(jnp.float32).astype(jnp.bfloat16)
            out[tile + i] = jnp.dot(cells[:8], low, preferred_element_type=jnp.float32) + jnp.dot(
                cells[8:], high, preferred_element_type=jnp.float32
            )


def look_up(index, table_ref):
    value = jnp.full(index.shape, table_ref[0], jnp.float32)
    for m in range(1, MATERIALS):
        value = jnp.where(index == float(m), table_ref[m], value)
    return value


def own_cells(m_ref, p_ref, permit_ref, scaled_ref):
    row, col = iota((NZ, LANES), 0), iota((NZ, LANES), 1)
    spread = (col // SOURCES == row).astype(jnp.bfloat16)
    cells = m_ref[...].reshape(BX * BY, NZ).astype(jnp.float32).astype(jnp.bfloat16)
    index = jnp.dot(cells, spread, preferred_element_type=jnp.float32)
    permit = look_up(index, p_ref)
    permit_ref[...] = permit.reshape(BX, BY, LANES)
    scaled_ref[...] = (TIME_STEP / permit).reshape(BX, BY, LANES)


def extend_x(e_ref, h_ref, s_ref, a_ref, b_ref, p_ref, ye_ref, yh_ref, ys_ref, ya_ref, yb_ref):
    even = lax.rem(lax.axis_index("gx"), 2) == 0
    row, col = iota((LANES, LANES), 0), iota((LANES, LANES), 1)
    low = (col // SOURCES == row).astype(jnp.bfloat16)
    high = (col // SOURCES == row - NZ).astype(jnp.bfloat16)
    ye_ref[:, :BX] = e_ref[...]
    yh_ref[:, :BX] = h_ref[...]
    ys_ref[:BX] = s_ref[...]
    for src, after in ((a_ref, even), (b_ref, jnp.logical_not(even))):
        wide = jnp.where(after, BX, BX + HALO)
        narrow = jnp.where(after, BX, BX + HALO + 1)
        tile = 0
        for ref, c, n, start in (
            (ye_ref, 0, 4, wide), (ye_ref, 1, 4, wide), (ye_ref, 2, 4, wide),
            (yh_ref, 0, 3, narrow), (yh_ref, 1, 4, wide), (yh_ref, 2, 4, wide),
        ):
            ref[c, pl.ds(start, n)] = src[pl.ds(tile, 2 * n)].reshape(n, BY, LANES)
            tile += 2 * n
        cells = src[pl.ds(tile, 3)].reshape(24, LANES).astype(jnp.bfloat16)
        for half, spread in ((0, low), (8, high)):
            index = jnp.dot(cells, spread, preferred_element_type=jnp.float32)
            value = TIME_STEP / look_up(index, p_ref)
            for i in range(3):
                ys_ref[narrow + i, pl.ds(half, 8)] = value[8 * i : 8 * i + 8]
    zero = jnp.zeros((BY, LANES), jnp.float32)
    yh_ref[0, BX + HALO] = zero
    yh_ref[0, BX + HALO - 1] = zero
    ys_ref[BX + HALO] = zero
    ys_ref[BX + HALO - 1] = zero
    fill_y(ye_ref, yh_ref, ys_ref, ya_ref, yb_ref)


def fill_y(ye_ref, yh_ref, ys_ref, ya_ref, yb_ref):
    even = lax.rem(lax.axis_index("gy"), 2) == 0
    first = iota((8, LANES), 0) < HALO
    for f in range(7):
        ref = (ye_ref, ye_ref, ye_ref, yh_ref, yh_ref, yh_ref)[f].at[f % 3] if f < 6 else ys_ref
        for p in range(PX // 2):
            top = jnp.where(first, pltpu.roll(ref[p, 8:16], HALO, 0), ref[p + PX // 2, 8:16])
            bottom = jnp.where(first, ref[p, 0:8], pltpu.roll(ref[p + PX // 2, 0:8], HALO, 0))
            ya_ref[f * 8 + p] = jnp.where(even, top, bottom)
            yb_ref[f * 8 + p] = jnp.where(even, bottom, top)


def steps(xe_ref, xh_ref, xs_ref, permit_ref, ya_ref, yb_ref, w_ref, e_ref, h_ref, part_ref, ee, hh, ss):
    even = lax.rem(lax.axis_index("gy"), 2) == 0
    first = iota((8, LANES), 0) < HALO
    for f in range(7):
        src = xe_ref.at[f % 3] if f < 3 else xh_ref.at[f % 3] if f < 6 else xs_ref
        dst = ee.at[0, f % 3] if f < 3 else hh.at[f % 3] if f < 6 else ss
        dst[:, :BY] = src[...]
        for p in range(PX // 2):
            a, b = ya_ref[f * 8 + p], yb_ref[f * 8 + p]
            after, before = jnp.where(even, a, b), jnp.where(even, b, a)
            dst[p, BY:PY] = jnp.where(first, after, pltpu.roll(before, HALO, 0))
            dst[p + PX // 2, BY:PY] = jnp.where(first, pltpu.roll(after, HALO, 0), before)

    lane = iota((PY, LANES), 1)
    not_last, not_first = lane < LANES - SOURCES, lane >= SOURCES

    def up_z(v):
        return jnp.where(not_last, pltpu.roll(v, LANES - SOURCES, 1), 0.0)

    def down_z(v):
        return jnp.where(not_first, pltpu.roll(v, SOURCES, 1), 0.0)

    def new_h(n, i):
        p, q = i & (PX - 1), (i + 1) & (PX - 1)
        e_x, e_y, e_z = ee[n, 0, p], ee[n, 1, p], ee[n, 2, p]
        e_yn, e_zn = ee[n, 1, q], ee[n, 2, q]
        h_x = hh[0, p] - TIME_STEP * ((pltpu.roll(e_z, PY - 1, 0) - e_z) - (up_z(e_y) - e_y))
        h_y = hh[1, p] - TIME_STEP * ((up_z(e_x) - e_x) - (e_zn - e_z))
        h_z = hh[2, p] - TIME_STEP * ((e_yn - e_y) - (pltpu.roll(e_x, PY - 1, 0) - e_x))
        hh[0, p], hh[1, p], hh[2, p] = h_x, h_y, h_z
        return h_x, h_y, h_z

    def new_e(n, i, h, h_before):
        p = i & (PX - 1)
        h_x, h_y, h_z = h
        h_yb, h_zb = h_before
        s = ss[p]
        e_x = ee[n, 0, p] + s * ((h_z - pltpu.roll(h_z, 1, 0)) - (h_y - down_z(h_y)))
        e_y = ee[n, 1, p] + s * ((h_x - down_z(h_x)) - (h_z - h_zb))
        e_z = ee[n, 2, p] + s * ((h_y - h_yb) - (h_x - pltpu.roll(h_x, 1, 0)))
        ee[n + 1, 0, p], ee[n + 1, 1, p], ee[n + 1, 2, p] = e_x, e_y, e_z

    for n in range(ITERS):
        left, right = -(HALO - n), BX + HALO - 1 - n
        h = new_h(n, jnp.int32(left))

        def plane(i, before, n=n):
            h = new_h(n, i)
            new_e(n, i, h, before)
            return h[1], h[2]

        lax.fori_loop(left + 1, right, plane, (h[1], h[2]))

    e_ref[...] = ee[ITERS, :, :BX, :BY]
    h_ref[...] = hh[:, :BX, :BY]

    even_lane = iota((BY, LANES), 1) % 2 == 0

    def gram(j, sums):
        c, p = j // BX, j % BX
        e = [ee[n + 1, c, p, pl.ds(0, BY)] for n in range(ITERS)]
        permit = permit_ref[p]
        f = [sum(w_ref[n, k] * e[n] for n in range(ITERS)) for k in range(FILTERS)]
        g = [v * permit for v in f]
        o = [jnp.where(even_lane, pltpu.roll(v, LANES - 1, 1), pltpu.roll(v, 1, 1)) for v in g]
        new = []
        for right in (g, o):
            for k in range(FILTERS):
                for l in range(k, FILTERS):
                    v = f[k] * right[l]
                    new.append(v[:8] + v[8:])
        return tuple(s + v for s, v in zip(sums, new))

    zero = jnp.zeros((8, LANES), jnp.float32)
    sums = lax.fori_loop(0, 3 * BX, gram, (zero,) * 20)
    row_of = iota((32, LANES), 0)
    rows = jnp.zeros((32, LANES), jnp.float32)
    at = 0
    for cross in range(2):
        for k in range(FILTERS):
            for l in range(k, FILTERS):
                line = jnp.sum(sums[at], axis=0, keepdims=True)
                rows = jnp.where(row_of == cross * 16 + k * 4 + l, line, rows)
                at += 1

    def entry(shape):
        j = iota(shape, 1)
        k, s, l, t = (j >> 4) & 3, (j >> 3) & 1, (j >> 1) & 3, j & 1
        source = jnp.where(k <= l, s, t)
        which = jnp.where(s == t, 0, 16) + jnp.minimum(k, l) * 4 + jnp.maximum(k, l)
        return jnp.where(j < 64, which, -1), source

    lane_source = (iota((LANES, LANES), 0) & 1 == entry((LANES, LANES))[1]).astype(jnp.float32)
    totals = jnp.dot(rows, lane_source, precision=lax.Precision.HIGHEST, preferred_element_type=jnp.float32)
    vector = jnp.sum(jnp.where(row_of == entry((32, LANES))[0], totals, 0.0), axis=0, keepdims=True)
    part_ref[...] = jnp.broadcast_to(vector[None], part_ref.shape)


def add_up(in_ref, out_ref):
    out_ref[...] = jnp.broadcast_to(jnp.sum(in_ref[...], axis=0, keepdims=True), out_ref.shape)


def finish(cells, in_ref, out_ref):
    vector = jnp.broadcast_to(jnp.sum(in_ref[...], axis=0), (8, LANES))
    picked = jnp.where(iota((8, LANES), 1) // 8 == iota((8, LANES), 0), vector, 0.0)
    fold = (iota((LANES, LANES), 0) % 8 == iota((LANES, LANES), 1)).astype(jnp.float32)
    total = jnp.dot(picked, fold, precision=lax.Precision.HIGHEST, preferred_element_type=jnp.float32)
    out_ref[...] = total[:, :8] / cells


def swap_pairs(count, odd):
    if not odd:
        return [(i, i ^ 1) for i in range(count)]
    return [(i, (i + 1) % count if i % 2 else (i - 1) % count) for i in range(count)]


def sum_groups(n_gx, n_gy):
    planes, columns = {}, {}
    for gx in range(n_gx):
        for gy in range(n_gy):
            y, z_high, x = gx // 8, (gx // 4) % 2, gx % 4
            z, core = z_high * 8 + gy // 2, gy % 2
            planes.setdefault(z, []).append(gx * n_gy + gy)
            columns.setdefault((x, y, core), []).append(gx * n_gy + gy)
    return list(planes.values()), list(columns.values())


def body(e_field, h_field, material, permittivity, frequencies):
    n_gx, n_gy = lax.axis_size("gx"), lax.axis_size("gy")
    weights = jnp.cos(frequencies[None, :] * (jnp.arange(1, ITERS + 1, dtype=jnp.float32)[:, None] * TIME_STEP))
    send_a, send_b = call(pack_x, (f32(XTILES, 8, LANES),) * 2, "pack_x", 3, size=1 << 20)(e_field, h_field, material)
    got_a = lax.ppermute(send_a, "gx", swap_pairs(n_gx, False))
    got_b = lax.ppermute(send_b, "gx", swap_pairs(n_gx, True))
    permit, scaled = call(own_cells, (f32(BX, BY, LANES),) * 2, "own_cells", 2, smem=(1,), size=1 << 18)(
        material, permittivity
    )
    ext = (f32(3, PX, BY, LANES), f32(3, PX, BY, LANES), f32(PX, BY, LANES), f32(YTILES, 8, LANES), f32(YTILES, 8, LANES))
    ext_e, ext_h, ext_s, send_a, send_b = call(extend_x, ext, "extend_x", 6, smem=(5,), size=1 << 21)(
        e_field, h_field, scaled, got_a, got_b, permittivity
    )
    got_a = lax.ppermute(send_a, "gy", swap_pairs(n_gy, False))
    got_b = lax.ppermute(send_b, "gy", swap_pairs(n_gy, True))
    planes, columns = sum_groups(n_gx, n_gy)
    n_plane, n_column = len(planes[0]), len(columns[0])
    scratch = (
        pltpu.VMEM((ITERS + 1, 3, PX, PY, LANES), jnp.float32),
        pltpu.VMEM((3, PX, PY, LANES), jnp.float32),
        pltpu.VMEM((PX, PY, LANES), jnp.float32),
    )
    outs = (f32(3, BX, BY, LANES), f32(3, BX, BY, LANES), f32(n_plane, 1, LANES))
    e_out, h_out, part = call(steps, outs, "steps", 7, scratch=scratch, smem=(6,), flops=1 << 24, size=1 << 22)(
        ext_e, ext_h, ext_s, permit, got_a, got_b, weights
    )
    both = ("gx", "gy")
    part = lax.all_to_all(part, both, 0, 0, axis_index_groups=planes, tiled=True)
    part = call(add_up, f32(n_column, 1, LANES), "add_up", 1, size=1 << 14)(part)
    part = lax.all_to_all(part, both, 0, 0, axis_index_groups=columns, tiled=True)
    cells = float(BX * n_gx * BY * n_gy * NZ)

    def last(in_ref, out_ref):
        finish(cells, in_ref, out_ref)

    gram = call(last, f32(8, 8), "finish", 1, size=1 << 14)(part)
    return e_out, h_out, gram


def solution(mesh):
    in_specs = (P(None, "gx", "gy", None), P(None, "gx", "gy", None), P("gx", "gy", None), P(), P())
    out_specs = (P(None, "gx", "gy", None), P(None, "gx", "gy", None), P())
    return jax.shard_map(body, mesh=mesh, in_specs=in_specs, out_specs=out_specs, check_vma=False)
```

time: 370 us -> 109 us (0.29)
  local copies, waits for them, and re-layouts: 113 us -> 2.7 us
  blocking collectives: 104 us -> 42.8 us
  waiting for transfers between devices: 67.1 us -> 18.8 us
  starting transfers between devices: 77.3 us -> 30.3 us
  Pallas kernels: 0 us -> 13.2 us
  other arithmetic: 4.46 us -> 0.12 us
    mul x12 -> x0, local copies, waits for them, and re-layouts: 108 us -> none  [the longest x8 86.2 us: body(): filtered = filtered + weights[:, None, None, None, None] * e_field[None]]
    psum x1 -> x0, blocking collectives: 104 us -> none  [body(): summed = lax.psum(local, ('gx', 'gy'))]
    ppermute x16 -> x4, waiting for transfers between devices: 67.1 us -> 18.8 us  [the longest x1 15.3 us: body(): got_b = lax.ppermute(send_b, 'gx', swap_pairs(n_gx, True))]
    ppermute x16 -> x4, starting transfers between devices: 77.3 us -> 30.3 us  [the longest x1 19.4 us: body(): got_b = lax.ppermute(send_b, 'gx', swap_pairs(n_gx, True))]
    all_to_all x0 -> x2, blocking collectives: none -> 42.8 us  [the longest x1 26 us: body(): lax.all_to_all(part, both, 0, 0, axis_index_groups=columns, tiled=True)]
    pallas_call x0 -> x6, Pallas kernels: none -> 13.2 us  [the longest x1 10.8 us: body(): call(steps, outs, 'steps', 7, scratch=scratch, smem=(6,), flops=1 << 24,...]
  transfers between devices with their start and end apart: 16 -> 4, of which waited for: 11 -> 2; matrix products, arithmetic and copies ran while one was open for 25% -> 0% of each run, Pallas kernels for 0% -> 1%
where the time goes in v1:
time: 109 us
  blocking collectives  42.8 us (39%)
  starting transfers between devices  30.3 us (28%)
  waiting for transfers between devices  18.8 us (17%)
  Pallas kernels  13.2 us (12%)
  local copies, waits for them, and re-layouts  2.7 us (2%)
    all_to_all x1, blocking collectives, body(): lax.all_to_all(part, both, 0, 0, axis_index_groups=columns, tiled=True)  26 us
    ppermute x1, starting transfers between devices, body(): got_b = lax.ppermute(send_b, 'gx', swap_pairs(n_gx, True))  19.4 us
    all_to_all x1, blocking collectives, body(): lax.all_to_all(part, both, 0, 0, axis_index_groups=planes, tiled=True)  16.7 us
    ppermute x1, waiting for transfers between devices, body(): got_b = lax.ppermute(send_b, 'gx', swap_pairs(n_gx, True))  15.3 us
    pallas_call x1, Pallas kernels, body(): call(steps, outs, 'steps', 7, scratch=scratch, smem=(6,), flops=1 << 24,...  10.8 us
    ppermute x1, starting transfers between devices, body(): got_a = lax.ppermute(send_a, 'gx', swap_pairs(n_gx, False))  4.08 us
    ppermute x1, starting transfers between devices, body(): got_b = lax.ppermute(send_b, 'gy', swap_pairs(n_gy, True))  3.98 us
    ppermute x1, waiting for transfers between devices, body(): got_b = lax.ppermute(send_b, 'gy', swap_pairs(n_gy, True))  3.55 us
  transfers between devices with their start and end apart: 4, of which 2 were waited for; matrix products, arithmetic and copies ran while one was open for 0% of the time, Pallas kernels for 1%

profile of v1, /device:TPU:1, one launch (start us, length us, event | category | flops | bytes accessed | tf_op | source)
XLA Modules:
  0.0 108.6 jit_solution(16671658536897225852)
XLA Ops:
  0.6 0.0 copy-start
  0.6 0.9 copy-done
  1.6 0.9 copy-done.2
  2.5 0.8 copy-done.3
  3.3 0.2 pack_x.1
  3.5 0.0 copy-start.4
  3.5 4.1 %collective-permute-start = (f32[49,8,128]{2,1,0:T(8,128)S(1)}, f32[49,8,128]{2,1,0:T(8,128)S(1)}, u32[]{:S(2)}, u32[]{:S(2)}) collective-permute-start(f32[49,8,128]{2,1,0:T(8,128)S(1)} %get-tuple-element.16), channel_id=1, source_target_pairs={{0,16},{16,0},{32,48},{48,32},{64,80},{80,64},{96,112},{112,96},{1... | collective-permute-start | bytes 602120 | tf_op jit(solution)/shard_map/ppermute | solution.py:262
  7.6 19.4 %collective-permute-start.1 = (f32[49,8,128]{2,1,0:T(8,128)S(1)}, f32[49,8,128]{2,1,0:T(8,128)S(1)}, u32[]{:S(2)}, u32[]{:S(2)}) collective-permute-start(f32[49,8,128]{2,1,0:T(8,128)S(1)} %get-tuple-element.17), channel_id=1, source_target_pairs={{0,496},{16,32},{32,16},{48,64},{64,48},{80,96},{96,80},{112,128},... | collective-permute-start | bytes 602120 | tf_op jit(solution)/shard_map/ppermute | solution.py:263
  27.0 0.0 copy-done.4
  27.0 0.7 own_cells.1
  27.7 0.0 collective-permute-done.a_ref
  27.8 15.3 %collective-permute-done.1.b_ref = f32[49,8,128]{2,1,0:T(8,128)S(1)} collective-permute-done((f32[49,8,128]{2,1,0:T(8,128)S(1)}, f32[49,8,128]{2,1,0:T(8,128)S(1)}, u32[]{:S(2)}, u32[]{:S(2)}) %collective-permute-start.1) | collective-permute-done | bytes 200736 | tf_op jit(solution)/shard_map/ppermute | solution.py:263
  43.0 0.0 copy-done.1
  43.0 0.7 extend_x.1
  43.8 2.8 %collective-permute-start.2 = (f32[56,8,128]{2,1,0:T(8,128)S(1)}, f32[56,8,128]{2,1,0:T(8,128)S(1)}, u32[]{:S(2)}, u32[]{:S(2)}) collective-permute-start(f32[56,8,128]{2,1,0:T(8,128)S(1)} %get-tuple-element.22), channel_id=1, source_target_pairs={{0,1},{1,0},{2,3},{3,2},{4,5},{5,4},{6,7},{7,6},{8,9},{9,8},{10,11... | collective-permute-start | bytes 688136 | tf_op jit(solution)/shard_map/ppermute | solution.py:271
  46.6 0.0 copy-start.5
  46.6 4.0 %collective-permute-start.3 = (f32[56,8,128]{2,1,0:T(8,128)S(1)}, f32[56,8,128]{2,1,0:T(8,128)S(1)}, u32[]{:S(2)}, u32[]{:S(2)}) collective-permute-start(f32[56,8,128]{2,1,0:T(8,128)S(1)} %get-tuple-element.23), channel_id=1, source_target_pairs={{0,15},{1,2},{2,1},{3,4},{4,3},{5,6},{6,5},{7,8},{8,7},{9,10},{10,... | collective-permute-start | bytes 688136 | tf_op jit(solution)/shard_map/ppermute | solution.py:272
  50.6 0.1 multiply_cosine_fusion.w_ref
  50.7 0.0 collective-permute-done.2.ya_ref
  50.7 3.5 %collective-permute-done.3.yb_ref = f32[56,8,128]{2,1,0:T(8,128)S(1)} collective-permute-done((f32[56,8,128]{2,1,0:T(8,128)S(1)}, f32[56,8,128]{2,1,0:T(8,128)S(1)}, u32[]{:S(2)}, u32[]{:S(2)}) %collective-permute-start.3) | collective-permute-done | bytes 229408 | tf_op jit(solution)/shard_map/ppermute | solution.py:272
  54.3 10.8 %steps.1 = (f32[3,8,16,128]{3,2,1,0:T(8,128)}, f32[3,8,16,128]{3,2,1,0:T(8,128)}, f32[32,1,128]{2,1,0:T(1,128)S(1)}) custom-call(f32[3,16,16,128]{3,2,1,0:T(8,128)S(1)} %get-tuple-element.18.xe_ref, f32[3,16,16,128]{3,2,1,0:T(8,128)S(1)} %get-tuple-element.19.xh_ref, f32[16,16,128]{2,1,0:T(8,128)S(1)} %get-tuple-element.20.xs_ref, ...), custom_call_target="tpu_custom_call" | custom-call | flops 16777216 | bytes 4194304 | tf_op jit(solution)/shard_map/steps/pallas_call | solution.py:281
  65.1 16.7 %all_to_all.10.in_ref = f32[32,1,128]{2,1,0:T(1,128)S(1)} all-to-all(f32[32,1,128]{2,1,0:T(1,128)S(1)} %get-tuple-element.26), channel_id=1, replica_groups={{0,1,16,17,32,33,48,49,128,129,144,145,160,161,176,177,256,257,272,273,..., dimensions={0} | all-to-all | bytes 32768 | tf_op jit(solution)/shard_map/all_to_all | solution.py:285
  81.9 26.0 %all_to_all.11.in_ref = f32[16,1,128]{2,1,0:T(1,128)S(1)} all-to-all(f32[16,1,128]{2,1,0:T(1,128)S(1)} %add_up.1), channel_id=1, replica_groups={{0,2,4,6,8,10,12,14,64,66,68,70,72,74,76,78},{1,3,5,7,9,11,13,15,65,67,..., dimensions={0} | all-to-all | bytes 16384 | tf_op jit(solution)/shard_map/all_to_all | solution.py:287
  107.9 0.8 finish.1
  (6 shorter events, 0.1 us)
Async XLA Ops:
  0.6 0.9 copy-start
  1.6 0.9 copy-start.2
  2.5 0.8 copy-start.3
  3.3 39.7 %copy-start.1 = (f32[3,8,16,128]{3,2,1,0:T(8,128)S(1)}, f32[3,8,16,128]{3,2,1,0:T(8,128)}, u32[]{:S(2)}) copy-start(f32[3,8,16,128]{3,2,1,0:T(8,128)} %e_ref.3) | copy-start | bytes 589828
  3.5 23.5 %copy-start.4 = (f32[4]{0:T(128)S(1)}, f32[4]{0:T(128)}, u32[]{:S(2)}) copy-start(f32[4]{0:T(128)} %p_ref.3) | copy-start | bytes 52
  3.5 24.2 %collective-permute-start = (f32[49,8,128]{2,1,0:T(8,128)S(1)}, f32[49,8,128]{2,1,0:T(8,128)S(1)}, u32[]{:S(2)}, u32[]{:S(2)}) collective-permute-start(f32[49,8,128]{2,1,0:T(8,128)S(1)} %get-tuple-element.16), channel_id=1, source_target_pairs={{0,16},{16,0},{32,48},{48,32},{64,80},{80,64},{96,112},{112,96},{1... | collective-permute-start | bytes 602120 | tf_op jit(solution)/shard_map/ppermute | solution.py:262
  7.6 35.4 %collective-permute-start.1 = (f32[49,8,128]{2,1,0:T(8,128)S(1)}, f32[49,8,128]{2,1,0:T(8,128)S(1)}, u32[]{:S(2)}, u32[]{:S(2)}) collective-permute-start(f32[49,8,128]{2,1,0:T(8,128)S(1)} %get-tuple-element.17), channel_id=1, source_target_pairs={{0,496},{16,32},{32,16},{48,64},{64,48},{80,96},{96,80},{112,128},... | collective-permute-start | bytes 602120 | tf_op jit(solution)/shard_map/ppermute | solution.py:263
  43.8 6.9 %collective-permute-start.2 = (f32[56,8,128]{2,1,0:T(8,128)S(1)}, f32[56,8,128]{2,1,0:T(8,128)S(1)}, u32[]{:S(2)}, u32[]{:S(2)}) collective-permute-start(f32[56,8,128]{2,1,0:T(8,128)S(1)} %get-tuple-element.22), channel_id=1, source_target_pairs={{0,1},{1,0},{2,3},{3,2},{4,5},{5,4},{6,7},{7,6},{8,9},{9,8},{10,11... | collective-permute-start | bytes 688136 | tf_op jit(solution)/shard_map/ppermute | solution.py:271
  46.6 4.0 %copy-start.5 = (f32[4]{0:T(128)S(1)}, f32[4]{0:T(128)}, u32[]{:S(2)}) copy-start(f32[4]{0:T(128)} %param.9) | copy-start | bytes 52
  46.6 7.7 %collective-permute-start.3 = (f32[56,8,128]{2,1,0:T(8,128)S(1)}, f32[56,8,128]{2,1,0:T(8,128)S(1)}, u32[]{:S(2)}, u32[]{:S(2)}) collective-permute-start(f32[56,8,128]{2,1,0:T(8,128)S(1)} %get-tuple-element.23), channel_id=1, source_target_pairs={{0,15},{1,2},{2,1},{3,4},{4,3},{5,6},{6,5},{7,8},{8,7},{9,10},{10,... | collective-permute-start | bytes 688136 | tf_op jit(solution)/shard_map/ppermute | solution.py:272

commit v2 on v1

--- a/solution.py
+++ b/solution.py
@@ -17,9 +17,10 @@
 PX = BX + 2 * HALO
 PY = BY + 2 * HALO
 XTILES = 49
-YTILES = 7 * PX // 2
+YTILES = 7 * BX // 2
 
 VMEM = pl.BlockSpec(memory_space=pltpu.VMEM)
+HBM = pl.BlockSpec(memory_space=pltpu.HBM)
 SMEM = pl.BlockSpec(memory_space=pltpu.SMEM)
 PARAMS = pltpu.CompilerParams(vmem_limit_bytes=32 * 1024 * 1024)
 
@@ -28,12 +29,13 @@
     return lax.broadcasted_iota(jnp.int32, shape, dim)
 
 
-def call(kernel, outs, name, n_in, scratch=(), smem=(), flops=0, size=0):
+def call(kernel, outs, name, n_in, scratch=(), smem=(), hbm=(), hbm_out=(), flops=0, size=0):
+    out_specs = tuple(HBM if i in hbm_out else VMEM for i in range(len(outs))) if isinstance(outs, tuple) else VMEM
     return pl.pallas_call(
         kernel,
         out_shape=outs,
-        in_specs=[SMEM if i in smem else VMEM for i in range(n_in)],
-        out_specs=jax.tree.map(lambda _: VMEM, outs),
+        in_specs=[SMEM if i in smem else HBM if i in hbm else VMEM for i in range(n_in)],
+        out_specs=out_specs,
         scratch_shapes=list(scratch),
         compiler_params=PARAMS,
         cost_estimate=pl.CostEstimate(flops=flops, bytes_accessed=size, transcendentals=0),
@@ -45,26 +47,37 @@
     return jax.ShapeDtypeStruct(shape, jnp.float32)
 
 
-def pack_x(e_ref, h_ref, m_ref, a_ref, b_ref):
+def x_parts(e, h, wide, narrow):
+    return ((e, 0, 4, wide), (e, 1, 4, wide), (e, 2, 4, wide), (h, 0, 3, narrow), (h, 1, 4, wide), (h, 2, 4, wide))
+
+
+def pack_x(e_ref, h_ref, m_ref, a_ref, b_ref, edge, sems):
     even = lax.rem(lax.axis_index("gx"), 2) == 0
-    row, col = iota((NZ, LANES), 0), iota((NZ, LANES), 1)
-    low = (col == row).astype(jnp.bfloat16)
-    high = (col == row + NZ).astype(jnp.bfloat16)
-    for out, upper in ((a_ref, even), (b_ref, jnp.logical_not(even))):
+    copies = []
+    for side, (out, upper) in enumerate(((a_ref, even), (b_ref, jnp.logical_not(even)))):
         wide = jnp.where(upper, BX - HALO, 0)
         narrow = jnp.where(upper, BX - HALO + 1, 0)
-        tile = 0
-        for ref, c, n, start in (
-            (e_ref, 0, 4, wide), (e_ref, 1, 4, wide), (e_ref, 2, 4, wide),
-            (h_ref, 0, 3, narrow), (h_ref, 1, 4, wide), (h_ref, 2, 4, wide),
-        ):
-            out[pl.ds(tile, 2 * n)] = ref[c, pl.ds(start, n)].reshape(2 * n, 8, LANES)
-            tile += 2 * n
+        copies.append(pltpu.make_async_copy(m_ref.at[pl.ds(narrow, 3)], edge.at[side], sems.at[side, 6]))
+        row = 0
+        for i, (ref, c, n, start) in enumerate(x_parts(e_ref, h_ref, wide, narrow)):
+            src = ref.at[c, pl.ds(pl.multiple_of(start * BY, BY), n * BY)]
+            copies.append(pltpu.make_async_copy(src, out.at[pl.ds(row, n * BY)], sems.at[side, i]))
+            row += n * BY
+    for copy in copies:
+        copy.start()
+    r, col = iota((NZ, LANES), 0), iota((NZ, LANES), 1)
+    low = (col == r).astype(jnp.bfloat16)
+    high = (col == r + NZ).astype(jnp.bfloat16)
+    for side, out in enumerate((a_ref, b_ref)):
+        copies[7 * side].wait()
         for i in range(3):
-            cells = m_ref[narrow + i].astype(jnp.float32).astype(jnp.bfloat16)
-            out[tile + i] = jnp.dot(cells[:8], low, preferred_element_type=jnp.float32) + jnp.dot(
-                cells[8:], high, preferred_element_type=jnp.float32
-            )
+            cells = edge[side, i].astype(jnp.float32).astype(jnp.bfloat16)
+            out[pl.ds(8 * (XTILES - 3 + i), 8)] = jnp.dot(
+                cells[:8], low, preferred_element_type=jnp.float32
+            ) + jnp.dot(cells[8:], high, preferred_element_type=jnp.float32)
+    for i, copy in enumerate(copies):
+        if i % 7:
+            copy.wait()
 
 
 def look_up(index, table_ref):
@@ -84,62 +97,71 @@
     scaled_ref[...] = (TIME_STEP / permit).reshape(BX, BY, LANES)
 
 
-def extend_x(e_ref, h_ref, s_ref, a_ref, b_ref, p_ref, ye_ref, yh_ref, ys_ref, ya_ref, yb_ref):
+def pack_y(refs, ya_ref, yb_ref):
+    even = lax.rem(lax.axis_index("gy"), 2) == 0
+    first = iota((8, LANES), 0) < HALO
+    for f, ref in enumerate(refs):
+        for p in range(4):
+            top = jnp.where(first, pltpu.roll(ref[p, 8:16], HALO, 0), ref[p + 4, 8:16])
+            bottom = jnp.where(first, ref[p, 0:8], pltpu.roll(ref[p + 4, 0:8], HALO, 0))
+            ya_ref[f * 4 + p] = jnp.where(even, top, bottom)
+            yb_ref[f * 4 + p] = jnp.where(even, bottom, top)
+
+
+def unpack_y(refs, base, ya_ref, yb_ref):
+    even = lax.rem(lax.axis_index("gy"), 2) == 0
+    first = iota((8, LANES), 0) < HALO
+    for f, ref in enumerate(refs):
+        for p in range(4):
+            a, b = ya_ref[f * 4 + p], yb_ref[f * 4 + p]
+            after, before = jnp.where(even, a, b), jnp.where(even, b, a)
+            ref[base + p, BY:PY] = jnp.where(first, after, pltpu.roll(before, HALO, 0))
+            ref[base + p + 4, BY:PY] = jnp.where(first, pltpu.roll(after, HALO, 0), before)
+
+
+def fields(e, h, s):
+    return [e.at[c] for c in range(3)] + [h.at[c] for c in range(3)] + [s]
+
+
+def own_rows(e_ref, h_ref, s_ref, ya_ref, yb_ref):
+    pack_y(fields(e_ref, h_ref, s_ref), ya_ref, yb_ref)
+
+
+def ghost_planes(a_ref, b_ref, p_ref, e_ref, h_ref, s_ref, ya_ref, yb_ref):
     even = lax.rem(lax.axis_index("gx"), 2) == 0
-    row, col = iota((LANES, LANES), 0), iota((LANES, LANES), 1)
-    low = (col // SOURCES == row).astype(jnp.bfloat16)
-    high = (col // SOURCES == row - NZ).astype(jnp.bfloat16)
-    ye_ref[:, :BX] = e_ref[...]
-    yh_ref[:, :BX] = h_ref[...]
-    ys_ref[:BX] = s_ref[...]
+    r, col = iota((LANES, LANES), 0), iota((LANES, LANES), 1)
+    low = (col // SOURCES == r).astype(jnp.bfloat16)
+    high = (col // SOURCES == r - NZ).astype(jnp.bfloat16)
     for src, after in ((a_ref, even), (b_ref, jnp.logical_not(even))):
-        wide = jnp.where(after, BX, BX + HALO)
-        narrow = jnp.where(after, BX, BX + HALO + 1)
-        tile = 0
-        for ref, c, n, start in (
-            (ye_ref, 0, 4, wide), (ye_ref, 1, 4, wide), (ye_ref, 2, 4, wide),
-            (yh_ref, 0, 3, narrow), (yh_ref, 1, 4, wide), (yh_ref, 2, 4, wide),
-        ):
-            ref[c, pl.ds(start, n)] = src[pl.ds(tile, 2 * n)].reshape(n, BY, LANES)
-            tile += 2 * n
-        cells = src[pl.ds(tile, 3)].reshape(24, LANES).astype(jnp.bfloat16)
+        wide = jnp.where(after, 0, HALO)
+        narrow = jnp.where(after, 0, HALO + 1)
+        row = 0
+        for ref, c, n, start in x_parts(e_ref, h_ref, wide, narrow):
+            ref[c, pl.ds(start, n)] = src[pl.ds(row, n * BY)].reshape(n, BY, LANES)
+            row += n * BY
+        cells = src[pl.ds(row, 24)].astype(jnp.bfloat16)
         for half, spread in ((0, low), (8, high)):
             index = jnp.dot(cells, spread, preferred_element_type=jnp.float32)
             value = TIME_STEP / look_up(index, p_ref)
             for i in range(3):
-                ys_ref[narrow + i, pl.ds(half, 8)] = value[8 * i : 8 * i + 8]
+                s_ref[narrow + i, pl.ds(half, 8)] = value[8 * i : 8 * i + 8]
     zero = jnp.zeros((BY, LANES), jnp.float32)
-    yh_ref[0, BX + HALO] = zero
-    yh_ref[0, BX + HALO - 1] = zero
-    ys_ref[BX + HALO] = zero
-    ys_ref[BX + HALO - 1] = zero
-    fill_y(ye_ref, yh_ref, ys_ref, ya_ref, yb_ref)
-
-
-def fill_y(ye_ref, yh_ref, ys_ref, ya_ref, yb_ref):
-    even = lax.rem(lax.axis_index("gy"), 2) == 0
-    first = iota((8, LANES), 0) < HALO
-    for f in range(7):
-        ref = (ye_ref, ye_ref, ye_ref, yh_ref, yh_ref, yh_ref)[f].at[f % 3] if f < 6 else ys_ref
-        for p in range(PX // 2):
-            top = jnp.where(first, pltpu.roll(ref[p, 8:16], HALO, 0), ref[p + PX // 2, 8:16])
-            bottom = jnp.where(first, ref[p, 0:8], pltpu.roll(ref[p + PX // 2, 0:8], HALO, 0))
-            ya_ref[f * 8 + p] = jnp.where(even, top, bottom)
-            yb_ref[f * 8 + p] = jnp.where(even, bottom, top)
-
-
-def steps(xe_ref, xh_ref, xs_ref, permit_ref, ya_ref, yb_ref, w_ref, e_ref, h_ref, part_ref, ee, hh, ss):
-    even = lax.rem(lax.axis_index("gy"), 2) == 0
-    first = iota((8, LANES), 0) < HALO
-    for f in range(7):
-        src = xe_ref.at[f % 3] if f < 3 else xh_ref.at[f % 3] if f < 6 else xs_ref
-        dst = ee.at[0, f % 3] if f < 3 else hh.at[f % 3] if f < 6 else ss
-        dst[:, :BY] = src[...]
-        for p in range(PX // 2):
-            a, b = ya_ref[f * 8 + p], yb_ref[f * 8 + p]
-            after, before = jnp.where(even, a, b), jnp.where(even, b, a)
-            dst[p, BY:PY] = jnp.where(first, after, pltpu.roll(before, HALO, 0))
-            dst[p + PX // 2, BY:PY] = jnp.where(first, pltpu.roll(after, HALO, 0), before)
+    for ref in (h_ref.at[0], s_ref):
+        ref[HALO - 1] = zero
+        ref[HALO] = zero
+    pack_y(fields(e_ref, h_ref, s_ref), ya_ref, yb_ref)
+
+
+def steps(
+    own_e, own_h, own_s, permit_ref, ghost_e, ghost_h, ghost_s, ya1, yb1, ya2, yb2, w_ref,
+    e_out, h_out, part_ref, ee, hh, ss, sems,
+):
+    extended = fields(ee.at[0], hh, ss)
+    for dst, own, ghost in zip(extended, fields(own_e, own_h, own_s), fields(ghost_e, ghost_h, ghost_s)):
+        dst[:BX, :BY] = own[...]
+        dst[BX:, :BY] = ghost[...]
+    unpack_y(extended, 0, ya1, yb1)
+    unpack_y(extended, BX, ya2, yb2)
 
     lane = iota((PY, LANES), 1)
     not_last, not_first = lane < LANES - SOURCES, lane >= SOURCES
@@ -179,10 +201,15 @@
             new_e(n, i, h, before)
             return h[1], h[2]
 
-        lax.fori_loop(left + 1, right, plane, (h[1], h[2]))
-
-    e_ref[...] = ee[ITERS, :, :BX, :BY]
-    h_ref[...] = hh[:, :BX, :BY]
+        lax.fori_loop(left + 1, right, plane, (h[1], h[2]), unroll=True)
+
+    own = (slice(None), pl.ds(0, BX), pl.ds(0, BY))
+    copies = [
+        pltpu.make_async_copy(ee.at[(ITERS,) + own], e_out, sems.at[0]),
+        pltpu.make_async_copy(hh.at[own], h_out, sems.at[1]),
+    ]
+    for copy in copies:
+        copy.start()
 
     even_lane = iota((BY, LANES), 1) % 2 == 0
 
@@ -202,7 +229,7 @@
         return tuple(s + v for s, v in zip(sums, new))
 
     zero = jnp.zeros((8, LANES), jnp.float32)
-    sums = lax.fori_loop(0, 3 * BX, gram, (zero,) * 20)
+    sums = lax.fori_loop(0, 3 * BX, gram, (zero,) * 20, unroll=4)
     row_of = iota((32, LANES), 0)
     rows = jnp.zeros((32, LANES), jnp.float32)
     at = 0
@@ -224,6 +251,8 @@
     totals = jnp.dot(rows, lane_source, precision=lax.Precision.HIGHEST, preferred_element_type=jnp.float32)
     vector = jnp.sum(jnp.where(row_of == entry((32, LANES))[0], totals, 0.0), axis=0, keepdims=True)
     part_ref[...] = jnp.broadcast_to(vector[None], part_ref.shape)
+    for copy in copies:
+        copy.wait()
 
 
 def add_up(in_ref, out_ref):
@@ -258,29 +287,41 @@
 def body(e_field, h_field, material, permittivity, frequencies):
     n_gx, n_gy = lax.axis_size("gx"), lax.axis_size("gy")
     weights = jnp.cos(frequencies[None, :] * (jnp.arange(1, ITERS + 1, dtype=jnp.float32)[:, None] * TIME_STEP))
-    send_a, send_b = call(pack_x, (f32(XTILES, 8, LANES),) * 2, "pack_x", 3, size=1 << 20)(e_field, h_field, material)
+    x_message = (f32(XTILES * 8, LANES),) * 2
+    y_message = (f32(YTILES, 8, LANES),) * 2
+    scratch = (pltpu.VMEM((2, 3, BY, NZ), jnp.int32), pltpu.SemaphoreType.DMA((2, 7)))
+    send_a, send_b = call(pack_x, x_message, "pack_x", 3, scratch=scratch, hbm=(0, 1, 2), size=1 << 20)(
+        *(
+            pltpu.with_memory_space_constraint(v, pltpu.HBM)
+            for v in (e_field.reshape(3, BX * BY, LANES), h_field.reshape(3, BX * BY, LANES), material)
+        )
+    )
     got_a = lax.ppermute(send_a, "gx", swap_pairs(n_gx, False))
     got_b = lax.ppermute(send_b, "gx", swap_pairs(n_gx, True))
     permit, scaled = call(own_cells, (f32(BX, BY, LANES),) * 2, "own_cells", 2, smem=(1,), size=1 << 18)(
         material, permittivity
     )
-    ext = (f32(3, PX, BY, LANES), f32(3, PX, BY, LANES), f32(PX, BY, LANES), f32(YTILES, 8, LANES), f32(YTILES, 8, LANES))
-    ext_e, ext_h, ext_s, send_a, send_b = call(extend_x, ext, "extend_x", 6, smem=(5,), size=1 << 21)(
-        e_field, h_field, scaled, got_a, got_b, permittivity
-    )
-    got_a = lax.ppermute(send_a, "gy", swap_pairs(n_gy, False))
-    got_b = lax.ppermute(send_b, "gy", swap_pairs(n_gy, True))
+    send_a, send_b = call(own_rows, y_message, "own_rows", 3, size=1 << 20)(e_field, h_field, scaled)
+    ya1 = lax.ppermute(send_a, "gy", swap_pairs(n_gy, False))
+    yb1 = lax.ppermute(send_b, "gy", swap_pairs(n_gy, True))
+    ghosts = (f32(3, 2 * HALO, BY, LANES), f32(3, 2 * HALO, BY, LANES), f32(2 * HALO, BY, LANES)) + y_message
+    ghost_e, ghost_h, ghost_s, send_a, send_b = call(ghost_planes, ghosts, "ghost_planes", 3, smem=(2,), size=1 << 20)(
+        got_a, got_b, permittivity
+    )
+    ya2 = lax.ppermute(send_a, "gy", swap_pairs(n_gy, False))
+    yb2 = lax.ppermute(send_b, "gy", swap_pairs(n_gy, True))
     planes, columns = sum_groups(n_gx, n_gy)
     n_plane, n_column = len(planes[0]), len(columns[0])
     scratch = (
         pltpu.VMEM((ITERS + 1, 3, PX, PY, LANES), jnp.float32),
         pltpu.VMEM((3, PX, PY, LANES), jnp.float32),
         pltpu.VMEM((PX, PY, LANES), jnp.float32),
+        pltpu.SemaphoreType.DMA((2,)),
     )
     outs = (f32(3, BX, BY, LANES), f32(3, BX, BY, LANES), f32(n_plane, 1, LANES))
-    e_out, h_out, part = call(steps, outs, "steps", 7, scratch=scratch, smem=(6,), flops=1 << 24, size=1 << 22)(
-        ext_e, ext_h, ext_s, permit, got_a, got_b, weights
-    )
+    e_out, h_out, part = call(
+        steps, outs, "steps", 12, scratch=scratch, smem=(11,), hbm_out=(0, 1), flops=1 << 24, size=1 << 22
+    )(e_field, h_field, scaled, permit, ghost_e, ghost_h, ghost_s, ya1, yb1, ya2, yb2, weights)
     both = ("gx", "gy")
     part = lax.all_to_all(part, both, 0, 0, axis_index_groups=planes, tiled=True)
     part = call(add_up, f32(n_column, 1, LANES), "add_up", 1, size=1 << 14)(part)

time: 109 us -> 99.8 us (0.916)
  waiting for transfers between devices: 18.8 us -> 11.9 us
  starting transfers between devices: 30.3 us -> 36.8 us
  Pallas kernels: 13.2 us -> 7.61 us
  local copies, waits for them, and re-layouts: 2.7 us -> 0.03 us
    ppermute x2 -> x4, starting transfers between devices: 6.78 us -> 13.4 us  [the longest x1 4.42 us: body(): yb2 = lax.ppermute(send_b, 'gy', swap_pairs(n_gy, True))]
    ppermute x1, waiting for transfers between devices: 15.3 us -> 9.55 us  [body(): got_b = lax.ppermute(send_b, 'gx', swap_pairs(n_gx, True))]
    pallas_call x3 -> x4, Pallas kernels: 11.7 us -> 6.11 us  [the longest x1 4.09 us: body(): call(steps, outs, 'steps', 12, scratch=scratch, smem=(11,), hbm_out=(0, 1...]
    unnamed x12 -> x10, local copies, waits for them, and re-layouts: 2.7 us -> 0.03 us
    all_to_all x1, blocking collectives: 26 us -> 24.4 us  [body(): lax.all_to_all(part, both, 0, 0, axis_index_groups=columns, tiled=True)]
    ppermute x2 -> x4, waiting for transfers between devices: 3.55 us -> 2.32 us  [the longest x1 2.31 us: body(): yb2 = lax.ppermute(send_b, 'gy', swap_pairs(n_gy, True))]
    all_to_all x1, blocking collectives: 16.7 us -> 17.8 us  [body(): lax.all_to_all(part, both, 0, 0, axis_index_groups=planes, tiled=True)]
  transfers between devices with their start and end apart: 4 -> 6, of which waited for: 2 -> 2; matrix products, arithmetic and copies ran while one was open for 0% -> 0% of each run, Pallas kernels for 1% -> 1%
where the time goes in v2:
time: 99.8 us; the launch traced here: 99.4 us
  blocking collectives  42.2 us (42%)
  starting transfers between devices  36.8 us (37%)
  waiting for transfers between devices  11.9 us (12%)
  Pallas kernels  7.61 us (8%)
    all_to_all x1, blocking collectives, body(): lax.all_to_all(part, both, 0, 0, axis_index_groups=columns, tiled=True)  24.4 us
    ppermute x1, starting transfers between devices, body(): got_b = lax.ppermute(send_b, 'gx', swap_pairs(n_gx, True))  19.4 us
    all_to_all x1, blocking collectives, body(): lax.all_to_all(part, both, 0, 0, axis_index_groups=planes, tiled=True)  17.8 us
    ppermute x1, waiting for transfers between devices, body(): got_b = lax.ppermute(send_b, 'gx', swap_pairs(n_gx, True))  9.55 us
    ppermute x1, starting transfers between devices, body(): yb2 = lax.ppermute(send_b, 'gy', swap_pairs(n_gy, True))  4.42 us
    pallas_call x1, Pallas kernels, body(): call(steps, outs, 'steps', 12, scratch=scratch, smem=(11,), hbm_out=(0, 1...  4.09 us
    ppermute x1, starting transfers between devices, body(): got_a = lax.ppermute(send_a, 'gx', swap_pairs(n_gx, False))  3.95 us
    ppermute x1, starting transfers between devices, body(): ya2 = lax.ppermute(send_a, 'gy', swap_pairs(n_gy, False))  3.3 us
  transfers between devices with their start and end apart: 6, of which 2 were waited for; matrix products, arithmetic and copies ran while one was open for 0% of the time, Pallas kernels for 1%

profile of v2, /device:TPU:1, one launch (start us, length us, event | category | flops | bytes accessed | tf_op | source)
XLA Modules:
  0.0 99.4 jit_solution(555160475503322356)
XLA Ops:
  0.6 0.0 copy-start.2
  0.6 0.0 copy-start
  0.7 1.3 %pack_x.1 = (f32[392,128]{1,0:T(8,128)S(1)}, f32[392,128]{1,0:T(8,128)S(1)}) custom-call(f32[3,128,128]{2,1,0:T(8,128)} %bitcast.2, f32[3,128,128]{2,1,0:T(8,128)} %bitcast.3, s32[8,16,64]{2,1,0:T(8,128)} %m_ref.3), custom_call_target="tpu_custom_call" | custom-call | bytes 1048576 | tf_op jit(solution)/shard_map/pack_x/pallas_call | solution.py:293
  1.9 0.0 copy-start.3
  1.9 3.9 %collective-permute-start = (f32[392,128]{1,0:T(8,128)S(1)}, f32[392,128]{1,0:T(8,128)S(1)}, u32[]{:S(2)}, u32[]{:S(2)}) collective-permute-start(f32[392,128]{1,0:T(8,128)S(1)} %get-tuple-element.19), channel_id=1, source_target_pairs={{0,16},{16,0},{32,48},{48,32},{64,80},{80,64},{96,112},{112,96},{1... | collective-permute-start | bytes 602120 | tf_op jit(solution)/shard_map/ppermute | solution.py:299
  5.9 19.4 %collective-permute-start.1 = (f32[392,128]{1,0:T(8,128)S(1)}, f32[392,128]{1,0:T(8,128)S(1)}, u32[]{:S(2)}, u32[]{:S(2)}) collective-permute-start(f32[392,128]{1,0:T(8,128)S(1)} %get-tuple-element.20), channel_id=1, source_target_pairs={{0,496},{16,32},{32,16},{48,64},{64,48},{80,96},{96,80},{112,128},... | collective-permute-start | bytes 602120 | tf_op jit(solution)/shard_map/ppermute | solution.py:300
  25.4 0.7 own_cells.1
  26.1 3.1 %collective-permute-start.2 = (f32[28,8,128]{2,1,0:T(8,128)S(1)}, f32[28,8,128]{2,1,0:T(8,128)S(1)}, u32[]{:S(2)}, u32[]{:S(2)}) collective-permute-start(f32[28,8,128]{2,1,0:T(8,128)S(1)} %get-tuple-element.24), channel_id=1, source_target_pairs={{0,1},{1,0},{2,3},{3,2},{4,5},{5,4},{6,7},{7,6},{8,9},{9,8},{10,11... | collective-permute-start | bytes 344072 | tf_op jit(solution)/shard_map/ppermute | solution.py:305
  29.3 2.5 %collective-permute-start.3 = (f32[28,8,128]{2,1,0:T(8,128)S(1)}, f32[28,8,128]{2,1,0:T(8,128)S(1)}, u32[]{:S(2)}, u32[]{:S(2)}) collective-permute-start(f32[28,8,128]{2,1,0:T(8,128)S(1)} %get-tuple-element.25), channel_id=1, source_target_pairs={{0,15},{1,2},{2,1},{3,4},{4,3},{5,6},{6,5},{7,8},{8,7},{9,10},{10,... | collective-permute-start | bytes 344072 | tf_op jit(solution)/shard_map/ppermute | solution.py:306
  31.8 0.0 collective-permute-done.a_ref
  31.8 9.5 %collective-permute-done.1.b_ref = f32[392,128]{1,0:T(8,128)S(1)} collective-permute-done((f32[392,128]{1,0:T(8,128)S(1)}, f32[392,128]{1,0:T(8,128)S(1)}, u32[]{:S(2)}, u32[]{:S(2)}) %collective-permute-start.1) | collective-permute-done | bytes 200736 | tf_op jit(solution)/shard_map/ppermute | solution.py:300
  41.4 0.7 ghost_planes.1
  42.1 0.0 copy-start.4
  42.1 3.3 %collective-permute-start.4 = (f32[28,8,128]{2,1,0:T(8,128)S(1)}, f32[28,8,128]{2,1,0:T(8,128)S(1)}, u32[]{:S(2)}, u32[]{:S(2)}) collective-permute-start(f32[28,8,128]{2,1,0:T(8,128)S(1)} %get-tuple-element.26), channel_id=1, source_target_pairs={{0,1},{1,0},{2,3},{3,2},{4,5},{5,4},{6,7},{7,6},{8,9},{9,8},{10,11... | collective-permute-start | bytes 344072 | tf_op jit(solution)/shard_map/ppermute | solution.py:311
  45.4 4.4 %collective-permute-start.5 = (f32[28,8,128]{2,1,0:T(8,128)S(1)}, f32[28,8,128]{2,1,0:T(8,128)S(1)}, u32[]{:S(2)}, u32[]{:S(2)}) collective-permute-start(f32[28,8,128]{2,1,0:T(8,128)S(1)} %get-tuple-element.27), channel_id=1, source_target_pairs={{0,15},{1,2},{2,1},{3,4},{4,3},{5,6},{6,5},{7,8},{8,7},{9,10},{10,... | collective-permute-start | bytes 344072 | tf_op jit(solution)/shard_map/ppermute | solution.py:312
  49.9 0.1 multiply_cosine_fusion.w_ref
  50.0 0.0 collective-permute-done.2.ya1
  50.0 0.0 collective-permute-done.3.yb1
  50.0 0.0 collective-permute-done.4.ya2
  50.0 2.3 %collective-permute-done.5.yb2 = f32[28,8,128]{2,1,0:T(8,128)S(1)} collective-permute-done((f32[28,8,128]{2,1,0:T(8,128)S(1)}, f32[28,8,128]{2,1,0:T(8,128)S(1)}, u32[]{:S(2)}, u32[]{:S(2)}) %collective-permute-start.5) | collective-permute-done | bytes 114720 | tf_op jit(solution)/shard_map/ppermute | solution.py:312
  52.3 4.1 %steps.1 = (f32[3,8,16,128]{3,2,1,0:T(8,128)}, f32[3,8,16,128]{3,2,1,0:T(8,128)}, f32[32,1,128]{2,1,0:T(1,128)S(1)}) custom-call(f32[3,8,16,128]{3,2,1,0:T(8,128)S(1)} %copy-done, f32[3,8,16,128]{3,2,1,0:T(8,128)S(1)} %copy-done.1, f32[8,16,128]{2,1,0:T(8,128)S(1)} %get-tuple-element.17.s_ref.own_s, f32[8,16,128]{2,1,0:T(8,128)S(1)} %get-tuple-element.18.permit_ref, ...), custom_call_target="tpu_custom_call" | custom-call | flops 16777216 | bytes 4194304 | tf_op jit(solution)/shard_map/steps/pallas_call | solution.py:322
  56.4 17.8 %all_to_all.10.in_ref = f32[32,1,128]{2,1,0:T(1,128)S(1)} all-to-all(f32[32,1,128]{2,1,0:T(1,128)S(1)} %get-tuple-element.30), channel_id=1, replica_groups={{0,1,16,17,32,33,48,49,128,129,144,145,160,161,176,177,256,257,272,273,..., dimensions={0} | all-to-all | bytes 32768 | tf_op jit(solution)/shard_map/all_to_all | solution.py:326
  74.3 24.4 %all_to_all.11.in_ref = f32[16,1,128]{2,1,0:T(1,128)S(1)} all-to-all(f32[16,1,128]{2,1,0:T(1,128)S(1)} %add_up.1), channel_id=1, replica_groups={{0,2,4,6,8,10,12,14,64,66,68,70,72,74,76,78},{1,3,5,7,9,11,13,15,65,67,..., dimensions={0} | all-to-all | bytes 16384 | tf_op jit(solution)/shard_map/all_to_all | solution.py:328
  98.6 0.8 finish.1
  (9 shorter events, 0.1 us)
Async XLA Ops:
  0.6 24.7 %copy-start.2 = (s32[8,16,64]{2,1,0:T(8,128)S(1)}, s32[8,16,64]{2,1,0:T(8,128)}, u32[]{:S(2)}) copy-start(s32[8,16,64]{2,1,0:T(8,128)} %m_ref.3) | copy-start | bytes 98308
  0.6 25.4 %copy-start = (f32[3,8,16,128]{3,2,1,0:T(8,128)S(1)}, f32[3,8,16,128]{3,2,1,0:T(8,128)}, u32[]{:S(2)}) copy-start(f32[3,8,16,128]{3,2,1,0:T(8,128)} %own_e.1) | copy-start | bytes 589828
  0.7 25.4 %copy-start.1 = (f32[3,8,16,128]{3,2,1,0:T(8,128)S(1)}, f32[3,8,16,128]{3,2,1,0:T(8,128)}, u32[]{:S(2)}) copy-start(f32[3,8,16,128]{3,2,1,0:T(8,128)} %own_h.1) | copy-start | bytes 589828
  1.9 23.4 %copy-start.3 = (f32[4]{0:T(128)S(1)}, f32[4]{0:T(128)}, u32[]{:S(2)}) copy-start(f32[4]{0:T(128)} %p_ref.3) | copy-start | bytes 52
  1.9 29.9 %collective-permute-start = (f32[392,128]{1,0:T(8,128)S(1)}, f32[392,128]{1,0:T(8,128)S(1)}, u32[]{:S(2)}, u32[]{:S(2)}) collective-permute-start(f32[392,128]{1,0:T(8,128)S(1)} %get-tuple-element.19), channel_id=1, source_target_pairs={{0,16},{16,0},{32,48},{48,32},{64,80},{80,64},{96,112},{112,96},{1... | collective-permute-start | bytes 602120 | tf_op jit(solution)/shard_map/ppermute | solution.py:299
  5.9 35.5 %collective-permute-start.1 = (f32[392,128]{1,0:T(8,128)S(1)}, f32[392,128]{1,0:T(8,128)S(1)}, u32[]{:S(2)}, u32[]{:S(2)}) collective-permute-start(f32[392,128]{1,0:T(8,128)S(1)} %get-tuple-element.20), channel_id=1, source_target_pairs={{0,496},{16,32},{32,16},{48,64},{64,48},{80,96},{96,80},{112,128},... | collective-permute-start | bytes 602120 | tf_op jit(solution)/shard_map/ppermute | solution.py:300
  26.1 23.9 %collective-permute-start.2 = (f32[28,8,128]{2,1,0:T(8,128)S(1)}, f32[28,8,128]{2,1,0:T(8,128)S(1)}, u32[]{:S(2)}, u32[]{:S(2)}) collective-permute-start(f32[28,8,128]{2,1,0:T(8,128)S(1)} %get-tuple-element.24), channel_id=1, source_target_pairs={{0,1},{1,0},{2,3},{3,2},{4,5},{5,4},{6,7},{7,6},{8,9},{9,8},{10,11... | collective-permute-start | bytes 344072 | tf_op jit(solution)/shard_map/ppermute | solution.py:305
  29.3 20.7 %collective-permute-start.3 = (f32[28,8,128]{2,1,0:T(8,128)S(1)}, f32[28,8,128]{2,1,0:T(8,128)S(1)}, u32[]{:S(2)}, u32[]{:S(2)}) collective-permute-start(f32[28,8,128]{2,1,0:T(8,128)S(1)} %get-tuple-element.25), channel_id=1, source_target_pairs={{0,15},{1,2},{2,1},{3,4},{4,3},{5,6},{6,5},{7,8},{8,7},{9,10},{10,... | collective-permute-start | bytes 344072 | tf_op jit(solution)/shard_map/ppermute | solution.py:306
  42.1 7.7 %copy-start.4 = (f32[4]{0:T(128)S(1)}, f32[4]{0:T(128)}, u32[]{:S(2)}) copy-start(f32[4]{0:T(128)} %param.9) | copy-start | bytes 52
  42.1 7.9 %collective-permute-start.4 = (f32[28,8,128]{2,1,0:T(8,128)S(1)}, f32[28,8,128]{2,1,0:T(8,128)S(1)}, u32[]{:S(2)}, u32[]{:S(2)}) collective-permute-start(f32[28,8,128]{2,1,0:T(8,128)S(1)} %get-tuple-element.26), channel_id=1, source_target_pairs={{0,1},{1,0},{2,3},{3,2},{4,5},{5,4},{6,7},{7,6},{8,9},{9,8},{10,11... | collective-permute-start | bytes 344072 | tf_op jit(solution)/shard_map/ppermute | solution.py:311
  45.4 6.9 %collective-permute-start.5 = (f32[28,8,128]{2,1,0:T(8,128)S(1)}, f32[28,8,128]{2,1,0:T(8,128)S(1)}, u32[]{:S(2)}, u32[]{:S(2)}) collective-permute-start(f32[28,8,128]{2,1,0:T(8,128)S(1)} %get-tuple-element.27), channel_id=1, source_target_pairs={{0,15},{1,2},{2,1},{3,4},{4,3},{5,6},{6,5},{7,8},{8,7},{9,10},{10,... | collective-permute-start | bytes 344072 | tf_op jit(solution)/shard_map/ppermute | solution.py:312

commit v3 on v2

--- a/solution.py
+++ b/solution.py
@@ -17,7 +17,6 @@
 PX = BX + 2 * HALO
 PY = BY + 2 * HALO
 XTILES = 49
-YTILES = 7 * BX // 2
 
 VMEM = pl.BlockSpec(memory_space=pltpu.VMEM)
 HBM = pl.BlockSpec(memory_space=pltpu.HBM)
@@ -87,81 +86,102 @@
     return value
 
 
+def spread(rows, offset):
+    shape = (rows, LANES)
+    return (iota(shape, 1) // SOURCES + offset == iota(shape, 0)).astype(jnp.bfloat16)
+
+
 def own_cells(m_ref, p_ref, permit_ref, scaled_ref):
-    row, col = iota((NZ, LANES), 0), iota((NZ, LANES), 1)
-    spread = (col // SOURCES == row).astype(jnp.bfloat16)
     cells = m_ref[...].reshape(BX * BY, NZ).astype(jnp.float32).astype(jnp.bfloat16)
-    index = jnp.dot(cells, spread, preferred_element_type=jnp.float32)
-    permit = look_up(index, p_ref)
+    permit = look_up(jnp.dot(cells, spread(NZ, 0), preferred_element_type=jnp.float32), p_ref)
     permit_ref[...] = permit.reshape(BX, BY, LANES)
     scaled_ref[...] = (TIME_STEP / permit).reshape(BX, BY, LANES)
 
 
-def pack_y(refs, ya_ref, yb_ref):
+def fill_ghosts(src, after, p_ref, e_ref, h_ref, s_ref):
+    narrow = jnp.where(after, 0, 1)
+    row = 0
+    for ref, c, n, start in x_parts(e_ref, h_ref, 0, narrow):
+        ref[c, pl.ds(start, n)] = src[pl.ds(row, n * BY)].reshape(n, BY, LANES)
+        row += n * BY
+    cells = src[pl.ds(row, 24)].astype(jnp.bfloat16)
+    for half in range(2):
+        index = jnp.dot(cells, spread(LANES, half * NZ), preferred_element_type=jnp.float32)
+        value = TIME_STEP / look_up(index, p_ref)
+        for i in range(3):
+            s_ref[narrow + i, pl.ds(8 * half, 8)] = value[8 * i : 8 * i + 8]
+    unused = jnp.where(after, 3, 0)
+    h_ref[0, unused] = jnp.zeros((BY, LANES), jnp.float32)
+    s_ref[unused] = jnp.zeros((BY, LANES), jnp.float32)
+
+
+def edge_rows(ref, low, high):
+    first = iota((8, LANES), 0) < HALO
+    top = jnp.where(first, pltpu.roll(ref[low, 8:16], HALO, 0), ref[high, 8:16])
+    bottom = jnp.where(first, ref[low, 0:8], pltpu.roll(ref[high, 0:8], HALO, 0))
+    return top, bottom
+
+
+def pack_y(parts, ya_ref, yb_ref):
     even = lax.rem(lax.axis_index("gy"), 2) == 0
+    for tile, (ref, low, high) in enumerate(parts):
+        top, bottom = edge_rows(ref, low, high)
+        ya_ref[tile] = jnp.where(even, top, bottom)
+        yb_ref[tile] = jnp.where(even, bottom, top)
+
+
+def unpack_y(parts, ya_ref, yb_ref, other=None):
+    even = lax.rem(lax.axis_index("gy"), 2) == 0
+    wraps = lax.rem(lax.axis_index("gy") + 1, lax.axis_size("gy")) < 2
     first = iota((8, LANES), 0) < HALO
-    for f, ref in enumerate(refs):
-        for p in range(4):
-            top = jnp.where(first, pltpu.roll(ref[p, 8:16], HALO, 0), ref[p + 4, 8:16])
-            bottom = jnp.where(first, ref[p, 0:8], pltpu.roll(ref[p + 4, 0:8], HALO, 0))
-            ya_ref[f * 4 + p] = jnp.where(even, top, bottom)
-            yb_ref[f * 4 + p] = jnp.where(even, bottom, top)
-
-
-def unpack_y(refs, base, ya_ref, yb_ref):
-    even = lax.rem(lax.axis_index("gy"), 2) == 0
-    first = iota((8, LANES), 0) < HALO
-    for f, ref in enumerate(refs):
-        for p in range(4):
-            a, b = ya_ref[f * 4 + p], yb_ref[f * 4 + p]
-            after, before = jnp.where(even, a, b), jnp.where(even, b, a)
-            ref[base + p, BY:PY] = jnp.where(first, after, pltpu.roll(before, HALO, 0))
-            ref[base + p + 4, BY:PY] = jnp.where(first, pltpu.roll(after, HALO, 0), before)
+    for tile, (ref, low, high) in enumerate(parts):
+        a, b = ya_ref[tile], yb_ref[tile]
+        if other is not None:
+            b = jnp.where(wraps, other[tile], b)
+        after, before = jnp.where(even, a, b), jnp.where(even, b, a)
+        ref[low, BY:PY] = jnp.where(first, after, pltpu.roll(before, HALO, 0))
+        ref[high, BY:PY] = jnp.where(first, pltpu.roll(after, HALO, 0), before)
 
 
 def fields(e, h, s):
     return [e.at[c] for c in range(3)] + [h.at[c] for c in range(3)] + [s]
 
 
-def own_rows(e_ref, h_ref, s_ref, ya_ref, yb_ref):
-    pack_y(fields(e_ref, h_ref, s_ref), ya_ref, yb_ref)
-
-
-def ghost_planes(a_ref, b_ref, p_ref, e_ref, h_ref, s_ref, ya_ref, yb_ref):
+def pairs_of(refs, planes, base=0):
+    return [(ref, base + p, base + p + planes // 2) for ref in refs for p in range(planes // 2)]
+
+
+def near_side(e_ref, h_ref, s_ref, a_ref, p_ref, ge_ref, gh_ref, gs_ref, ya_ref, yb_ref, corner_ref):
     even = lax.rem(lax.axis_index("gx"), 2) == 0
-    r, col = iota((LANES, LANES), 0), iota((LANES, LANES), 1)
-    low = (col // SOURCES == r).astype(jnp.bfloat16)
-    high = (col // SOURCES == r - NZ).astype(jnp.bfloat16)
-    for src, after in ((a_ref, even), (b_ref, jnp.logical_not(even))):
-        wide = jnp.where(after, 0, HALO)
-        narrow = jnp.where(after, 0, HALO + 1)
-        row = 0
-        for ref, c, n, start in x_parts(e_ref, h_ref, wide, narrow):
-            ref[c, pl.ds(start, n)] = src[pl.ds(row, n * BY)].reshape(n, BY, LANES)
-            row += n * BY
-        cells = src[pl.ds(row, 24)].astype(jnp.bfloat16)
-        for half, spread in ((0, low), (8, high)):
-            index = jnp.dot(cells, spread, preferred_element_type=jnp.float32)
-            value = TIME_STEP / look_up(index, p_ref)
-            for i in range(3):
-                s_ref[narrow + i, pl.ds(half, 8)] = value[8 * i : 8 * i + 8]
-    zero = jnp.zeros((BY, LANES), jnp.float32)
-    for ref in (h_ref.at[0], s_ref):
-        ref[HALO - 1] = zero
-        ref[HALO] = zero
-    pack_y(fields(e_ref, h_ref, s_ref), ya_ref, yb_ref)
+    fill_ghosts(a_ref, even, p_ref, ge_ref, gh_ref, gs_ref)
+    own = fields(e_ref, h_ref, s_ref)
+    pack_y(pairs_of(own, BX) + pairs_of(fields(ge_ref, gh_ref, gs_ref), HALO), ya_ref, yb_ref)
+    start = jnp.where(even, 0, BX - HALO)
+    upper = lax.rem(lax.axis_index("gy"), 2) == 1
+    for tile, (ref, low, high) in enumerate(pairs_of(own, HALO, start)):
+        top, bottom = edge_rows(ref, low, high)
+        corner_ref[tile] = jnp.where(upper, top, bottom)
+
+
+def far_side(b_ref, p_ref, ge_ref, gh_ref, gs_ref, ya_ref, yb_ref):
+    odd = lax.rem(lax.axis_index("gx"), 2) == 1
+    fill_ghosts(b_ref, odd, p_ref, ge_ref, gh_ref, gs_ref)
+    pack_y(pairs_of(fields(ge_ref, gh_ref, gs_ref), HALO), ya_ref, yb_ref)
 
 
 def steps(
-    own_e, own_h, own_s, permit_ref, ghost_e, ghost_h, ghost_s, ya1, yb1, ya2, yb2, w_ref,
+    own_e, own_h, own_s, permit_ref, ae, ah, sa, be, bh, sb, ya1, yb1, ya2, yb2, corner, w_ref,
     e_out, h_out, part_ref, ee, hh, ss, sems,
 ):
+    even = lax.rem(lax.axis_index("gx"), 2) == 0
+    base_a, base_b = jnp.where(even, BX, BX + HALO), jnp.where(even, BX + HALO, BX)
     extended = fields(ee.at[0], hh, ss)
-    for dst, own, ghost in zip(extended, fields(own_e, own_h, own_s), fields(ghost_e, ghost_h, ghost_s)):
+    for dst, own, a, b in zip(extended, fields(own_e, own_h, own_s), fields(ae, ah, sa), fields(be, bh, sb)):
         dst[:BX, :BY] = own[...]
-        dst[BX:, :BY] = ghost[...]
-    unpack_y(extended, 0, ya1, yb1)
-    unpack_y(extended, BX, ya2, yb2)
+        dst[pl.ds(base_a, HALO), :BY] = a[...]
+        dst[pl.ds(base_b, HALO), :BY] = b[...]
+    unpack_y(pairs_of(extended, BX) + pairs_of(extended, HALO, base_a), ya1, yb1)
+    unpack_y(pairs_of(extended, HALO, base_b), ya2, yb2, corner)
 
     lane = iota((PY, LANES), 1)
     not_last, not_first = lane < LANES - SOURCES, lane >= SOURCES
@@ -267,10 +287,11 @@
     out_ref[...] = total[:, :8] / cells
 
 
-def swap_pairs(count, odd):
+def swap_pairs(count, odd, wrap=True):
     if not odd:
         return [(i, i ^ 1) for i in range(count)]
-    return [(i, (i + 1) % count if i % 2 else (i - 1) % count) for i in range(count)]
+    inner = range(count) if wrap else range(1, count - 1)
+    return [(i, (i + 1) % count if i % 2 else (i - 1) % count) for i in inner]
 
 
 def sum_groups(n_gx, n_gy):
@@ -288,7 +309,8 @@
     n_gx, n_gy = lax.axis_size("gx"), lax.axis_size("gy")
     weights = jnp.cos(frequencies[None, :] * (jnp.arange(1, ITERS + 1, dtype=jnp.float32)[:, None] * TIME_STEP))
     x_message = (f32(XTILES * 8, LANES),) * 2
-    y_message = (f32(YTILES, 8, LANES),) * 2
+    y_first = (f32(7 * (BX + HALO) // 2, 8, LANES),) * 2
+    y_corner = f32(7 * HALO // 2, 8, LANES)
     scratch = (pltpu.VMEM((2, 3, BY, NZ), jnp.int32), pltpu.SemaphoreType.DMA((2, 7)))
     send_a, send_b = call(pack_x, x_message, "pack_x", 3, scratch=scratch, hbm=(0, 1, 2), size=1 << 20)(
         *(
@@ -301,15 +323,21 @@
     permit, scaled = call(own_cells, (f32(BX, BY, LANES),) * 2, "own_cells", 2, smem=(1,), size=1 << 18)(
         material, permittivity
     )
-    send_a, send_b = call(own_rows, y_message, "own_rows", 3, size=1 << 20)(e_field, h_field, scaled)
+    ghosts = (f32(3, HALO, BY, LANES), f32(3, HALO, BY, LANES), f32(HALO, BY, LANES))
+    *near, send_a, send_b, send_c = call(near_side, ghosts + y_first + (y_corner,), "near_side", 5, smem=(4,), size=1 << 20)(
+        e_field, h_field, scaled, got_a, permittivity
+    )
+    end = n_gy - 1
+    diagonal = [(a * n_gy + g, b * n_gy + end - g) for a, b in swap_pairs(n_gx, True) for g in (0, end)]
+    yb1 = lax.ppermute(send_b, "gy", swap_pairs(n_gy, True))
+    corner = lax.ppermute(send_c, ("gx", "gy"), diagonal)
     ya1 = lax.ppermute(send_a, "gy", swap_pairs(n_gy, False))
-    yb1 = lax.ppermute(send_b, "gy", swap_pairs(n_gy, True))
-    ghosts = (f32(3, 2 * HALO, BY, LANES), f32(3, 2 * HALO, BY, LANES), f32(2 * HALO, BY, LANES)) + y_message
-    ghost_e, ghost_h, ghost_s, send_a, send_b = call(ghost_planes, ghosts, "ghost_planes", 3, smem=(2,), size=1 << 20)(
-        got_a, got_b, permittivity
+    got_b, ya1 = lax.optimization_barrier((got_b, ya1))
+    *far, send_a, send_b = call(far_side, ghosts + (y_corner, y_corner), "far_side", 2, smem=(1,), size=1 << 20)(
+        got_b, permittivity
     )
     ya2 = lax.ppermute(send_a, "gy", swap_pairs(n_gy, False))
-    yb2 = lax.ppermute(send_b, "gy", swap_pairs(n_gy, True))
+    yb2 = lax.ppermute(send_b, "gy", swap_pairs(n_gy, True, wrap=False))
     planes, columns = sum_groups(n_gx, n_gy)
     n_plane, n_column = len(planes[0]), len(columns[0])
     scratch = (
@@ -320,8 +348,8 @@
     )
     outs = (f32(3, BX, BY, LANES), f32(3, BX, BY, LANES), f32(n_plane, 1, LANES))
     e_out, h_out, part = call(
-        steps, outs, "steps", 12, scratch=scratch, smem=(11,), hbm_out=(0, 1), flops=1 << 24, size=1 << 22
-    )(e_field, h_field, scaled, permit, ghost_e, ghost_h, ghost_s, ya1, yb1, ya2, yb2, weights)
+        steps, outs, "steps", 16, scratch=scratch, smem=(15,), hbm_out=(0, 1), flops=1 << 24, size=1 << 22
+    )(e_field, h_field, scaled, permit, *near, *far, ya1, yb1, ya2, yb2, corner, weights)
     both = ("gx", "gy")
     part = lax.all_to_all(part, both, 0, 0, axis_index_groups=planes, tiled=True)
     part = call(add_up, f32(n_column, 1, LANES), "add_up", 1, size=1 << 14)(part)

time: 99.8 us -> 94.8 us (0.950)
  blocking collectives: 42.2 us -> 37.1 us
  waiting for transfers between devices: 11.9 us -> 9.96 us
  starting transfers between devices: 36.8 us -> 38.1 us
    all_to_all x1, blocking collectives: 17.8 us -> 8.68 us  [body(): lax.all_to_all(part, both, 0, 0, axis_index_groups=planes, tiled=True)]
    all_to_all x1, blocking collectives: 24.4 us -> 28.4 us  [body(): lax.all_to_all(part, both, 0, 0, axis_index_groups=columns, tiled=True)]
    ppermute x1 -> x2, starting transfers between devices: 4.42 us -> 5.74 us  [the longest x1 5.08 us: body(): yb2 = lax.ppermute(send_b, 'gy', swap_pairs(n_gy, True, wrap=False))]
    ppermute x1, waiting for transfers between devices: 9.55 us -> 8.26 us  [body(): got_b = lax.ppermute(send_b, 'gx', swap_pairs(n_gx, True))]
    ppermute x1 -> x2, waiting for transfers between devices: 2.31 us -> 1.7 us  [the longest x1 1.7 us: body(): yb2 = lax.ppermute(send_b, 'gy', swap_pairs(n_gy, True, wrap=False))]
  transfers between devices with their start and end apart: 6 -> 7, of which waited for: 2 -> 2; matrix products, arithmetic and copies ran while one was open for 0% -> 0% of each run, Pallas kernels for 1% -> 2%
where the time goes in v3:
time: 94.8 us; the launch traced here: 94.5 us
  starting transfers between devices  38.1 us (40%)
  blocking collectives  37.1 us (39%)
  waiting for transfers between devices  9.96 us (11%)
  Pallas kernels  8.33 us (9%)
    all_to_all x1, blocking collectives, body(): lax.all_to_all(part, both, 0, 0, axis_index_groups=columns, tiled=True)  28.4 us
    ppermute x1, starting transfers between devices, body(): got_b = lax.ppermute(send_b, 'gx', swap_pairs(n_gx, True))  19.4 us
    all_to_all x1, blocking collectives, body(): lax.all_to_all(part, both, 0, 0, axis_index_groups=planes, tiled=True)  8.68 us
    ppermute x1, waiting for transfers between devices, body(): got_b = lax.ppermute(send_b, 'gx', swap_pairs(n_gx, True))  8.26 us
    ppermute x1, starting transfers between devices, body(): yb2 = lax.ppermute(send_b, 'gy', swap_pairs(n_gy, True, wrap=False))  5.08 us
    pallas_call x1, Pallas kernels, body(): call(steps, outs, 'steps', 16, scratch=scratch, smem=(15,), hbm_out=(0, 1...  4.16 us
    ppermute x1, starting transfers between devices, body(): got_a = lax.ppermute(send_a, 'gx', swap_pairs(n_gx, False))  3.95 us
    ppermute x1, starting transfers between devices, body(): ya2 = lax.ppermute(send_a, 'gy', swap_pairs(n_gy, False))  3.3 us
  transfers between devices with their start and end apart: 7, of which 2 were waited for; matrix products, arithmetic and copies ran while one was open for 0% of the time, Pallas kernels for 2%

profile of v3, /device:TPU:1, one launch (start us, length us, event | category | flops | bytes accessed | tf_op | source)
XLA Modules:
  0.0 94.5 jit_solution(14909178924140346816)
XLA Ops:
  0.7 1.3 %pack_x.1 = (f32[392,128]{1,0:T(8,128)S(1)}, f32[392,128]{1,0:T(8,128)S(1)}) custom-call(f32[3,128,128]{2,1,0:T(8,128)} %bitcast.2, f32[3,128,128]{2,1,0:T(8,128)} %bitcast.3, s32[8,16,64]{2,1,0:T(8,128)} %m_ref.3), custom_call_target="tpu_custom_call" | custom-call | bytes 1048576 | tf_op jit(solution)/shard_map/pack_x/pallas_call | solution.py:315
  1.9 0.0 copy-start.3
  1.9 3.9 %collective-permute-start = (f32[392,128]{1,0:T(8,128)S(1)}, f32[392,128]{1,0:T(8,128)S(1)}, u32[]{:S(2)}, u32[]{:S(2)}) collective-permute-start(f32[392,128]{1,0:T(8,128)S(1)} %get-tuple-element.25), channel_id=1, source_target_pairs={{0,16},{16,0},{32,48},{48,32},{64,80},{80,64},{96,112},{112,96},{1... | collective-permute-start | bytes 602120 | tf_op jit(solution)/shard_map/ppermute | solution.py:321
  5.9 19.4 %collective-permute-start.1 = (f32[392,128]{1,0:T(8,128)S(1)}, f32[392,128]{1,0:T(8,128)S(1)}, u32[]{:S(2)}, u32[]{:S(2)}) collective-permute-start(f32[392,128]{1,0:T(8,128)S(1)} %get-tuple-element.29), channel_id=1, source_target_pairs={{0,496},{16,32},{32,16},{48,64},{64,48},{80,96},{96,80},{112,128},... | collective-permute-start | bytes 602120 | tf_op jit(solution)/shard_map/ppermute | solution.py:322
  25.4 0.7 own_cells.1
  26.1 0.0 collective-permute-done.a_ref
  26.1 0.7 near_side.1
  26.8 3.1 %collective-permute-start.2 = (f32[42,8,128]{2,1,0:T(8,128)S(1)}, f32[42,8,128]{2,1,0:T(8,128)S(1)}, u32[]{:S(2)}, u32[]{:S(2)}) collective-permute-start(f32[42,8,128]{2,1,0:T(8,128)S(1)} %get-tuple-element.30), channel_id=1, source_target_pairs={{0,1},{1,0},{2,3},{3,2},{4,5},{5,4},{6,7},{7,6},{8,9},{9,8},{10,11... | collective-permute-start | bytes 516104 | tf_op jit(solution)/shard_map/ppermute | solution.py:334
  29.9 0.7 collective-permute-start.6
  30.6 2.5 %collective-permute-start.3 = (f32[42,8,128]{2,1,0:T(8,128)S(1)}, f32[42,8,128]{2,1,0:T(8,128)S(1)}, u32[]{:S(2)}, u32[]{:S(2)}) collective-permute-start(f32[42,8,128]{2,1,0:T(8,128)S(1)} %get-tuple-element.36), channel_id=1, source_target_pairs={{0,15},{1,2},{2,1},{3,4},{4,3},{5,6},{6,5},{7,8},{8,7},{9,10},{10,... | collective-permute-start | bytes 516104 | tf_op jit(solution)/shard_map/ppermute | solution.py:332
  33.2 8.3 %collective-permute-done.1.b_ref = f32[392,128]{1,0:T(8,128)S(1)} collective-permute-done((f32[392,128]{1,0:T(8,128)S(1)}, f32[392,128]{1,0:T(8,128)S(1)}, u32[]{:S(2)}, u32[]{:S(2)}) %collective-permute-start.1) | collective-permute-done | bytes 200736 | tf_op jit(solution)/shard_map/ppermute | solution.py:322
  41.4 0.0 collective-permute-done.2.ya1
  41.4 0.7 far_side.1
  42.1 0.0 copy-start.4
  42.1 3.3 %collective-permute-start.4 = (f32[14,8,128]{2,1,0:T(8,128)S(1)}, f32[14,8,128]{2,1,0:T(8,128)S(1)}, u32[]{:S(2)}, u32[]{:S(2)}) collective-permute-start(f32[14,8,128]{2,1,0:T(8,128)S(1)} %get-tuple-element.37), channel_id=1, source_target_pairs={{0,1},{1,0},{2,3},{3,2},{4,5},{5,4},{6,7},{7,6},{8,9},{9,8},{10,11... | collective-permute-start | bytes 172040 | tf_op jit(solution)/shard_map/ppermute | solution.py:339
  45.4 5.1 %collective-permute-start.5 = (f32[14,8,128]{2,1,0:T(8,128)S(1)}, f32[14,8,128]{2,1,0:T(8,128)S(1)}, u32[]{:S(2)}, u32[]{:S(2)}) collective-permute-start(f32[14,8,128]{2,1,0:T(8,128)S(1)} %get-tuple-element.38), channel_id=1, source_target_pairs={{1,2},{2,1},{3,4},{4,3},{5,6},{6,5},{7,8},{8,7},{9,10},{10,9},{11,... | collective-permute-start | bytes 172040 | tf_op jit(solution)/shard_map/ppermute | solution.py:340
  50.5 0.1 multiply_cosine_fusion.w_ref
  50.7 0.0 collective-permute-done.6.corner
  50.7 0.0 collective-permute-done.3.yb1
  50.7 1.7 %collective-permute-done.5.yb2 = f32[14,8,128]{2,1,0:T(8,128)S(1)} collective-permute-done((f32[14,8,128]{2,1,0:T(8,128)S(1)}, f32[14,8,128]{2,1,0:T(8,128)S(1)}, u32[]{:S(2)}, u32[]{:S(2)}) %collective-permute-start.5) | collective-permute-done | bytes 57376 | tf_op jit(solution)/shard_map/ppermute | solution.py:340
  52.4 4.2 %steps.1 = (f32[3,8,16,128]{3,2,1,0:T(8,128)}, f32[3,8,16,128]{3,2,1,0:T(8,128)}, f32[32,1,128]{2,1,0:T(1,128)S(1)}) custom-call(f32[3,8,16,128]{3,2,1,0:T(8,128)S(1)} %copy-done, f32[3,8,16,128]{3,2,1,0:T(8,128)S(1)} %copy-done.1, f32[8,16,128]{2,1,0:T(8,128)S(1)} %get-tuple-element.23.s_ref.own_s, f32[8,16,128]{2,1,0:T(8,128)S(1)} %get-tuple-element.24.permit_ref, ...), custom_call_target="tpu_custom_call" | custom-call | flops 16777216 | bytes 4194304 | tf_op jit(solution)/shard_map/steps/pallas_call | solution.py:350
  56.5 8.7 %all_to_all.10.in_ref = f32[32,1,128]{2,1,0:T(1,128)S(1)} all-to-all(f32[32,1,128]{2,1,0:T(1,128)S(1)} %get-tuple-element.42), channel_id=1, replica_groups={{0,1,16,17,32,33,48,49,128,129,144,145,160,161,176,177,256,257,272,273,..., dimensions={0} | all-to-all | bytes 32768 | tf_op jit(solution)/shard_map/all_to_all | solution.py:354
  65.3 28.4 %all_to_all.11.in_ref = f32[16,1,128]{2,1,0:T(1,128)S(1)} all-to-all(f32[16,1,128]{2,1,0:T(1,128)S(1)} %add_up.1), channel_id=1, replica_groups={{0,2,4,6,8,10,12,14,64,66,68,70,72,74,76,78},{1,3,5,7,9,11,13,15,65,67,..., dimensions={0} | all-to-all | bytes 16384 | tf_op jit(solution)/shard_map/all_to_all | solution.py:356
  93.7 0.8 finish.1
  (11 shorter events, 0.1 us)
Async XLA Ops:
  0.6 24.7 %copy-start.2 = (s32[8,16,64]{2,1,0:T(8,128)S(1)}, s32[8,16,64]{2,1,0:T(8,128)}, u32[]{:S(2)}) copy-start(s32[8,16,64]{2,1,0:T(8,128)} %m_ref.3) | copy-start | bytes 98308
  0.6 25.4 %copy-start = (f32[3,8,16,128]{3,2,1,0:T(8,128)S(1)}, f32[3,8,16,128]{3,2,1,0:T(8,128)}, u32[]{:S(2)}) copy-start(f32[3,8,16,128]{3,2,1,0:T(8,128)} %own_e.1) | copy-start | bytes 589828
  0.7 25.4 %copy-start.1 = (f32[3,8,16,128]{3,2,1,0:T(8,128)S(1)}, f32[3,8,16,128]{3,2,1,0:T(8,128)}, u32[]{:S(2)}) copy-start(f32[3,8,16,128]{3,2,1,0:T(8,128)} %own_h.1) | copy-start | bytes 589828
  1.9 23.4 %copy-start.3 = (f32[4]{0:T(128)S(1)}, f32[4]{0:T(128)}, u32[]{:S(2)}) copy-start(f32[4]{0:T(128)} %p_ref.5) | copy-start | bytes 52
  1.9 24.1 %collective-permute-start = (f32[392,128]{1,0:T(8,128)S(1)}, f32[392,128]{1,0:T(8,128)S(1)}, u32[]{:S(2)}, u32[]{:S(2)}) collective-permute-start(f32[392,128]{1,0:T(8,128)S(1)} %get-tuple-element.25), channel_id=1, source_target_pairs={{0,16},{16,0},{32,48},{48,32},{64,80},{80,64},{96,112},{112,96},{1... | collective-permute-start | bytes 602120 | tf_op jit(solution)/shard_map/ppermute | solution.py:321
  5.9 35.5 %collective-permute-start.1 = (f32[392,128]{1,0:T(8,128)S(1)}, f32[392,128]{1,0:T(8,128)S(1)}, u32[]{:S(2)}, u32[]{:S(2)}) collective-permute-start(f32[392,128]{1,0:T(8,128)S(1)} %get-tuple-element.29), channel_id=1, source_target_pairs={{0,496},{16,32},{32,16},{48,64},{64,48},{80,96},{96,80},{112,128},... | collective-permute-start | bytes 602120 | tf_op jit(solution)/shard_map/ppermute | solution.py:322
  26.8 14.6 %collective-permute-start.2 = (f32[42,8,128]{2,1,0:T(8,128)S(1)}, f32[42,8,128]{2,1,0:T(8,128)S(1)}, u32[]{:S(2)}, u32[]{:S(2)}) collective-permute-start(f32[42,8,128]{2,1,0:T(8,128)S(1)} %get-tuple-element.30), channel_id=1, source_target_pairs={{0,1},{1,0},{2,3},{3,2},{4,5},{5,4},{6,7},{7,6},{8,9},{9,8},{10,11... | collective-permute-start | bytes 516104 | tf_op jit(solution)/shard_map/ppermute | solution.py:334
  29.9 20.7 %collective-permute-start.6 = (f32[14,8,128]{2,1,0:T(8,128)S(1)}, f32[14,8,128]{2,1,0:T(8,128)S(1)}, u32[]{:S(2)}, u32[]{:S(2)}) collective-permute-start(f32[14,8,128]{2,1,0:T(8,128)S(1)} %get-tuple-element.39), channel_id=1, source_target_pairs={{0,511},{15,496},{16,47},{31,32},{32,31},{47,16},{48,79},{63,64},{... | collective-permute-start | bytes 172040 | tf_op jit(solution)/shard_map/ppermute | solution.py:333
  30.6 20.0 %collective-permute-start.3 = (f32[42,8,128]{2,1,0:T(8,128)S(1)}, f32[42,8,128]{2,1,0:T(8,128)S(1)}, u32[]{:S(2)}, u32[]{:S(2)}) collective-permute-start(f32[42,8,128]{2,1,0:T(8,128)S(1)} %get-tuple-element.36), channel_id=1, source_target_pairs={{0,15},{1,2},{2,1},{3,4},{4,3},{5,6},{6,5},{7,8},{8,7},{9,10},{10,... | collective-permute-start | bytes 516104 | tf_op jit(solution)/shard_map/ppermute | solution.py:332
  42.1 8.4 %copy-start.4 = (f32[4]{0:T(128)S(1)}, f32[4]{0:T(128)}, u32[]{:S(2)}) copy-start(f32[4]{0:T(128)} %param.9) | copy-start | bytes 52
  42.1 8.5 %collective-permute-start.4 = (f32[14,8,128]{2,1,0:T(8,128)S(1)}, f32[14,8,128]{2,1,0:T(8,128)S(1)}, u32[]{:S(2)}, u32[]{:S(2)}) collective-permute-start(f32[14,8,128]{2,1,0:T(8,128)S(1)} %get-tuple-element.37), channel_id=1, source_target_pairs={{0,1},{1,0},{2,3},{3,2},{4,5},{5,4},{6,7},{7,6},{8,9},{9,8},{10,11... | collective-permute-start | bytes 172040 | tf_op jit(solution)/shard_map/ppermute | solution.py:339
  45.4 6.9 %collective-permute-start.5 = (f32[14,8,128]{2,1,0:T(8,128)S(1)}, f32[14,8,128]{2,1,0:T(8,128)S(1)}, u32[]{:S(2)}, u32[]{:S(2)}) collective-permute-start(f32[14,8,128]{2,1,0:T(8,128)S(1)} %get-tuple-element.38), channel_id=1, source_target_pairs={{1,2},{2,1},{3,4},{4,3},{5,6},{6,5},{7,8},{8,7},{9,10},{10,9},{11,... | collective-permute-start | bytes 172040 | tf_op jit(solution)/shard_map/ppermute | solution.py:340

commit v4 on v3

--- a/solution.py
+++ b/solution.py
@@ -91,11 +91,18 @@
     return (iota(shape, 1) // SOURCES + offset == iota(shape, 0)).astype(jnp.bfloat16)
 
 
-def own_cells(m_ref, p_ref, permit_ref, scaled_ref):
-    cells = m_ref[...].reshape(BX * BY, NZ).astype(jnp.float32).astype(jnp.bfloat16)
-    permit = look_up(jnp.dot(cells, spread(NZ, 0), preferred_element_type=jnp.float32), p_ref)
+def own_block(e_in, h_in, m_in, p_ref, e_ref, h_ref, permit_ref, scaled_ref, cells, sems):
+    ends = ((e_in, e_ref), (h_in, h_ref), (m_in, cells))
+    copies = [pltpu.make_async_copy(src, dst, sems.at[i]) for i, (src, dst) in enumerate(ends)]
+    for copy in copies:
+        copy.start()
+    copies[2].wait()
+    index = cells[...].reshape(BX * BY, NZ).astype(jnp.float32).astype(jnp.bfloat16)
+    permit = look_up(jnp.dot(index, spread(NZ, 0), preferred_element_type=jnp.float32), p_ref)
     permit_ref[...] = permit.reshape(BX, BY, LANES)
     scaled_ref[...] = (TIME_STEP / permit).reshape(BX, BY, LANES)
+    for copy in copies[:2]:
+        copy.wait()
 
 
 def fill_ghosts(src, after, p_ref, e_ref, h_ref, s_ref):
@@ -169,94 +176,189 @@
     pack_y(pairs_of(fields(ge_ref, gh_ref, gs_ref), HALO), ya_ref, yb_ref)
 
 
-def steps(
-    own_e, own_h, own_s, permit_ref, ae, ah, sa, be, bh, sb, ya1, yb1, ya2, yb2, corner, w_ref,
-    e_out, h_out, part_ref, ee, hh, ss, sems,
+def up_z(v):
+    return jnp.where(iota(v.shape, 1) < LANES - SOURCES, pltpu.roll(v, LANES - SOURCES, 1), 0.0)
+
+
+def down_z(v):
+    return jnp.where(iota(v.shape, 1) >= SOURCES, pltpu.roll(v, SOURCES, 1), 0.0)
+
+
+def next_y(v):
+    return pltpu.roll(v, PY - 1, 0)
+
+
+def prev_y(v):
+    return pltpu.roll(v, 1, 0)
+
+
+def advance(h_planes, e_planes, e_at, h_at, scale_at, put_e, put_h):
+    fresh = {}
+
+    def new_h(c, i):
+        return fresh[i][c] if i in fresh else h_at(c, i)
+
+    for i in sorted({*h_planes, *e_planes}):
+        e_x, e_y, e_z = (e_at(c, i) for c in range(3))
+        if i in h_planes:
+            e_yn, e_zn = e_at(1, i + 1), e_at(2, i + 1)
+            h_x = h_at(0, i) - TIME_STEP * ((next_y(e_z) - e_z) - (up_z(e_y) - e_y))
+            h_y = h_at(1, i) - TIME_STEP * ((up_z(e_x) - e_x) - (e_zn - e_z))
+            h_z = h_at(2, i) - TIME_STEP * ((e_yn - e_y) - (next_y(e_x) - e_x))
+            fresh[i] = (h_x, h_y, h_z)
+            put_h(i, fresh[i])
+        if i in e_planes:
+            h_x, h_y, h_z = (new_h(c, i) for c in range(3))
+            h_yb, h_zb = new_h(1, i - 1), new_h(2, i - 1)
+            s = scale_at(i)
+            e_x = e_x + s * ((h_z - prev_y(h_z)) - (h_y - down_z(h_y)))
+            e_y = e_y + s * ((h_x - down_z(h_x)) - (h_z - h_zb))
+            e_z = e_z + s * ((h_y - h_yb) - (h_x - prev_y(h_x)))
+            put_e(i, (e_x, e_y, e_z))
+
+
+def gram_terms(e_at, permit_ref, w_ref, planes, sums):
+    even_lane = iota((BY, LANES), 1) % 2 == 0
+    for i in planes:
+        permit = permit_ref[i]
+        for c in range(3):
+            e = [e_at(n, c, i)[:BY] for n in range(1, ITERS + 1)]
+            f = [sum(w_ref[n, k] * e[n] for n in range(ITERS)) for k in range(FILTERS)]
+            g = [v * permit for v in f]
+            o = [jnp.where(even_lane, pltpu.roll(v, LANES - 1, 1), pltpu.roll(v, 1, 1)) for v in g]
+            at = 0
+            sums = list(sums)
+            for right in (g, o):
+                for k in range(FILTERS):
+                    for l in range(k, FILTERS):
+                        v = f[k] * right[l]
+                        sums[at] = sums[at] + (v[:8] + v[8:])
+                        at += 1
+    return sums
+
+
+def both_sides(act):
+    even = lax.rem(lax.axis_index("gx"), 2) == 0
+    pl.when(even)(lambda: act(True))
+    pl.when(jnp.logical_not(even))(lambda: act(False))
+
+
+def near_h(before, n):
+    return range(n - 1, BX + HALO - n) if before else range(n - 1 - HALO, BX - n)
+
+
+def near_e(before, n):
+    if n == 0:
+        return range(0, BX + HALO) if before else range(-HALO, BX)
+    return range(n, BX + HALO - n) if before else range(n - HALO, BX - n)
+
+
+def near_planes(before):
+    near = range(HALO, BX) if before else range(0, BX - HALO)
+    return near, [i for i in range(BX) if i not in near]
+
+
+def near_steps(own_e, own_h, own_s, permit_ref, ge, gh, gs, ya1, yb1, w_ref, ee, hh, ss, sums_ref):
+    def act(before):
+        base = BX if before else BX + HALO
+        extended = fields(ee.at[0], hh, ss)
+        for dst, own, ghost in zip(extended, fields(own_e, own_h, own_s), fields(ge, gh, gs)):
+            dst[:BX, :BY] = own[...]
+            dst[base : base + HALO, :BY] = ghost[...]
+        unpack_y(pairs_of(extended, BX) + pairs_of(extended, HALO, base), ya1, yb1)
+
+        def put_h(i, values):
+            for c in range(3):
+                hh[c, i % PX] = values[c]
+
+        for n in range(1, ITERS + 1):
+
+            def put_e(i, values, n=n):
+                for c in range(3):
+                    ee[n, c, i % PX] = values[c]
+
+            advance(
+                near_h(before, n), near_e(before, n),
+                lambda c, i: ee[n - 1, c, i % PX], lambda c, i: hh[c, i % PX], lambda i: ss[i % PX], put_e, put_h,
+            )
+        sums = gram_terms(
+            lambda n, c, i: ee[n, c, i], permit_ref, w_ref, near_planes(before)[0], [jnp.zeros((8, LANES), jnp.float32)] * 20
+        )
+        for i in range(20):
+            sums_ref[i] = sums[i]
+
+    both_sides(act)
+
+
+def far_steps(
+    ee, hh, ss, sums_in, permit_ref, ge, gh, gs, corner, yb2, ya2, w_ref, e_out, h_out, part_ref, fe, fh, fs, sums_ref, sems
 ):
-    even = lax.rem(lax.axis_index("gx"), 2) == 0
-    base_a, base_b = jnp.where(even, BX, BX + HALO), jnp.where(even, BX + HALO, BX)
-    extended = fields(ee.at[0], hh, ss)
-    for dst, own, a, b in zip(extended, fields(own_e, own_h, own_s), fields(ae, ah, sa), fields(be, bh, sb)):
-        dst[:BX, :BY] = own[...]
-        dst[pl.ds(base_a, HALO), :BY] = a[...]
-        dst[pl.ds(base_b, HALO), :BY] = b[...]
-    unpack_y(pairs_of(extended, BX) + pairs_of(extended, HALO, base_a), ya1, yb1)
-    unpack_y(pairs_of(extended, HALO, base_b), ya2, yb2, corner)
-
-    lane = iota((PY, LANES), 1)
-    not_last, not_first = lane < LANES - SOURCES, lane >= SOURCES
-
-    def up_z(v):
-        return jnp.where(not_last, pltpu.roll(v, LANES - SOURCES, 1), 0.0)
-
-    def down_z(v):
-        return jnp.where(not_first, pltpu.roll(v, SOURCES, 1), 0.0)
-
-    def new_h(n, i):
-        p, q = i & (PX - 1), (i + 1) & (PX - 1)
-        e_x, e_y, e_z = ee[n, 0, p], ee[n, 1, p], ee[n, 2, p]
-        e_yn, e_zn = ee[n, 1, q], ee[n, 2, q]
-        h_x = hh[0, p] - TIME_STEP * ((pltpu.roll(e_z, PY - 1, 0) - e_z) - (up_z(e_y) - e_y))
-        h_y = hh[1, p] - TIME_STEP * ((up_z(e_x) - e_x) - (e_zn - e_z))
-        h_z = hh[2, p] - TIME_STEP * ((e_yn - e_y) - (pltpu.roll(e_x, PY - 1, 0) - e_x))
-        hh[0, p], hh[1, p], hh[2, p] = h_x, h_y, h_z
-        return h_x, h_y, h_z
-
-    def new_e(n, i, h, h_before):
-        p = i & (PX - 1)
-        h_x, h_y, h_z = h
-        h_yb, h_zb = h_before
-        s = ss[p]
-        e_x = ee[n, 0, p] + s * ((h_z - pltpu.roll(h_z, 1, 0)) - (h_y - down_z(h_y)))
-        e_y = ee[n, 1, p] + s * ((h_x - down_z(h_x)) - (h_z - h_zb))
-        e_z = ee[n, 2, p] + s * ((h_y - h_yb) - (h_x - pltpu.roll(h_x, 1, 0)))
-        ee[n + 1, 0, p], ee[n + 1, 1, p], ee[n + 1, 2, p] = e_x, e_y, e_z
-
-    for n in range(ITERS):
-        left, right = -(HALO - n), BX + HALO - 1 - n
-        h = new_h(n, jnp.int32(left))
-
-        def plane(i, before, n=n):
-            h = new_h(n, i)
-            new_e(n, i, h, before)
-            return h[1], h[2]
-
-        lax.fori_loop(left + 1, right, plane, (h[1], h[2]), unroll=True)
-
-    own = (slice(None), pl.ds(0, BX), pl.ds(0, BY))
-    copies = [
-        pltpu.make_async_copy(ee.at[(ITERS,) + own], e_out, sems.at[0]),
-        pltpu.make_async_copy(hh.at[own], h_out, sems.at[1]),
-    ]
-    for copy in copies:
-        copy.start()
-
-    even_lane = iota((BY, LANES), 1) % 2 == 0
-
-    def gram(j, sums):
-        c, p = j // BX, j % BX
-        e = [ee[n + 1, c, p, pl.ds(0, BY)] for n in range(ITERS)]
-        permit = permit_ref[p]
-        f = [sum(w_ref[n, k] * e[n] for n in range(ITERS)) for k in range(FILTERS)]
-        g = [v * permit for v in f]
-        o = [jnp.where(even_lane, pltpu.roll(v, LANES - 1, 1), pltpu.roll(v, 1, 1)) for v in g]
-        new = []
-        for right in (g, o):
-            for k in range(FILTERS):
-                for l in range(k, FILTERS):
-                    v = f[k] * right[l]
-                    new.append(v[:8] + v[8:])
-        return tuple(s + v for s, v in zip(sums, new))
-
-    zero = jnp.zeros((8, LANES), jnp.float32)
-    sums = lax.fori_loop(0, 3 * BX, gram, (zero,) * 20, unroll=4)
+    def act(before):
+        base = BX + HALO if before else BX
+        near, rest = near_planes(before)
+        near_h_out = [i for i in range(BX) if i in near_h(before, ITERS)]
+        rest_h_out = [i for i in range(BX) if i not in near_h_out]
+
+        def copies_of(which, e, h, e_planes, h_planes):
+            e_at, h_at = pl.ds(e_planes[0], len(e_planes)), pl.ds(h_planes[0], len(h_planes))
+            return [
+                pltpu.make_async_copy(e.at[ITERS, :, e_at, pl.ds(0, BY)], e_out.at[:, e_at], sems.at[which, 0]),
+                pltpu.make_async_copy(h.at[:, h_at, pl.ds(0, BY)], h_out.at[:, h_at], sems.at[which, 1]),
+            ]
+
+        copies = copies_of(0, ee, hh, near, near_h_out)
+        for copy in copies:
+            copy.start()
+        extended = fields(fe.at[0], fh, fs)
+        for dst, ghost in zip(extended, fields(ge, gh, gs)):
+            dst[base : base + HALO, :BY] = ghost[...]
+        unpack_y(pairs_of(extended, HALO, base), ya2, yb2, corner)
+        done = set()
+        far = range(-HALO, 0) if before else range(BX, BX + HALO)
+
+        def e_at(n, c, i):
+            return (ee if i in near_e(before, n) else fe)[n, c, i % PX]
+
+        def h_at(c, i):
+            return (fh if i in done or i in far else hh)[c, i % PX]
+
+        def scale_at(i):
+            return (fs if i in far else ss)[i % PX]
+
+        def put_h(i, values):
+            done.add(i)
+            for c in range(3):
+                fh[c, i % PX] = values[c]
+
+        for n in range(1, ITERS + 1):
+
+            def put_e(i, values, n=n):
+                for c in range(3):
+                    fe[n, c, i % PX] = values[c]
+
+            all_h = range(n - 1 - HALO, BX + HALO - n)
+            all_e = range(n - HALO, BX + HALO - n)
+            advance(
+                [i for i in all_h if i not in near_h(before, n)], [i for i in all_e if i not in near_e(before, n)],
+                lambda c, i: e_at(n - 1, c, i), h_at, scale_at, put_e, put_h,
+            )
+        last = copies_of(1, fe, fh, rest, rest_h_out)
+        for copy in last:
+            copy.start()
+        sums = gram_terms(e_at, permit_ref, w_ref, rest, [sums_in[i] for i in range(20)])
+        for i in range(20):
+            sums_ref[i] = sums[i]
+        for copy in copies + last:
+            copy.wait()
+
+    both_sides(act)
     row_of = iota((32, LANES), 0)
     rows = jnp.zeros((32, LANES), jnp.float32)
     at = 0
     for cross in range(2):
         for k in range(FILTERS):
             for l in range(k, FILTERS):
-                line = jnp.sum(sums[at], axis=0, keepdims=True)
+                line = jnp.sum(sums_ref[at], axis=0, keepdims=True)
                 rows = jnp.where(row_of == cross * 16 + k * 4 + l, line, rows)
                 at += 1
 
@@ -271,8 +373,6 @@
     totals = jnp.dot(rows, lane_source, precision=lax.Precision.HIGHEST, preferred_element_type=jnp.float32)
     vector = jnp.sum(jnp.where(row_of == entry((32, LANES))[0], totals, 0.0), axis=0, keepdims=True)
     part_ref[...] = jnp.broadcast_to(vector[None], part_ref.shape)
-    for copy in copies:
-        copy.wait()
 
 
 def add_up(in_ref, out_ref):
@@ -312,20 +412,23 @@
     y_first = (f32(7 * (BX + HALO) // 2, 8, LANES),) * 2
     y_corner = f32(7 * HALO // 2, 8, LANES)
     scratch = (pltpu.VMEM((2, 3, BY, NZ), jnp.int32), pltpu.SemaphoreType.DMA((2, 7)))
-    send_a, send_b = call(pack_x, x_message, "pack_x", 3, scratch=scratch, hbm=(0, 1, 2), size=1 << 20)(
-        *(
-            pltpu.with_memory_space_constraint(v, pltpu.HBM)
-            for v in (e_field.reshape(3, BX * BY, LANES), h_field.reshape(3, BX * BY, LANES), material)
-        )
-    )
+    block = [
+        pltpu.with_memory_space_constraint(v, pltpu.HBM)
+        for v in (e_field.reshape(3, BX * BY, LANES), h_field.reshape(3, BX * BY, LANES), material)
+    ]
+    send_a, send_b = call(pack_x, x_message, "pack_x", 3, scratch=scratch, hbm=(0, 1, 2), size=1 << 20)(*block)
     got_a = lax.ppermute(send_a, "gx", swap_pairs(n_gx, False))
     got_b = lax.ppermute(send_b, "gx", swap_pairs(n_gx, True))
-    permit, scaled = call(own_cells, (f32(BX, BY, LANES),) * 2, "own_cells", 2, smem=(1,), size=1 << 18)(
-        material, permittivity
-    )
+    outs = (f32(3, BX * BY, LANES), f32(3, BX * BY, LANES), f32(BX, BY, LANES), f32(BX, BY, LANES))
+    scratch = (pltpu.VMEM((BX, BY, NZ), jnp.int32), pltpu.SemaphoreType.DMA((3,)))
+    permittivity, weights = lax.optimization_barrier((permittivity, weights))
+    own_e, own_h, permit, scaled = call(
+        own_block, outs, "own_block", 4, scratch=scratch, smem=(3,), hbm=(0, 1, 2), size=1 << 20
+    )(*block, permittivity)
+    own_e, own_h = own_e.reshape(e_field.shape), own_h.reshape(h_field.shape)
     ghosts = (f32(3, HALO, BY, LANES), f32(3, HALO, BY, LANES), f32(HALO, BY, LANES))
     *near, send_a, send_b, send_c = call(near_side, ghosts + y_first + (y_corner,), "near_side", 5, smem=(4,), size=1 << 20)(
-        e_field, h_field, scaled, got_a, permittivity
+        own_e, own_h, scaled, got_a, permittivity
     )
     end = n_gy - 1
     diagonal = [(a * n_gy + g, b * n_gy + end - g) for a, b in swap_pairs(n_gx, True) for g in (0, end)]
@@ -340,16 +443,16 @@
     yb2 = lax.ppermute(send_b, "gy", swap_pairs(n_gy, True, wrap=False))
     planes, columns = sum_groups(n_gx, n_gy)
     n_plane, n_column = len(planes[0]), len(columns[0])
-    scratch = (
-        pltpu.VMEM((ITERS + 1, 3, PX, PY, LANES), jnp.float32),
-        pltpu.VMEM((3, PX, PY, LANES), jnp.float32),
-        pltpu.VMEM((PX, PY, LANES), jnp.float32),
-        pltpu.SemaphoreType.DMA((2,)),
+    levels = (f32(ITERS + 1, 3, PX, PY, LANES), f32(3, PX, PY, LANES), f32(PX, PY, LANES))
+    sums = f32(20, 8, LANES)
+    state = call(near_steps, levels + (sums,), "near_steps", 10, smem=(9,), flops=1 << 24, size=1 << 22)(
+        own_e, own_h, scaled, permit, *near, ya1, yb1, weights
     )
+    scratch = [pltpu.VMEM(v.shape, jnp.float32) for v in levels + (sums,)] + [pltpu.SemaphoreType.DMA((2, 2))]
     outs = (f32(3, BX, BY, LANES), f32(3, BX, BY, LANES), f32(n_plane, 1, LANES))
     e_out, h_out, part = call(
-        steps, outs, "steps", 16, scratch=scratch, smem=(15,), hbm_out=(0, 1), flops=1 << 24, size=1 << 22
-    )(e_field, h_field, scaled, permit, *near, *far, ya1, yb1, ya2, yb2, corner, weights)
+        far_steps, outs, "far_steps", 12, scratch=scratch, smem=(11,), hbm_out=(0, 1), flops=1 << 24, size=1 << 22
+    )(*state, permit, *far, corner, yb2, ya2, weights)
     both = ("gx", "gy")
     part = lax.all_to_all(part, both, 0, 0, axis_index_groups=planes, tiled=True)
     part = call(add_up, f32(n_column, 1, LANES), "add_up", 1, size=1 << 14)(part)

time: 94.8 us -> 92.5 us (0.976)
  waiting for transfers between devices: 9.96 us -> 5.82 us
    ppermute x1, waiting for transfers between devices: 8.26 us -> 5.81 us  [body(): got_b = lax.ppermute(send_b, 'gx', swap_pairs(n_gx, True))]
    all_to_all x1, blocking collectives: 28.4 us -> 26.7 us  [body(): lax.all_to_all(part, both, 0, 0, axis_index_groups=columns, tiled=True)]
    ppermute x1, waiting for transfers between devices: 1.7 us -> 0.01 us  [body(): yb2 = lax.ppermute(send_b, 'gy', swap_pairs(n_gy, True, wrap=False))]
    all_to_all x1, blocking collectives: 8.68 us -> 10.2 us  [body(): lax.all_to_all(part, both, 0, 0, axis_index_groups=planes, tiled=True)]
    ppermute x1, starting transfers between devices: 3.3 us -> 1.92 us  [body(): ya2 = lax.ppermute(send_a, 'gy', swap_pairs(n_gy, False))]
    ppermute x1, starting transfers between devices: 5.08 us -> 6.4 us  [body(): yb2 = lax.ppermute(send_b, 'gy', swap_pairs(n_gy, True, wrap=False))]
    pallas_call x2 -> x3, Pallas kernels: 4.85 us -> 5.71 us  [the longest x1 2.13 us: body(): call(far_steps, outs, 'far_steps', 12, scratch=scratch, smem=(11,), hbm_o...]
  transfers between devices with their start and end apart: 7 -> 7, of which waited for: 2 -> 1; matrix products, arithmetic and copies ran while one was open for 0% -> 1% of each run, Pallas kernels for 2% -> 5%
where the time goes in v4:
time: 92.5 us; the launch traced here: 92.1 us
  starting transfers between devices  38.1 us (41%)
  blocking collectives  36.9 us (40%)
  Pallas kernels  9.13 us (10%)
  waiting for transfers between devices  5.82 us (6%)
    all_to_all x1, blocking collectives, body(): lax.all_to_all(part, both, 0, 0, axis_index_groups=columns, tiled=True)  26.7 us
    ppermute x1, starting transfers between devices, body(): got_b = lax.ppermute(send_b, 'gx', swap_pairs(n_gx, True))  19.4 us
    all_to_all x1, blocking collectives, body(): lax.all_to_all(part, both, 0, 0, axis_index_groups=planes, tiled=True)  10.2 us
    ppermute x1, starting transfers between devices, body(): yb2 = lax.ppermute(send_b, 'gy', swap_pairs(n_gy, True, wrap=False))  6.4 us
    ppermute x1, waiting for transfers between devices, body(): got_b = lax.ppermute(send_b, 'gx', swap_pairs(n_gx, True))  5.81 us
    ppermute x1, starting transfers between devices, body(): got_a = lax.ppermute(send_a, 'gx', swap_pairs(n_gx, False))  3.95 us
    ppermute x1, starting transfers between devices, body(): ya1 = lax.ppermute(send_a, 'gy', swap_pairs(n_gy, False))  3.14 us
    ppermute x1, starting transfers between devices, body(): yb1 = lax.ppermute(send_b, 'gy', swap_pairs(n_gy, True))  2.54 us
  transfers between devices with their start and end apart: 7, of which 1 were waited for; matrix products, arithmetic and copies ran while one was open for 1% of the time, Pallas kernels for 5%

profile of v4, /device:TPU:1, one launch (start us, length us, event | category | flops | bytes accessed | tf_op | source)
XLA Modules:
  0.0 92.1 jit_solution(9599689249695842263)
XLA Ops:
  0.6 1.2 %pack_x.1 = (f32[392,128]{1,0:T(8,128)S(1)}, f32[392,128]{1,0:T(8,128)S(1)}) custom-call(f32[3,128,128]{2,1,0:T(8,128)} %bitcast.8, f32[3,128,128]{2,1,0:T(8,128)} %bitcast.10, s32[8,16,64]{2,1,0:T(8,128)} %m_ref.1), custom_call_target="tpu_custom_call" | custom-call | bytes 1048576 | tf_op jit(solution)/shard_map/pack_x/pallas_call | solution.py:419
  1.8 3.9 %collective-permute-start = (f32[392,128]{1,0:T(8,128)S(1)}, f32[392,128]{1,0:T(8,128)S(1)}, u32[]{:S(2)}, u32[]{:S(2)}) collective-permute-start(f32[392,128]{1,0:T(8,128)S(1)} %get-tuple-element.36), channel_id=1, source_target_pairs={{0,16},{16,0},{32,48},{48,32},{64,80},{80,64},{96,112},{112,96},{1... | collective-permute-start | bytes 602120 | tf_op jit(solution)/shard_map/ppermute | solution.py:420
  5.8 19.4 %collective-permute-start.1 = (f32[392,128]{1,0:T(8,128)S(1)}, f32[392,128]{1,0:T(8,128)S(1)}, u32[]{:S(2)}, u32[]{:S(2)}) collective-permute-start(f32[392,128]{1,0:T(8,128)S(1)} %get-tuple-element.40), channel_id=1, source_target_pairs={{0,496},{16,32},{32,16},{48,64},{64,48},{80,96},{96,80},{112,128},... | collective-permute-start | bytes 602120 | tf_op jit(solution)/shard_map/ppermute | solution.py:421
  25.2 0.8 multiply_cosine_fusion.w_ref
  26.0 0.0 copy-start
  26.0 0.6 copy-done
  26.7 1.7 %own_block.1 = (f32[3,128,128]{2,1,0:T(8,128)S(1)}, f32[3,128,128]{2,1,0:T(8,128)S(1)}, f32[8,16,128]{2,1,0:T(8,128)S(1)}, f32[8,16,128]{2,1,0:T(8,128)S(1)}) custom-call(f32[3,128,128]{2,1,0:T(8,128)} %bitcast.9, f32[3,128,128]{2,1,0:T(8,128)} %bitcast.11, s32[8,16,64]{2,1,0:T(8,128)} %m_ref.1, f32[4]{0:T(128)S(1)} %copy-done), custom_call_target="tpu_custom_call" | custom-call | bytes 1048576 | tf_op jit(solution)/shard_map/own_block/pallas_call | solution.py:425
  28.4 0.0 collective-permute-done.a_ref
  28.4 0.7 near_side.1
  29.1 3.1 %collective-permute-start.2 = (f32[42,8,128]{2,1,0:T(8,128)S(1)}, f32[42,8,128]{2,1,0:T(8,128)S(1)}, u32[]{:S(2)}, u32[]{:S(2)}) collective-permute-start(f32[42,8,128]{2,1,0:T(8,128)S(1)} %get-tuple-element.41), channel_id=1, source_target_pairs={{0,1},{1,0},{2,3},{3,2},{4,5},{5,4},{6,7},{7,6},{8,9},{9,8},{10,11... | collective-permute-start | bytes 516104 | tf_op jit(solution)/shard_map/ppermute | solution.py:437
  32.3 2.5 %collective-permute-start.3 = (f32[42,8,128]{2,1,0:T(8,128)S(1)}, f32[42,8,128]{2,1,0:T(8,128)S(1)}, u32[]{:S(2)}, u32[]{:S(2)}) collective-permute-start(f32[42,8,128]{2,1,0:T(8,128)S(1)} %get-tuple-element.43), channel_id=1, source_target_pairs={{0,15},{1,2},{2,1},{3,4},{4,3},{5,6},{6,5},{7,8},{8,7},{9,10},{10,... | collective-permute-start | bytes 516104 | tf_op jit(solution)/shard_map/ppermute | solution.py:435
  34.8 0.7 collective-permute-start.4
  35.5 5.8 %collective-permute-done.1.b_ref = f32[392,128]{1,0:T(8,128)S(1)} collective-permute-done((f32[392,128]{1,0:T(8,128)S(1)}, f32[392,128]{1,0:T(8,128)S(1)}, u32[]{:S(2)}, u32[]{:S(2)}) %collective-permute-start.1) | collective-permute-done | bytes 200736 | tf_op jit(solution)/shard_map/ppermute | solution.py:421
  41.3 0.0 collective-permute-done.2.ya1
  41.3 0.7 far_side.1
  42.0 6.4 %collective-permute-start.5 = (f32[14,8,128]{2,1,0:T(8,128)S(1)}, f32[14,8,128]{2,1,0:T(8,128)S(1)}, u32[]{:S(2)}, u32[]{:S(2)}) collective-permute-start(f32[14,8,128]{2,1,0:T(8,128)S(1)} %get-tuple-element.54), channel_id=1, source_target_pairs={{1,2},{2,1},{3,4},{4,3},{5,6},{6,5},{7,8},{8,7},{9,10},{10,9},{11,... | collective-permute-start | bytes 172040 | tf_op jit(solution)/shard_map/ppermute | solution.py:443
  48.4 1.9 %collective-permute-start.6 = (f32[14,8,128]{2,1,0:T(8,128)S(1)}, f32[14,8,128]{2,1,0:T(8,128)S(1)}, u32[]{:S(2)}, u32[]{:S(2)}) collective-permute-start(f32[14,8,128]{2,1,0:T(8,128)S(1)} %get-tuple-element.55), channel_id=1, source_target_pairs={{0,1},{1,0},{2,3},{3,2},{4,5},{5,4},{6,7},{7,6},{8,9},{9,8},{10,11... | collective-permute-start | bytes 172040 | tf_op jit(solution)/shard_map/ppermute | solution.py:442
  50.4 1.8 %near_steps.1 = (f32[5,3,16,24,128]{4,3,2,1,0:T(8,128)S(1)}, f32[3,16,24,128]{3,2,1,0:T(8,128)S(1)}, f32[16,24,128]{2,1,0:T(8,128)S(1)}, f32[20,8,128]{2,1,0:T(8,128)S(1)}) custom-call(f32[3,8,16,128]{3,2,1,0:T(8,128)S(1)} %bitcast.5, f32[3,8,16,128]{3,2,1,0:T(8,128)S(1)} %bitcast.7, f32[8,16,128]{2,1,0:T(8,128)S(1)} %get-tuple-element.34.s_ref.own_s, ...), custom_call_target="tpu_custom_call" | custom-call | flops 16777216 | bytes 4194304 | tf_op jit(solution)/shard_map/near_steps/pallas_call | solution.py:448
  52.2 0.0 collective-permute-done.5.yb2
  52.2 0.0 collective-permute-done.6.ya2
  52.2 2.1 %far_steps.1 = (f32[3,8,16,128]{3,2,1,0:T(8,128)}, f32[3,8,16,128]{3,2,1,0:T(8,128)}, f32[32,1,128]{2,1,0:T(1,128)S(1)}) custom-call(f32[5,3,16,24,128]{4,3,2,1,0:T(8,128)S(1)} %get-tuple-element.45.ee, f32[3,16,24,128]{3,2,1,0:T(8,128)S(1)} %get-tuple-element.46.hh, f32[16,24,128]{2,1,0:T(8,128)S(1)} %get-tuple-element.47.ss, ...), custom_call_target="tpu_custom_call" | custom-call | flops 16777216 | bytes 4194304 | tf_op jit(solution)/shard_map/far_steps/pallas_call | solution.py:453
  54.4 10.2 %all_to_all.10.in_ref = f32[32,1,128]{2,1,0:T(1,128)S(1)} all-to-all(f32[32,1,128]{2,1,0:T(1,128)S(1)} %get-tuple-element.58), channel_id=1, replica_groups={{0,1,16,17,32,33,48,49,128,129,144,145,160,161,176,177,256,257,272,273,..., dimensions={0} | all-to-all | bytes 32768 | tf_op jit(solution)/shard_map/all_to_all | solution.py:457
  64.6 26.7 %all_to_all.11.in_ref = f32[16,1,128]{2,1,0:T(1,128)S(1)} all-to-all(f32[16,1,128]{2,1,0:T(1,128)S(1)} %add_up.1), channel_id=1, replica_groups={{0,2,4,6,8,10,12,14,64,66,68,70,72,74,76,78},{1,3,5,7,9,11,13,15,65,67,..., dimensions={0} | all-to-all | bytes 16384 | tf_op jit(solution)/shard_map/all_to_all | solution.py:459
  91.3 0.8 finish.1
  (4 shorter events, 0.1 us)
Async XLA Ops:
  1.8 26.6 %collective-permute-start = (f32[392,128]{1,0:T(8,128)S(1)}, f32[392,128]{1,0:T(8,128)S(1)}, u32[]{:S(2)}, u32[]{:S(2)}) collective-permute-start(f32[392,128]{1,0:T(8,128)S(1)} %get-tuple-element.36), channel_id=1, source_target_pairs={{0,16},{16,0},{32,48},{48,32},{64,80},{80,64},{96,112},{112,96},{1... | collective-permute-start | bytes 602120 | tf_op jit(solution)/shard_map/ppermute | solution.py:420
  5.8 35.5 %collective-permute-start.1 = (f32[392,128]{1,0:T(8,128)S(1)}, f32[392,128]{1,0:T(8,128)S(1)}, u32[]{:S(2)}, u32[]{:S(2)}) collective-permute-start(f32[392,128]{1,0:T(8,128)S(1)} %get-tuple-element.40), channel_id=1, source_target_pairs={{0,496},{16,32},{32,16},{48,64},{64,48},{80,96},{96,80},{112,128},... | collective-permute-start | bytes 602120 | tf_op jit(solution)/shard_map/ppermute | solution.py:421
  26.0 0.7 copy-start
  29.1 12.2 %collective-permute-start.2 = (f32[42,8,128]{2,1,0:T(8,128)S(1)}, f32[42,8,128]{2,1,0:T(8,128)S(1)}, u32[]{:S(2)}, u32[]{:S(2)}) collective-permute-start(f32[42,8,128]{2,1,0:T(8,128)S(1)} %get-tuple-element.41), channel_id=1, source_target_pairs={{0,1},{1,0},{2,3},{3,2},{4,5},{5,4},{6,7},{7,6},{8,9},{9,8},{10,11... | collective-permute-start | bytes 516104 | tf_op jit(solution)/shard_map/ppermute | solution.py:437
  32.3 18.1 %collective-permute-start.3 = (f32[42,8,128]{2,1,0:T(8,128)S(1)}, f32[42,8,128]{2,1,0:T(8,128)S(1)}, u32[]{:S(2)}, u32[]{:S(2)}) collective-permute-start(f32[42,8,128]{2,1,0:T(8,128)S(1)} %get-tuple-element.43), channel_id=1, source_target_pairs={{0,15},{1,2},{2,1},{3,4},{4,3},{5,6},{6,5},{7,8},{8,7},{9,10},{10,... | collective-permute-start | bytes 516104 | tf_op jit(solution)/shard_map/ppermute | solution.py:435
  34.8 17.4 %collective-permute-start.4 = (f32[14,8,128]{2,1,0:T(8,128)S(1)}, f32[14,8,128]{2,1,0:T(8,128)S(1)}, u32[]{:S(2)}, u32[]{:S(2)}) collective-permute-start(f32[14,8,128]{2,1,0:T(8,128)S(1)} %get-tuple-element.53), channel_id=1, source_target_pairs={{0,511},{15,496},{16,47},{31,32},{32,31},{47,16},{48,79},{63,64},{... | collective-permute-start | bytes 172040 | tf_op jit(solution)/shard_map/ppermute | solution.py:436
  42.0 10.2 %collective-permute-start.5 = (f32[14,8,128]{2,1,0:T(8,128)S(1)}, f32[14,8,128]{2,1,0:T(8,128)S(1)}, u32[]{:S(2)}, u32[]{:S(2)}) collective-permute-start(f32[14,8,128]{2,1,0:T(8,128)S(1)} %get-tuple-element.54), channel_id=1, source_target_pairs={{1,2},{2,1},{3,4},{4,3},{5,6},{6,5},{7,8},{8,7},{9,10},{10,9},{11,... | collective-permute-start | bytes 172040 | tf_op jit(solution)/shard_map/ppermute | solution.py:443
  48.4 3.8 %collective-permute-start.6 = (f32[14,8,128]{2,1,0:T(8,128)S(1)}, f32[14,8,128]{2,1,0:T(8,128)S(1)}, u32[]{:S(2)}, u32[]{:S(2)}) collective-permute-start(f32[14,8,128]{2,1,0:T(8,128)S(1)} %get-tuple-element.55), channel_id=1, source_target_pairs={{0,1},{1,0},{2,3},{3,2},{4,5},{5,4},{6,7},{7,6},{8,9},{9,8},{10,11... | collective-permute-start | bytes 172040 | tf_op jit(solution)/shard_map/ppermute | solution.py:442

commit v5 on v4

--- a/solution.py
+++ b/solution.py
@@ -105,13 +105,13 @@
         copy.wait()
 
 
-def fill_ghosts(src, after, p_ref, e_ref, h_ref, s_ref):
+def fill_ghosts(src, after, p_ref, e_ref, h_ref, s_ref, first_row=0):
     narrow = jnp.where(after, 0, 1)
     row = 0
     for ref, c, n, start in x_parts(e_ref, h_ref, 0, narrow):
-        ref[c, pl.ds(start, n)] = src[pl.ds(row, n * BY)].reshape(n, BY, LANES)
+        ref[c, pl.ds(start, n)] = src[pl.ds(first_row + row, n * BY)].reshape(n, BY, LANES)
         row += n * BY
-    cells = src[pl.ds(row, 24)].astype(jnp.bfloat16)
+    cells = src[pl.ds(first_row + row, 24)].astype(jnp.bfloat16)
     for half in range(2):
         index = jnp.dot(cells, spread(LANES, half * NZ), preferred_element_type=jnp.float32)
         value = TIME_STEP / look_up(index, p_ref)
@@ -160,7 +160,8 @@
 
 def near_side(e_ref, h_ref, s_ref, a_ref, p_ref, ge_ref, gh_ref, gs_ref, ya_ref, yb_ref, corner_ref):
     even = lax.rem(lax.axis_index("gx"), 2) == 0
-    fill_ghosts(a_ref, even, p_ref, ge_ref, gh_ref, gs_ref)
+    other = pl.multiple_of(jnp.where(even, 8 * XTILES, 0), 8)
+    fill_ghosts(a_ref, even, p_ref, ge_ref, gh_ref, gs_ref, other)
     own = fields(e_ref, h_ref, s_ref)
     pack_y(pairs_of(own, BX) + pairs_of(fields(ge_ref, gh_ref, gs_ref), HALO), ya_ref, yb_ref)
     start = jnp.where(even, 0, BX - HALO)
@@ -417,7 +418,8 @@
         for v in (e_field.reshape(3, BX * BY, LANES), h_field.reshape(3, BX * BY, LANES), material)
     ]
     send_a, send_b = call(pack_x, x_message, "pack_x", 3, scratch=scratch, hbm=(0, 1, 2), size=1 << 20)(*block)
-    got_a = lax.ppermute(send_a, "gx", swap_pairs(n_gx, False))
+    near_pairs = [[i, i + 1] for i in range(0, n_gx, 2)]
+    got_a = lax.all_gather(send_a, "gx", axis_index_groups=near_pairs, tiled=True)
     got_b = lax.ppermute(send_b, "gx", swap_pairs(n_gx, True))
     outs = (f32(3, BX * BY, LANES), f32(3, BX * BY, LANES), f32(BX, BY, LANES), f32(BX, BY, LANES))
     scratch = (pltpu.VMEM((BX, BY, NZ), jnp.int32), pltpu.SemaphoreType.DMA((3,)))

time: 92.5 us -> 88.5 us (0.957)
  waiting for transfers between devices: 5.82 us -> 0.02 us
  blocking collectives: 36.9 us -> 41.7 us
  starting transfers between devices: 38.1 us -> 35 us
    all_gather x0 -> x1, blocking collectives: none -> 6.22 us  [body(): lax.all_gather(send_a, 'gx', axis_index_groups=near_pairs, tiled=True)]
    all_to_all x1, blocking collectives: 26.7 us -> 20.7 us  [body(): lax.all_to_all(part, both, 0, 0, axis_index_groups=columns, tiled=True)]
    ppermute x1, waiting for transfers between devices: 5.81 us -> 0.01 us  [body(): got_b = lax.ppermute(send_b, 'gx', swap_pairs(n_gx, True))]
    all_to_all x1, blocking collectives: 10.2 us -> 14.7 us  [body(): lax.all_to_all(part, both, 0, 0, axis_index_groups=planes, tiled=True)]
    ppermute x1 -> x0, starting transfers between devices: 3.95 us -> none  [body(): got_a = lax.ppermute(send_a, 'gx', swap_pairs(n_gx, False))]
    ppermute x1, starting transfers between devices: 6.4 us -> 3.65 us  [body(): yb2 = lax.ppermute(send_b, 'gy', swap_pairs(n_gy, True, wrap=False))]
    ppermute x1, starting transfers between devices: 19.4 us -> 20.9 us  [body(): got_b = lax.ppermute(send_b, 'gx', swap_pairs(n_gx, True))]
    ppermute x1, starting transfers between devices: 1.92 us -> 3.4 us  [body(): ya2 = lax.ppermute(send_a, 'gy', swap_pairs(n_gy, False))]
  transfers between devices with their start and end apart: 7 -> 6, of which waited for: 1 -> 0; matrix products, arithmetic and copies ran while one was open for 1% -> 1% of each run, Pallas kernels for 5% -> 6%
where the time goes in v5:
time: 88.5 us; the launch traced here: 88 us
  blocking collectives  41.7 us (47%)
  starting transfers between devices  35 us (40%)
  Pallas kernels  9.18 us (10%)
    ppermute x1, starting transfers between devices, body(): got_b = lax.ppermute(send_b, 'gx', swap_pairs(n_gx, True))  20.9 us
    all_to_all x1, blocking collectives, body(): lax.all_to_all(part, both, 0, 0, axis_index_groups=columns, tiled=True)  20.7 us
    all_to_all x1, blocking collectives, body(): lax.all_to_all(part, both, 0, 0, axis_index_groups=planes, tiled=True)  14.7 us
    all_gather x1, blocking collectives, body(): lax.all_gather(send_a, 'gx', axis_index_groups=near_pairs, tiled=True)  6.22 us
    ppermute x1, starting transfers between devices, body(): ya1 = lax.ppermute(send_a, 'gy', swap_pairs(n_gy, False))  3.77 us
    ppermute x1, starting transfers between devices, body(): yb2 = lax.ppermute(send_b, 'gy', swap_pairs(n_gy, True, wrap=False))  3.65 us
    ppermute x1, starting transfers between devices, body(): ya2 = lax.ppermute(send_a, 'gy', swap_pairs(n_gy, False))  3.4 us
    ppermute x1, starting transfers between devices, body(): yb1 = lax.ppermute(send_b, 'gy', swap_pairs(n_gy, True))  2.54 us
  transfers between devices with their start and end apart: 6, of which 0 were waited for; matrix products, arithmetic and copies ran while one was open for 1% of the time, Pallas kernels for 6%

profile of v5, /device:TPU:1, one launch (start us, length us, event | category | flops | bytes accessed | tf_op | source)
XLA Modules:
  0.0 88.0 jit_solution(13518177550197450249)
XLA Ops:
  0.6 1.2 %pack_x.1 = (f32[392,128]{1,0:T(8,128)S(1)}, f32[392,128]{1,0:T(8,128)S(1)}) custom-call(f32[3,128,128]{2,1,0:T(8,128)} %bitcast.8, f32[3,128,128]{2,1,0:T(8,128)} %bitcast.10, s32[8,16,64]{2,1,0:T(8,128)} %m_ref.1), custom_call_target="tpu_custom_call" | custom-call | bytes 1048576 | tf_op jit(solution)/shard_map/pack_x/pallas_call | solution.py:420
  1.8 20.9 %collective-permute-start = (f32[392,128]{1,0:T(8,128)S(1)}, f32[392,128]{1,0:T(8,128)S(1)}, u32[]{:S(2)}, u32[]{:S(2)}) collective-permute-start(f32[392,128]{1,0:T(8,128)S(1)} %get-tuple-element.40), channel_id=1, source_target_pairs={{0,496},{16,32},{32,16},{48,64},{64,48},{80,96},{96,80},{112,128},... | collective-permute-start | bytes 602120 | tf_op jit(solution)/shard_map/ppermute | solution.py:423
  22.8 0.8 multiply_cosine_fusion.w_ref
  23.5 6.2 %all_gather.3.a_ref = f32[784,128]{1,0:T(8,128)S(1)} all-gather(f32[392,128]{1,0:T(8,128)S(1)} %get-tuple-element.36), channel_id=1, replica_groups={{0,16},{32,48},{64,80},{96,112},{128,144},{160,176},{192,208},{224,240}..., dimensions={0}, use_global_device_ids=true | all-gather | bytes 602112 | tf_op jit(solution)/shard_map/all_gather | solution.py:422
  29.8 0.7 copy-done
  30.4 1.7 %own_block.1 = (f32[3,128,128]{2,1,0:T(8,128)S(1)}, f32[3,128,128]{2,1,0:T(8,128)S(1)}, f32[8,16,128]{2,1,0:T(8,128)S(1)}, f32[8,16,128]{2,1,0:T(8,128)S(1)}) custom-call(f32[3,128,128]{2,1,0:T(8,128)} %bitcast.9, f32[3,128,128]{2,1,0:T(8,128)} %bitcast.11, s32[8,16,64]{2,1,0:T(8,128)} %m_ref.1, f32[4]{0:T(128)S(1)} %copy-done), custom_call_target="tpu_custom_call" | custom-call | bytes 1048576 | tf_op jit(solution)/shard_map/own_block/pallas_call | solution.py:427
  32.2 0.8 near_side.1
  32.9 3.8 %collective-permute-start.1 = (f32[42,8,128]{2,1,0:T(8,128)S(1)}, f32[42,8,128]{2,1,0:T(8,128)S(1)}, u32[]{:S(2)}, u32[]{:S(2)}) collective-permute-start(f32[42,8,128]{2,1,0:T(8,128)S(1)} %get-tuple-element.41), channel_id=1, source_target_pairs={{0,1},{1,0},{2,3},{3,2},{4,5},{5,4},{6,7},{7,6},{8,9},{9,8},{10,11... | collective-permute-start | bytes 516104 | tf_op jit(solution)/shard_map/ppermute | solution.py:439
  36.7 2.5 %collective-permute-start.2 = (f32[42,8,128]{2,1,0:T(8,128)S(1)}, f32[42,8,128]{2,1,0:T(8,128)S(1)}, u32[]{:S(2)}, u32[]{:S(2)}) collective-permute-start(f32[42,8,128]{2,1,0:T(8,128)S(1)} %get-tuple-element.43), channel_id=1, source_target_pairs={{0,15},{1,2},{2,1},{3,4},{4,3},{5,6},{6,5},{7,8},{8,7},{9,10},{10,... | collective-permute-start | bytes 516104 | tf_op jit(solution)/shard_map/ppermute | solution.py:437
  39.3 0.7 collective-permute-start.3
  39.9 0.0 collective-permute-done.1.ya1
  40.0 0.0 collective-permute-done.b_ref
  40.0 0.7 far_side.1
  40.7 3.7 %collective-permute-start.4 = (f32[14,8,128]{2,1,0:T(8,128)S(1)}, f32[14,8,128]{2,1,0:T(8,128)S(1)}, u32[]{:S(2)}, u32[]{:S(2)}) collective-permute-start(f32[14,8,128]{2,1,0:T(8,128)S(1)} %get-tuple-element.54), channel_id=1, source_target_pairs={{1,2},{2,1},{3,4},{4,3},{5,6},{6,5},{7,8},{8,7},{9,10},{10,9},{11,... | collective-permute-start | bytes 172040 | tf_op jit(solution)/shard_map/ppermute | solution.py:445
  44.3 3.4 %collective-permute-start.5 = (f32[14,8,128]{2,1,0:T(8,128)S(1)}, f32[14,8,128]{2,1,0:T(8,128)S(1)}, u32[]{:S(2)}, u32[]{:S(2)}) collective-permute-start(f32[14,8,128]{2,1,0:T(8,128)S(1)} %get-tuple-element.55), channel_id=1, source_target_pairs={{0,1},{1,0},{2,3},{3,2},{4,5},{5,4},{6,7},{7,6},{8,9},{9,8},{10,11... | collective-permute-start | bytes 172040 | tf_op jit(solution)/shard_map/ppermute | solution.py:444
  47.7 0.0 collective-permute-done.2.yb1
  47.7 1.8 %near_steps.1 = (f32[5,3,16,24,128]{4,3,2,1,0:T(8,128)S(1)}, f32[3,16,24,128]{3,2,1,0:T(8,128)S(1)}, f32[16,24,128]{2,1,0:T(8,128)S(1)}, f32[20,8,128]{2,1,0:T(8,128)S(1)}) custom-call(f32[3,8,16,128]{3,2,1,0:T(8,128)S(1)} %bitcast.5, f32[3,8,16,128]{3,2,1,0:T(8,128)S(1)} %bitcast.7, f32[8,16,128]{2,1,0:T(8,128)S(1)} %get-tuple-element.34.s_ref.own_s, ...), custom_call_target="tpu_custom_call" | custom-call | flops 16777216 | bytes 4194304 | tf_op jit(solution)/shard_map/near_steps/pallas_call | solution.py:450
  49.6 0.0 collective-permute-done.3.corner
  49.6 0.0 collective-permute-done.4.yb2
  49.6 0.0 collective-permute-done.5.ya2
  49.6 2.1 %far_steps.1 = (f32[3,8,16,128]{3,2,1,0:T(8,128)}, f32[3,8,16,128]{3,2,1,0:T(8,128)}, f32[32,1,128]{2,1,0:T(1,128)S(1)}) custom-call(f32[5,3,16,24,128]{4,3,2,1,0:T(8,128)S(1)} %get-tuple-element.45.ee, f32[3,16,24,128]{3,2,1,0:T(8,128)S(1)} %get-tuple-element.46.hh, f32[16,24,128]{2,1,0:T(8,128)S(1)} %get-tuple-element.47.ss, ...), custom_call_target="tpu_custom_call" | custom-call | flops 16777216 | bytes 4194304 | tf_op jit(solution)/shard_map/far_steps/pallas_call | solution.py:455
  51.7 14.7 %all_to_all.10.in_ref = f32[32,1,128]{2,1,0:T(1,128)S(1)} all-to-all(f32[32,1,128]{2,1,0:T(1,128)S(1)} %get-tuple-element.58), channel_id=1, replica_groups={{0,1,16,17,32,33,48,49,128,129,144,145,160,161,176,177,256,257,272,273,..., dimensions={0} | all-to-all | bytes 32768 | tf_op jit(solution)/shard_map/all_to_all | solution.py:459
  66.5 20.7 %all_to_all.11.in_ref = f32[16,1,128]{2,1,0:T(1,128)S(1)} all-to-all(f32[16,1,128]{2,1,0:T(1,128)S(1)} %add_up.1), channel_id=1, replica_groups={{0,2,4,6,8,10,12,14,64,66,68,70,72,74,76,78},{1,3,5,7,9,11,13,15,65,67,..., dimensions={0} | all-to-all | bytes 16384 | tf_op jit(solution)/shard_map/all_to_all | solution.py:461
  87.3 0.8 finish.1
  (3 shorter events, 0.0 us)
Async XLA Ops:
  1.8 38.1 %collective-permute-start = (f32[392,128]{1,0:T(8,128)S(1)}, f32[392,128]{1,0:T(8,128)S(1)}, u32[]{:S(2)}, u32[]{:S(2)}) collective-permute-start(f32[392,128]{1,0:T(8,128)S(1)} %get-tuple-element.40), channel_id=1, source_target_pairs={{0,496},{16,32},{32,16},{48,64},{64,48},{80,96},{96,80},{112,128},... | collective-permute-start | bytes 602120 | tf_op jit(solution)/shard_map/ppermute | solution.py:423
  29.8 0.7 copy-start
  32.9 7.0 %collective-permute-start.1 = (f32[42,8,128]{2,1,0:T(8,128)S(1)}, f32[42,8,128]{2,1,0:T(8,128)S(1)}, u32[]{:S(2)}, u32[]{:S(2)}) collective-permute-start(f32[42,8,128]{2,1,0:T(8,128)S(1)} %get-tuple-element.41), channel_id=1, source_target_pairs={{0,1},{1,0},{2,3},{3,2},{4,5},{5,4},{6,7},{7,6},{8,9},{9,8},{10,11... | collective-permute-start | bytes 516104 | tf_op jit(solution)/shard_map/ppermute | solution.py:439
  36.7 11.0 %collective-permute-start.2 = (f32[42,8,128]{2,1,0:T(8,128)S(1)}, f32[42,8,128]{2,1,0:T(8,128)S(1)}, u32[]{:S(2)}, u32[]{:S(2)}) collective-permute-start(f32[42,8,128]{2,1,0:T(8,128)S(1)} %get-tuple-element.43), channel_id=1, source_target_pairs={{0,15},{1,2},{2,1},{3,4},{4,3},{5,6},{6,5},{7,8},{8,7},{9,10},{10,... | collective-permute-start | bytes 516104 | tf_op jit(solution)/shard_map/ppermute | solution.py:437
  39.3 10.3 %collective-permute-start.3 = (f32[14,8,128]{2,1,0:T(8,128)S(1)}, f32[14,8,128]{2,1,0:T(8,128)S(1)}, u32[]{:S(2)}, u32[]{:S(2)}) collective-permute-start(f32[14,8,128]{2,1,0:T(8,128)S(1)} %get-tuple-element.53), channel_id=1, source_target_pairs={{0,511},{15,496},{16,47},{31,32},{32,31},{47,16},{48,79},{63,64},{... | collective-permute-start | bytes 172040 | tf_op jit(solution)/shard_map/ppermute | solution.py:438
  40.7 8.9 %collective-permute-start.4 = (f32[14,8,128]{2,1,0:T(8,128)S(1)}, f32[14,8,128]{2,1,0:T(8,128)S(1)}, u32[]{:S(2)}, u32[]{:S(2)}) collective-permute-start(f32[14,8,128]{2,1,0:T(8,128)S(1)} %get-tuple-element.54), channel_id=1, source_target_pairs={{1,2},{2,1},{3,4},{4,3},{5,6},{6,5},{7,8},{8,7},{9,10},{10,9},{11,... | collective-permute-start | bytes 172040 | tf_op jit(solution)/shard_map/ppermute | solution.py:445
  44.3 5.3 %collective-permute-start.5 = (f32[14,8,128]{2,1,0:T(8,128)S(1)}, f32[14,8,128]{2,1,0:T(8,128)S(1)}, u32[]{:S(2)}, u32[]{:S(2)}) collective-permute-start(f32[14,8,128]{2,1,0:T(8,128)S(1)} %get-tuple-element.55), channel_id=1, source_target_pairs={{0,1},{1,0},{2,3},{3,2},{4,5},{5,4},{6,7},{7,6},{8,9},{9,8},{10,11... | collective-permute-start | bytes 172040 | tf_op jit(solution)/shard_map/ppermute | solution.py:444

commit v6 on v5

--- a/solution.py
+++ b/solution.py
@@ -50,7 +50,7 @@
     return ((e, 0, 4, wide), (e, 1, 4, wide), (e, 2, 4, wide), (h, 0, 3, narrow), (h, 1, 4, wide), (h, 2, 4, wide))
 
 
-def pack_x(e_ref, h_ref, m_ref, a_ref, b_ref, edge, sems):
+def pack_x(e_ref, h_ref, m_ref, p_ref, f_ref, a_ref, b_ref, own_e, own_h, own_m, table_ref, edge, table, freqs, sems):
     even = lax.rem(lax.axis_index("gx"), 2) == 0
     copies = []
     for side, (out, upper) in enumerate(((a_ref, even), (b_ref, jnp.logical_not(even)))):
@@ -62,6 +62,8 @@
             src = ref.at[c, pl.ds(pl.multiple_of(start * BY, BY), n * BY)]
             copies.append(pltpu.make_async_copy(src, out.at[pl.ds(row, n * BY)], sems.at[side, i]))
             row += n * BY
+    for i, (src, dst) in enumerate(((p_ref, table), (f_ref, freqs), (m_ref, own_m), (e_ref, own_e), (h_ref, own_h))):
+        copies.append(pltpu.make_async_copy(src, dst, sems.at[2, i]))
     for copy in copies:
         copy.start()
     r, col = iota((NZ, LANES), 0), iota((NZ, LANES), 1)
@@ -74,15 +76,21 @@
             out[pl.ds(8 * (XTILES - 3 + i), 8)] = jnp.dot(
                 cells[:8], low, preferred_element_type=jnp.float32
             ) + jnp.dot(cells[8:], high, preferred_element_type=jnp.float32)
+    copies[14].wait()
+    copies[15].wait()
+    for m in range(MATERIALS):
+        table_ref[m] = jnp.full((8, LANES), table[m], jnp.float32)
+    for k in range(FILTERS):
+        table_ref[MATERIALS + k] = jnp.full((8, LANES), freqs[k], jnp.float32)
     for i, copy in enumerate(copies):
-        if i % 7:
+        if i not in (0, 7, 14, 15):
             copy.wait()
 
 
 def look_up(index, table_ref):
-    value = jnp.full(index.shape, table_ref[0], jnp.float32)
+    value = jnp.broadcast_to(table_ref[0, 0:1], index.shape)
     for m in range(1, MATERIALS):
-        value = jnp.where(index == float(m), table_ref[m], value)
+        value = jnp.where(index == float(m), table_ref[m, 0:1], value)
     return value
 
 
@@ -91,18 +99,17 @@
     return (iota(shape, 1) // SOURCES + offset == iota(shape, 0)).astype(jnp.bfloat16)
 
 
-def own_block(e_in, h_in, m_in, p_ref, e_ref, h_ref, permit_ref, scaled_ref, cells, sems):
-    ends = ((e_in, e_ref), (h_in, h_ref), (m_in, cells))
-    copies = [pltpu.make_async_copy(src, dst, sems.at[i]) for i, (src, dst) in enumerate(ends)]
-    for copy in copies:
-        copy.start()
-    copies[2].wait()
-    index = cells[...].reshape(BX * BY, NZ).astype(jnp.float32).astype(jnp.bfloat16)
-    permit = look_up(jnp.dot(index, spread(NZ, 0), preferred_element_type=jnp.float32), p_ref)
+def own_cells(m_ref, p_ref, permit_ref, scaled_ref, w_ref):
+    row = iota((ITERS * FILTERS, LANES), 0)
+    times = (row // FILTERS + 1).astype(jnp.float32) * TIME_STEP
+    freqs = jnp.broadcast_to(p_ref[MATERIALS, 0:1], row.shape)
+    for k in range(1, FILTERS):
+        freqs = jnp.where(row % FILTERS == k, p_ref[MATERIALS + k, 0:1], freqs)
+    w_ref[...] = jnp.cos(freqs * times)
+    cells = m_ref[...].reshape(BX * BY, NZ).astype(jnp.float32).astype(jnp.bfloat16)
+    permit = look_up(jnp.dot(cells, spread(NZ, 0), preferred_element_type=jnp.float32), p_ref)
     permit_ref[...] = permit.reshape(BX, BY, LANES)
     scaled_ref[...] = (TIME_STEP / permit).reshape(BX, BY, LANES)
-    for copy in copies[:2]:
-        copy.wait()
 
 
 def fill_ghosts(src, after, p_ref, e_ref, h_ref, s_ref, first_row=0):
@@ -220,11 +227,12 @@
 
 def gram_terms(e_at, permit_ref, w_ref, planes, sums):
     even_lane = iota((BY, LANES), 1) % 2 == 0
+    w = [jnp.broadcast_to(w_ref[i : i + 1], (BY, LANES)) for i in range(ITERS * FILTERS)]
     for i in planes:
         permit = permit_ref[i]
         for c in range(3):
             e = [e_at(n, c, i)[:BY] for n in range(1, ITERS + 1)]
-            f = [sum(w_ref[n, k] * e[n] for n in range(ITERS)) for k in range(FILTERS)]
+            f = [sum(w[n * FILTERS + k] * e[n] for n in range(ITERS)) for k in range(FILTERS)]
             g = [v * permit for v in f]
             o = [jnp.where(even_lane, pltpu.roll(v, LANES - 1, 1), pltpu.roll(v, 1, 1)) for v in g]
             at = 0
@@ -408,29 +416,28 @@
 
 def body(e_field, h_field, material, permittivity, frequencies):
     n_gx, n_gy = lax.axis_size("gx"), lax.axis_size("gy")
-    weights = jnp.cos(frequencies[None, :] * (jnp.arange(1, ITERS + 1, dtype=jnp.float32)[:, None] * TIME_STEP))
     x_message = (f32(XTILES * 8, LANES),) * 2
     y_first = (f32(7 * (BX + HALO) // 2, 8, LANES),) * 2
     y_corner = f32(7 * HALO // 2, 8, LANES)
-    scratch = (pltpu.VMEM((2, 3, BY, NZ), jnp.int32), pltpu.SemaphoreType.DMA((2, 7)))
+    scratch = (pltpu.VMEM((2, 3, BY, NZ), jnp.int32), pltpu.SMEM((MATERIALS,), jnp.float32), pltpu.SMEM((FILTERS,), jnp.float32), pltpu.SemaphoreType.DMA((3, 7)))
     block = [
         pltpu.with_memory_space_constraint(v, pltpu.HBM)
-        for v in (e_field.reshape(3, BX * BY, LANES), h_field.reshape(3, BX * BY, LANES), material)
+        for v in (e_field.reshape(3, BX * BY, LANES), h_field.reshape(3, BX * BY, LANES), material, permittivity, frequencies)
     ]
-    send_a, send_b = call(pack_x, x_message, "pack_x", 3, scratch=scratch, hbm=(0, 1, 2), size=1 << 20)(*block)
+    outs = x_message + (f32(3, BX * BY, LANES), f32(3, BX * BY, LANES), jax.ShapeDtypeStruct((BX, BY, NZ), jnp.int32))
+    outs += (f32(MATERIALS + FILTERS, 8, LANES),)
+    send_a, send_b, own_e, own_h, own_m, table = call(
+        pack_x, outs, "pack_x", 5, scratch=scratch, hbm=(0, 1, 2, 3, 4), size=1 << 20
+    )(*block)
+    own_e, own_h = own_e.reshape(e_field.shape), own_h.reshape(h_field.shape)
     near_pairs = [[i, i + 1] for i in range(0, n_gx, 2)]
     got_a = lax.all_gather(send_a, "gx", axis_index_groups=near_pairs, tiled=True)
     got_b = lax.ppermute(send_b, "gx", swap_pairs(n_gx, True))
-    outs = (f32(3, BX * BY, LANES), f32(3, BX * BY, LANES), f32(BX, BY, LANES), f32(BX, BY, LANES))
-    scratch = (pltpu.VMEM((BX, BY, NZ), jnp.int32), pltpu.SemaphoreType.DMA((3,)))
-    permittivity, weights = lax.optimization_barrier((permittivity, weights))
-    own_e, own_h, permit, scaled = call(
-        own_block, outs, "own_block", 4, scratch=scratch, smem=(3,), hbm=(0, 1, 2), size=1 << 20
-    )(*block, permittivity)
-    own_e, own_h = own_e.reshape(e_field.shape), own_h.reshape(h_field.shape)
+    outs = (f32(BX, BY, LANES), f32(BX, BY, LANES), f32(ITERS * FILTERS, LANES))
+    permit, scaled, weights = call(own_cells, outs, "own_cells", 2, size=1 << 18)(own_m, table)
     ghosts = (f32(3, HALO, BY, LANES), f32(3, HALO, BY, LANES), f32(HALO, BY, LANES))
-    *near, send_a, send_b, send_c = call(near_side, ghosts + y_first + (y_corner,), "near_side", 5, smem=(4,), size=1 << 20)(
-        own_e, own_h, scaled, got_a, permittivity
+    *near, send_a, send_b, send_c = call(near_side, ghosts + y_first + (y_corner,), "near_side", 5, size=1 << 20)(
+        own_e, own_h, scaled, got_a, table
     )
     end = n_gy - 1
     diagonal = [(a * n_gy + g, b * n_gy + end - g) for a, b in swap_pairs(n_gx, True) for g in (0, end)]
@@ -438,8 +445,8 @@
     corner = lax.ppermute(send_c, ("gx", "gy"), diagonal)
     ya1 = lax.ppermute(send_a, "gy", swap_pairs(n_gy, False))
     got_b, ya1 = lax.optimization_barrier((got_b, ya1))
-    *far, send_a, send_b = call(far_side, ghosts + (y_corner, y_corner), "far_side", 2, smem=(1,), size=1 << 20)(
-        got_b, permittivity
+    *far, send_a, send_b = call(far_side, ghosts + (y_corner, y_corner), "far_side", 2, size=1 << 20)(
+        got_b, table
     )
     ya2 = lax.ppermute(send_a, "gy", swap_pairs(n_gy, False))
     yb2 = lax.ppermute(send_b, "gy", swap_pairs(n_gy, True, wrap=False))
@@ -447,13 +454,13 @@
     n_plane, n_column = len(planes[0]), len(columns[0])
     levels = (f32(ITERS + 1, 3, PX, PY, LANES), f32(3, PX, PY, LANES), f32(PX, PY, LANES))
     sums = f32(20, 8, LANES)
-    state = call(near_steps, levels + (sums,), "near_steps", 10, smem=(9,), flops=1 << 24, size=1 << 22)(
+    state = call(near_steps, levels + (sums,), "near_steps", 10, flops=1 << 24, size=1 << 22)(
         own_e, own_h, scaled, permit, *near, ya1, yb1, weights
     )
     scratch = [pltpu.VMEM(v.shape, jnp.float32) for v in levels + (sums,)] + [pltpu.SemaphoreType.DMA((2, 2))]
     outs = (f32(3, BX, BY, LANES), f32(3, BX, BY, LANES), f32(n_plane, 1, LANES))
     e_out, h_out, part = call(
-        far_steps, outs, "far_steps", 12, scratch=scratch, smem=(11,), hbm_out=(0, 1), flops=1 << 24, size=1 << 22
+        far_steps, outs, "far_steps", 12, scratch=scratch, hbm_out=(0, 1), flops=1 << 24, size=1 << 22
     )(*state, permit, *far, corner, yb2, ya2, weights)
     both = ("gx", "gy")
     part = lax.all_to_all(part, both, 0, 0, axis_index_groups=planes, tiled=True)

time: 88.5 us -> 86.9 us (0.982)
  Pallas kernels: 9.18 us -> 5.58 us
  waiting for transfers between devices: 0.02 us -> 3.21 us
  blocking collectives: 41.7 us -> 43 us
  starting transfers between devices: 35 us -> 34 us
    pallas_call x6, Pallas kernels: 8.37 us -> 4.77 us  [the longest x1 1.56 us: body(): call(far_steps, outs, 'far_steps', 12, scratch=scratch, hbm_out=(0, 1), f...]
    ppermute x1, waiting for transfers between devices: 0.01 us -> 3.2 us  [body(): got_b = lax.ppermute(send_b, 'gx', swap_pairs(n_gx, True))]
    all_to_all x1, blocking collectives: 20.7 us -> 23.4 us  [body(): lax.all_to_all(part, both, 0, 0, axis_index_groups=columns, tiled=True)]
    ppermute x1, starting transfers between devices: 3.4 us -> 1.92 us  [body(): ya2 = lax.ppermute(send_a, 'gy', swap_pairs(n_gy, False))]
    all_to_all x1, blocking collectives: 14.7 us -> 13.4 us  [body(): lax.all_to_all(part, both, 0, 0, axis_index_groups=planes, tiled=True)]
  transfers between devices with their start and end apart: 6 -> 6, of which waited for: 0 -> 1; matrix products, arithmetic and copies ran while one was open for 1% -> 0% of each run, Pallas kernels for 6% -> 2%
where the time goes in v6:
time: 86.9 us; the launch traced here: 86.6 us
  blocking collectives  43 us (49%)
  starting transfers between devices  34 us (39%)
  Pallas kernels  5.58 us (6%)
  waiting for transfers between devices  3.21 us (4%)
    all_to_all x1, blocking collectives, body(): lax.all_to_all(part, both, 0, 0, axis_index_groups=columns, tiled=True)  23.4 us
    ppermute x1, starting transfers between devices, body(): got_b = lax.ppermute(send_b, 'gx', swap_pairs(n_gx, True))  20.9 us
    all_to_all x1, blocking collectives, body(): lax.all_to_all(part, both, 0, 0, axis_index_groups=planes, tiled=True)  13.4 us
    all_gather x1, blocking collectives, body(): lax.all_gather(send_a, 'gx', axis_index_groups=near_pairs, tiled=True)  6.22 us
    ppermute x1, starting transfers between devices, body(): yb2 = lax.ppermute(send_b, 'gy', swap_pairs(n_gy, True, wrap=False))  4.19 us
    ppermute x1, starting transfers between devices, body(): ya1 = lax.ppermute(send_a, 'gy', swap_pairs(n_gy, False))  3.77 us
    ppermute x1, waiting for transfers between devices, body(): got_b = lax.ppermute(send_b, 'gx', swap_pairs(n_gx, True))  3.2 us
    ppermute x1, starting transfers between devices, body(): yb1 = lax.ppermute(send_b, 'gy', swap_pairs(n_gy, True))  2.54 us
  transfers between devices with their start and end apart: 6, of which 1 were waited for; matrix products, arithmetic and copies ran while one was open for 0% of the time, Pallas kernels for 2%

profile of v6, /device:TPU:1, one launch (start us, length us, event | category | flops | bytes accessed | tf_op | source)
XLA Modules:
  0.0 86.6 jit_solution(13437394200416269200)
XLA Ops:
  0.6 1.5 %pack_x.1 = (f32[392,128]{1,0:T(8,128)S(1)}, f32[392,128]{1,0:T(8,128)S(1)}, f32[3,128,128]{2,1,0:T(8,128)S(1)}, f32[3,128,128]{2,1,0:T(8,128)S(1)}, s32[8,16,64]{2,1,0:T(8,128)S(1)}, /*index=5*/f32[8,8,128]{2,1,0:T(8,128)S(1)}) custom-call(f32[3,128,128]{2,1,0:T(8,128)} %bitcast.8, f32[3,128,128]{2,1,0:T(8,128)} %bitcast.9, s32[8,16,64]{2,1,0:T(8,128)} %m_ref.1, ...), custom_call_target="tpu_custom_call" | custom-call | bytes 1048576 | tf_op jit(solution)/shard_map/pack_x/pallas_call | solution.py:429
  2.1 20.9 %collective-permute-start = (f32[392,128]{1,0:T(8,128)S(1)}, f32[392,128]{1,0:T(8,128)S(1)}, u32[]{:S(2)}, u32[]{:S(2)}) collective-permute-start(f32[392,128]{1,0:T(8,128)S(1)} %get-tuple-element.42), channel_id=1, source_target_pairs={{0,496},{16,32},{32,16},{48,64},{64,48},{80,96},{96,80},{112,128},... | collective-permute-start | bytes 602120 | tf_op jit(solution)/shard_map/ppermute | solution.py:435
  23.1 6.2 %all_gather.3.a_ref = f32[784,128]{1,0:T(8,128)S(1)} all-gather(f32[392,128]{1,0:T(8,128)S(1)} %get-tuple-element.38), channel_id=1, replica_groups={{0,16},{32,48},{64,80},{96,112},{128,144},{160,176},{192,208},{224,240}..., dimensions={0}, use_global_device_ids=true | all-gather | bytes 602112 | tf_op jit(solution)/shard_map/all_gather | solution.py:434
  29.3 0.2 own_cells.1
  29.4 0.2 near_side.1
  29.6 3.8 %collective-permute-start.1 = (f32[42,8,128]{2,1,0:T(8,128)S(1)}, f32[42,8,128]{2,1,0:T(8,128)S(1)}, u32[]{:S(2)}, u32[]{:S(2)}) collective-permute-start(f32[42,8,128]{2,1,0:T(8,128)S(1)} %get-tuple-element.43), channel_id=1, source_target_pairs={{0,1},{1,0},{2,3},{3,2},{4,5},{5,4},{6,7},{7,6},{8,9},{9,8},{10,11... | collective-permute-start | bytes 516104 | tf_op jit(solution)/shard_map/ppermute | solution.py:446
  33.4 2.5 %collective-permute-start.2 = (f32[42,8,128]{2,1,0:T(8,128)S(1)}, f32[42,8,128]{2,1,0:T(8,128)S(1)}, u32[]{:S(2)}, u32[]{:S(2)}) collective-permute-start(f32[42,8,128]{2,1,0:T(8,128)S(1)} %get-tuple-element.45), channel_id=1, source_target_pairs={{0,15},{1,2},{2,1},{3,4},{4,3},{5,6},{6,5},{7,8},{8,7},{9,10},{10,... | collective-permute-start | bytes 516104 | tf_op jit(solution)/shard_map/ppermute | solution.py:444
  35.9 0.7 collective-permute-start.3
  36.6 0.0 collective-permute-done.1.ya1
  36.6 3.2 %collective-permute-done.b_ref = f32[392,128]{1,0:T(8,128)S(1)} collective-permute-done((f32[392,128]{1,0:T(8,128)S(1)}, f32[392,128]{1,0:T(8,128)S(1)}, u32[]{:S(2)}, u32[]{:S(2)}) %collective-permute-start) | collective-permute-done | bytes 200736 | tf_op jit(solution)/shard_map/ppermute | solution.py:435
  39.8 0.2 far_side.1
  40.0 4.2 %collective-permute-start.4 = (f32[14,8,128]{2,1,0:T(8,128)S(1)}, f32[14,8,128]{2,1,0:T(8,128)S(1)}, u32[]{:S(2)}, u32[]{:S(2)}) collective-permute-start(f32[14,8,128]{2,1,0:T(8,128)S(1)} %get-tuple-element.56), channel_id=1, source_target_pairs={{1,2},{2,1},{3,4},{4,3},{5,6},{6,5},{7,8},{8,7},{9,10},{10,9},{11,... | collective-permute-start | bytes 172040 | tf_op jit(solution)/shard_map/ppermute | solution.py:452
  44.2 1.9 %collective-permute-start.5 = (f32[14,8,128]{2,1,0:T(8,128)S(1)}, f32[14,8,128]{2,1,0:T(8,128)S(1)}, u32[]{:S(2)}, u32[]{:S(2)}) collective-permute-start(f32[14,8,128]{2,1,0:T(8,128)S(1)} %get-tuple-element.57), channel_id=1, source_target_pairs={{0,1},{1,0},{2,3},{3,2},{4,5},{5,4},{6,7},{7,6},{8,9},{9,8},{10,11... | collective-permute-start | bytes 172040 | tf_op jit(solution)/shard_map/ppermute | solution.py:451
  46.1 0.0 collective-permute-done.2.yb1
  46.1 1.2 %near_steps.1 = (f32[5,3,16,24,128]{4,3,2,1,0:T(8,128)S(1)}, f32[3,16,24,128]{3,2,1,0:T(8,128)S(1)}, f32[16,24,128]{2,1,0:T(8,128)S(1)}, f32[20,8,128]{2,1,0:T(8,128)S(1)}) custom-call(f32[3,8,16,128]{3,2,1,0:T(8,128)S(1)} %bitcast.5, f32[3,8,16,128]{3,2,1,0:T(8,128)S(1)} %bitcast.7, f32[8,16,128]{2,1,0:T(8,128)S(1)} %get-tuple-element.36.s_ref.own_s, ...), custom_call_target="tpu_custom_call" | custom-call | flops 16777216 | bytes 4194304 | tf_op jit(solution)/shard_map/near_steps/pallas_call | solution.py:457
  47.4 0.0 collective-permute-done.3.corner
  47.4 0.0 collective-permute-done.4.yb2
  47.4 0.0 collective-permute-done.5.ya2
  47.4 1.6 %far_steps.1 = (f32[3,8,16,128]{3,2,1,0:T(8,128)}, f32[3,8,16,128]{3,2,1,0:T(8,128)}, f32[32,1,128]{2,1,0:T(1,128)S(1)}) custom-call(f32[5,3,16,24,128]{4,3,2,1,0:T(8,128)S(1)} %get-tuple-element.47.ee, f32[3,16,24,128]{3,2,1,0:T(8,128)S(1)} %get-tuple-element.48.hh, f32[16,24,128]{2,1,0:T(8,128)S(1)} %get-tuple-element.49.ss, ...), custom_call_target="tpu_custom_call" | custom-call | flops 16777216 | bytes 4194304 | tf_op jit(solution)/shard_map/far_steps/pallas_call | solution.py:462
  49.0 13.4 %all_to_all.10.in_ref = f32[32,1,128]{2,1,0:T(1,128)S(1)} all-to-all(f32[32,1,128]{2,1,0:T(1,128)S(1)} %get-tuple-element.60), channel_id=1, replica_groups={{0,1,16,17,32,33,48,49,128,129,144,145,160,161,176,177,256,257,272,273,..., dimensions={0} | all-to-all | bytes 32768 | tf_op jit(solution)/shard_map/all_to_all | solution.py:466
  62.4 23.4 %all_to_all.11.in_ref = f32[16,1,128]{2,1,0:T(1,128)S(1)} all-to-all(f32[16,1,128]{2,1,0:T(1,128)S(1)} %add_up.1), channel_id=1, replica_groups={{0,2,4,6,8,10,12,14,64,66,68,70,72,74,76,78},{1,3,5,7,9,11,13,15,65,67,..., dimensions={0} | all-to-all | bytes 16384 | tf_op jit(solution)/shard_map/all_to_all | solution.py:468
  85.8 0.8 finish.1
  (1 shorter events, 0.0 us)
Async XLA Ops:
  2.1 37.7 %collective-permute-start = (f32[392,128]{1,0:T(8,128)S(1)}, f32[392,128]{1,0:T(8,128)S(1)}, u32[]{:S(2)}, u32[]{:S(2)}) collective-permute-start(f32[392,128]{1,0:T(8,128)S(1)} %get-tuple-element.42), channel_id=1, source_target_pairs={{0,496},{16,32},{32,16},{48,64},{64,48},{80,96},{96,80},{112,128},... | collective-permute-start | bytes 602120 | tf_op jit(solution)/shard_map/ppermute | solution.py:435
  29.6 7.0 %collective-permute-start.1 = (f32[42,8,128]{2,1,0:T(8,128)S(1)}, f32[42,8,128]{2,1,0:T(8,128)S(1)}, u32[]{:S(2)}, u32[]{:S(2)}) collective-permute-start(f32[42,8,128]{2,1,0:T(8,128)S(1)} %get-tuple-element.43), channel_id=1, source_target_pairs={{0,1},{1,0},{2,3},{3,2},{4,5},{5,4},{6,7},{7,6},{8,9},{9,8},{10,11... | collective-permute-start | bytes 516104 | tf_op jit(solution)/shard_map/ppermute | solution.py:446
  33.4 12.7 %collective-permute-start.2 = (f32[42,8,128]{2,1,0:T(8,128)S(1)}, f32[42,8,128]{2,1,0:T(8,128)S(1)}, u32[]{:S(2)}, u32[]{:S(2)}) collective-permute-start(f32[42,8,128]{2,1,0:T(8,128)S(1)} %get-tuple-element.45), channel_id=1, source_target_pairs={{0,15},{1,2},{2,1},{3,4},{4,3},{5,6},{6,5},{7,8},{8,7},{9,10},{10,... | collective-permute-start | bytes 516104 | tf_op jit(solution)/shard_map/ppermute | solution.py:444
  35.9 11.4 %collective-permute-start.3 = (f32[14,8,128]{2,1,0:T(8,128)S(1)}, f32[14,8,128]{2,1,0:T(8,128)S(1)}, u32[]{:S(2)}, u32[]{:S(2)}) collective-permute-start(f32[14,8,128]{2,1,0:T(8,128)S(1)} %get-tuple-element.55), channel_id=1, source_target_pairs={{0,511},{15,496},{16,47},{31,32},{32,31},{47,16},{48,79},{63,64},{... | collective-permute-start | bytes 172040 | tf_op jit(solution)/shard_map/ppermute | solution.py:445
  40.0 7.4 %collective-permute-start.4 = (f32[14,8,128]{2,1,0:T(8,128)S(1)}, f32[14,8,128]{2,1,0:T(8,128)S(1)}, u32[]{:S(2)}, u32[]{:S(2)}) collective-permute-start(f32[14,8,128]{2,1,0:T(8,128)S(1)} %get-tuple-element.56), channel_id=1, source_target_pairs={{1,2},{2,1},{3,4},{4,3},{5,6},{6,5},{7,8},{8,7},{9,10},{10,9},{11,... | collective-permute-start | bytes 172040 | tf_op jit(solution)/shard_map/ppermute | solution.py:452
  44.2 3.2 %collective-permute-start.5 = (f32[14,8,128]{2,1,0:T(8,128)S(1)}, f32[14,8,128]{2,1,0:T(8,128)S(1)}, u32[]{:S(2)}, u32[]{:S(2)}) collective-permute-start(f32[14,8,128]{2,1,0:T(8,128)S(1)} %get-tuple-element.57), channel_id=1, source_target_pairs={{0,1},{1,0},{2,3},{3,2},{4,5},{5,4},{6,7},{7,6},{8,9},{9,8},{10,11... | collective-permute-start | bytes 172040 | tf_op jit(solution)/shard_map/ppermute | solution.py:451
